TPU v7x, 32 devices: a whole 2x2x4 slice. The times are simulated.
32 devices in a mesh: gx: 2 (over x), gy: 4 (over y, core), gz: 4 (over z).
Axes of the slice: x: 2, y: 2, z: 4, core: 2. Of those that a mesh axis runs over, the one named last changes fastest.
Arguments:
- features: bfloat16 [32, 8, 256, 512], P(None, 'gz', 'gx', 'gy'), may hold values from -6 to 6
- conv_weight: bfloat16 [27, 32, 32], replicated, may hold values from -0.21875 to 0.21875
- conv_bias: float32 [32], replicated, may hold values from -3 to 3
- head_weight: bfloat16 [3, 32], replicated, may hold values from -3 to 3
- head_bias: float32 [3], replicated, may hold values from -3 to 3
- fragments: int32 [8, 256, 512], P('gz', 'gx', 'gy'), may hold values from 0 to 63
- edge_cells: int32 [2, 32768], P(None, ('gx', 'gy', 'gz')), may hold values from 0 to 16384, as said below
- edge_owner: int32 [32768, 1], P(('gx', 'gy', 'gz')), may hold values from 0 to 31; in each aligned block of 1024 rows (0 to 1023, 1024 to 2047, ...) at most 48 rows name the same one
- edge_count: int32 [32], P(('gx', 'gy', 'gz')), may hold values from 1 to 1024, 24576 in all
- recv_slot: int32 [32, 1536], P(('gx', 'gy', 'gz')), may hold values from 0 to 383
Outputs:
- affinity: bfloat16 [3, 8, 256, 512], P(None, 'gz', 'gx', 'gy')
- edge_mean: float32 [32, 384], P(('gx', 'gy', 'gz'))
Inputs may be any that keep to these rules, and one draw needn't show every extreme that they name: `edge_cells`: each code is a 256 + c with a < 64 and c < 256, or 16384, which names the zero entry. `edge_owner`: at most 48 slots of one device name the same owner; some device has exactly 48 for one owner.
All inputs are finite; a program needn't handle non-finite values. No bound on the sum of `edge_count` on one device may be relied on, other than what follows from the above.
Results may differ from a plain program's by a relative error of at most 0.0041.
Values may be sent and summed in bfloat16 or wider, within the bound.
No kernel may reach another device: no remote copies, remote signals or barrier semaphores. Data moves between devices by JAX's collectives and lax.ppermute only.
A program may use at most 128 MiB of HBM per device.

v0:
```python
import jax
import jax.numpy as jnp
from jax import lax
from jax.sharding import PartitionSpec as P

F = 64


def with_halo(block, sides, width):
    for axis, dim in sides:
        count = lax.axis_size(axis)
        forward = [(i, i + 1) for i in range(count - 1)]
        backward = [(target, source) for source, target in forward]
        low = lax.ppermute(
            lax.slice_in_dim(block, block.shape[dim] - width, None, axis=dim), axis, forward
        )
        high = lax.ppermute(lax.slice_in_dim(block, 0, width, axis=dim), axis, backward)
        block = jnp.concatenate([low, block, high], axis=dim)
    return block


def shifted(value, axis, by):
    length = lax.axis_size(axis)
    pairs = [(i, i + by) for i in range(length) if 0 <= i + by < length]
    return lax.ppermute(value, axis, pairs)


def code_below(partner, along, first_live):
    line = lax.broadcasted_iota(jnp.int32, partner.shape, along)
    outer = jnp.where(first_live, F * (1 + along) + partner, -1)
    return jnp.where(line >= 1, partner, outer)


def shards(
    features,
    conv_weight,
    conv_bias,
    head_weight,
    head_bias,
    fragments,
    edge_cells,
    edge_owner,
    edge_count,
    recv_slot,
):
    channels = features.shape[0]
    voxels = fragments.shape[0] * fragments.shape[1] * fragments.shape[2]
    padded = with_halo(features, (("gx", 2), ("gy", 3), ("gz", 1)), 1)
    below_z = shifted(fragments[-1], "gz", 1)
    below_x = shifted(fragments[:, -1], "gx", 1)
    below_y = shifted(fragments[:, :, -1], "gy", 1)
    kernel = conv_weight.reshape(3, 3, 3, channels, channels).transpose(3, 4, 0, 1, 2)
    pre_act = lax.conv_general_dilated(
        padded[None],
        kernel,
        (1, 1, 1),
        "VALID",
        dimension_numbers=("NCDHW", "OIDHW", "NCDHW"),
        preferred_element_type=jnp.float32,
    )[0]
    hidden = jnp.maximum(pre_act + conv_bias[:, None, None, None], 0.0).astype(jnp.bfloat16)
    logits = (
        jnp.einsum("oc,czxy->ozxy", head_weight, hidden, preferred_element_type=jnp.float32)
        + head_bias[:, None, None, None]
    )
    affinity = jax.nn.sigmoid(logits).astype(jnp.bfloat16)
    partners = (
        jnp.concatenate([below_z[None], fragments[:-1]], 0),
        jnp.concatenate([below_x[:, None], fragments[:, :-1]], 1),
        jnp.concatenate([below_y[:, :, None], fragments[:, :, :-1]], 2),
    )
    first_flags = (lax.axis_index("gz") > 0, lax.axis_index("gx") > 0, lax.axis_index("gy") > 0)
    own_hot = (jnp.arange(F)[:, None] == fragments.reshape(1, voxels)).astype(jnp.bfloat16)
    columns = jnp.arange(2 * F)[None, :]
    own_sum = jnp.zeros((F, F), jnp.float32)
    own_count = jnp.zeros((F, F), jnp.float32)
    outer_sums = []
    outer_counts = []
    for along in range(3):
        codes = code_below(partners[along], along, first_flags[along]).reshape(voxels, 1)
        local_col = jnp.where(codes < F, codes, codes - along * F)
        partner_hot = (local_col == columns).astype(jnp.bfloat16)
        weighted = own_hot * affinity[along].reshape(1, voxels)
        left_side = jnp.concatenate([weighted, own_hot], 0)
        product = jnp.dot(left_side, partner_hot, preferred_element_type=jnp.float32)
        own_sum = own_sum + product[:F, :F]
        own_count = own_count + product[F:, :F]
        outer_sums.append(product[:F, F:])
        outer_counts.append(product[F:, F:])
    tail = jnp.zeros((1,), jnp.float32)
    table_sum = jnp.concatenate([jnp.concatenate([own_sum] + outer_sums, 1).reshape(-1), tail])
    table_count = jnp.concatenate(
        [jnp.concatenate([own_count] + outer_counts, 1).reshape(-1), tail]
    )
    slot_count = edge_cells.shape[1]
    live_mask = (jnp.arange(slot_count) < edge_count[0]).astype(jnp.float32)
    part_sum = (table_sum[edge_cells[0]] + table_sum[edge_cells[1]]) * live_mask
    part_count = (table_count[edge_cells[0]] + table_count[edge_cells[1]]) * live_mask
    devices = lax.axis_size("gx") * lax.axis_size("gy") * lax.axis_size("gz")
    capacity = recv_slot.shape[1] // devices
    own_slots = devices * capacity // 4
    owners = edge_owner[:, 0]
    owner_hot = (owners[:, None] == jnp.arange(devices)[None, :]).astype(jnp.int32)
    owner_rank = jnp.sum(jnp.cumsum(owner_hot, axis=0) * owner_hot, axis=1) - 1
    position = owners * capacity + owner_rank
    outgoing = (
        jnp.zeros((2, devices * capacity), jnp.float32)
        .at[:, position]
        .add(jnp.stack([part_sum, part_count]))
    )
    outgoing = outgoing.reshape(
        2, lax.axis_size("gx") * lax.axis_size("gy"), lax.axis_size("gz"), capacity
    )
    received = lax.all_to_all(
        lax.all_to_all(outgoing, ("gx", "gy"), split_axis=1, concat_axis=1, tiled=True),
        "gz",
        split_axis=2,
        concat_axis=2,
        tiled=True,
    )
    received = received.reshape(2, devices * capacity)
    totals = jax.ops.segment_sum(received.T, recv_slot[0], num_segments=own_slots)
    edge_mean = totals[:, 0] / jnp.maximum(totals[:, 1], 1.0)
    return (affinity, edge_mean[None])


def solution(mesh):
    in_specs = (
        P(None, "gz", "gx", "gy"),
        P(),
        P(),
        P(),
        P(),
        P("gz", "gx", "gy"),
        P(None, ("gx", "gy", "gz")),
        P(("gx", "gy", "gz"), None),
        P(("gx", "gy", "gz")),
        P(("gx", "gy", "gz"), None),
    )
    out_specs = (P(None, "gz", "gx", "gy"), P(("gx", "gy", "gz"), None))
    return jax.shard_map(shards, mesh=mesh, in_specs=in_specs, out_specs=out_specs, check_vma=False)
```

profile of v0, /device:TPU:0, one launch (start us, length us, event | category | flops | bytes accessed | tf_op | source)
XLA Modules:
  0.0 349.2 jit_solution(16262090606981638411)
XLA Ops:
  1.8 4.8 %collective-permute-start = (bf16[32,2,1,128]{3,0,2,1:T(8,128)(2,1)S(1)}, bf16[32,2,1,128]{3,0,2,1:T(8,128)(2,1)S(1)}, u32[]{:S(2)}, u32[]{:S(2)}) collective-permute-start(bf16[32,2,1,128]{3,0,2,1:T(8,128)(2,1)S(1)} %copy.107), channel_id=1, source_target_pairs={{0,16},{1,17},{2,18},{3,19},{4,20},{5,21},{6,22},{7,23},{8,24},{9,... | collective-permute-start | bytes 49160 | tf_op jit(solution)/shard_map/ppermute | solution.py:14
  8.8 3.5 collective-permute-start.6
  13.0 4.5 %collective-permute-start.7 = (s32[2,128]{1,0:T(2,128)S(1)}, s32[2,128]{1,0:T(2,128)S(1)}, u32[]{:S(2)}, u32[]{:S(2)}) collective-permute-start(s32[2,128]{1,0:T(2,128)S(1)} %bitcast.148), channel_id=1, source_target_pairs={{0,16},{1,17},{2,18},{3,19},{4,20},{5,21},{6,22},{7,23},{8,24},{9,... | collective-permute-start | bytes 3080 | tf_op jit(solution)/shard_map/ppermute | solution.py:25
  20.0 3.6 %fusion.20 = bf16[64,32768]{1,0:T(8,128)(2,1)} fusion(s32[32768]{0:T(1024)} %bitcast.113), kind=kLoop, calls=%fused_computation.35 | loop fusion | flops 4194304 | bytes 4325376 | tf_op jit(solution)/shard_map/convert_element_type | solution.py:73
  25.1 9.0 %reduce-window.6 = s32[32,8,128]{2,1,0:T(8,128)S(1)} reduce-window(s32[32,8,128]{2,1,0:T(8,128)S(1)} %fusion.56, s32[]{:T(128)} %constant.22.clone.1), window={size=1x1x128 pad=0_0x0_0x127_0}, to_apply=%region_0.1 | reduce-window | flops 4161536 | bytes 262148 | tf_op jit(solution)/shard_map/reduce-window
  36.0 3.5 copy.88
  40.5 3.9 %copy.87 = bf16[32,2,1,128]{2,0,3,1:T(8,128)(2,1)} copy(bf16[32,2,1,128]{3,0,2,1:T(8,128)(2,1)S(1)} %collective-permute-done) | data formatting | bytes 32768 | tf_op jit(solution)/shard_map/ppermute | solution.py:14
  44.4 3.9 %copy.89 = bf16[32,2,1,128]{2,0,3,1:T(8,128)(2,1)} copy(bf16[32,2,1,128]{3,0,2,1:T(8,128)(2,1)S(1)} %collective-permute-done.1) | data formatting | bytes 32768 | tf_op jit(solution)/shard_map/ppermute | solution.py:17
  49.2 4.2 %collective-permute-start.2 = (bf16[32,2,130,1]{2,0,3,1:T(8,128)(2,1)S(1)}, bf16[32,2,130,1]{2,0,3,1:T(8,128)(2,1)S(1)}, u32[]{:S(2)}, u32[]{:S(2)}) collective-permute-start(bf16[32,2,130,1]{2,0,3,1:T(8,128)(2,1)S(1)} %get-tuple-element.14), channel_id=1, source_target_pairs={{0,4},{4,8},{8,12},{1,5},{5,9},{9,13},{2,6},{6,10},{10,14},{3,7},{... | collective-permute-start | bytes 49928 | tf_op jit(solution)/shard_map/ppermute | solution.py:14
  56.5 4.3 %pad_maximum_fusion.6 = bf16[32,2,130,130]{2,0,3,1:T(8,128)(2,1)S(1)} fusion(bf16[32,2,130,1]{2,0,3,1:T(8,128)(2,1)S(1)} %collective-permute-done.3, bf16[32,2,1,128]{2,0,3,1:T(8,128)(2,1)} %copy.89, bf16[32,2,128,128]{2,0,3,1:T(8,128)(2,1)S(1)} %copy.88, bf16[32,2,1,128]{2,0,3,1:T(8,128)(2,1)} %copy.87, bf16[32,2,130,1]{2,0,3,1:T(8,128)(2,1)S(1)} %collective-permute-done.2), kind=kLoop, calls=%fused_computation.37 | loop fusion | flops 10816000 | bytes 4326400 | tf_op jit(solution)/shard_map/concatenate | solution.py:18
  61.2 3.6 %collective-permute-start.4 = (bf16[32,1,130,130]{2,0,3,1:T(8,128)(2,1)S(1)}, bf16[32,1,130,130]{2,0,3,1:T(8,128)(2,1)S(1)}, u32[]{:S(2)}, u32[]{:S(2)}) collective-permute-start(bf16[32,1,130,130]{2,0,3,1:T(8,128)(2,1)S(1)} %get-tuple-element.16), channel_id=1, source_target_pairs={{0,1},{1,2},{2,3},{4,5},{5,6},{6,7},{8,9},{9,10},{10,11},{12,13},{... | collective-permute-start | bytes 3244808 | tf_op jit(solution)/shard_map/ppermute | solution.py:14
  66.5 43.7 %collective-permute-done.4 = bf16[32,1,130,130]{2,0,3,1:T(8,128)(2,1)S(1)} collective-permute-done((bf16[32,1,130,130]{2,0,3,1:T(8,128)(2,1)S(1)}, bf16[32,1,130,130]{2,0,3,1:T(8,128)(2,1)S(1)}, u32[]{:S(2)}, u32[]{:S(2)}) %collective-permute-start.4) | collective-permute-done | bytes 1081632 | tf_op jit(solution)/shard_map/ppermute | solution.py:14
  110.2 4.8 %collective-permute-done.5 = bf16[32,1,130,130]{2,0,3,1:T(8,128)(2,1)S(1)} collective-permute-done((bf16[32,1,130,130]{2,0,3,1:T(8,128)(2,1)S(1)}, bf16[32,1,130,130]{2,0,3,1:T(8,128)(2,1)S(1)}, u32[]{:S(2)}, u32[]{:S(2)}) %collective-permute-start.5) | collective-permute-done | bytes 1081632 | tf_op jit(solution)/shard_map/ppermute | solution.py:17
  115.0 7.0 %maximum_bitcast_fusion = bf16[32,4,130,1,130]{2,0,4,1,3:T(8,128)(2,1)} fusion(bf16[32,1,130,130]{2,0,3,1:T(8,128)(2,1)S(1)} %collective-permute-done.5, bf16[32,2,130,1]{2,0,3,1:T(8,128)(2,1)S(1)} %collective-permute-done.3, bf16[32,2,1,128]{2,0,3,1:T(8,128)(2,1)S(1)} %copy-done.3, bf16[32,2,128,128]{2,0,3,1:T(8,128)(2,1)S(1)} %copy.88, ...), kind=kLoop, calls=%fused_computation.25 | loop fusion | flops 30284800 | bytes 8652800 | tf_op jit(solution)/shard_map/broadcast_in_dim | solution.py:54
  122.0 9.5 %pad = bf16[32,4,130,1,136]{2,0,4,1,3:T(8,128)(2,1)} pad(bf16[32,4,130,1,130]{2,0,4,1,3:T(8,128)(2,1)} %maximum_bitcast_fusion, bf16[]{:T(256)} %constant.17.clone.1), padding=0_0x0_0x0_0x0_0x0_6 | pad | bytes 8852482 | tf_op jit(solution)/shard_map/broadcast_in_dim | solution.py:54
  131.6 23.7 %copy.91 = bf16[32,4,130,1,8,17]{0,4,5,2,1,3:T(8,128)(2,1)} copy(bf16[32,4,130,1,8,17]{2,0,5,4,1,3:T(8,128)(2,1)} %bitcast.112) | data formatting | bytes 9052160 | tf_op jit(solution)/shard_map/conv_general_dilated | solution.py:53
  157.5 29.0 %broadcast_select_fusion = f32[2,128,8,17,32]{4,2,3,1,0:T(8,128)} fusion(pred[8,17]{0,1:T(8,128)(4,1)S(1)} %copy-done.10, bf16[3,3,3,32,32]{4,3,2,1,0:T(8,128)(2,1)S(1)} %bitcast.111, bf16[32,4,130,1,7,2]{0,4,5,2,1,3:T(8,128)(2,1)S(1)} %slice.146, bf16[32,4,130,1,8,17]{0,4,5,2,1,3:T(8,128)(2,1)} %copy.91), kind=kOutput, calls=%fused_computation.24 | convolution fusion | flops 1941475328 | bytes 9503880 | tf_op jit(solution)/shard_map/conv_general_dilated | solution.py:53
  186.4 13.4 %copy.92 = f32[2,128,8,17,32]{1,4,3,2,0:T(8,128)} copy(f32[2,128,8,17,32]{4,2,3,1,0:T(8,128)} %broadcast_select_fusion) | data formatting | bytes 8912896 | tf_op jit(solution)/shard_map/conv_general_dilated | solution.py:53
  199.8 2.8 fusion.47
  203.4 2.3 fusion.21
  205.7 27.6 %fusion.8 = f32[128,128]{1,0:T(8,128)S(1)} fusion(bf16[64,32768]{1,0:T(8,128)(2,1)S(1)} %copy-done.5, bf16[64,32768]{1,0:T(8,128)(2,1)S(1)} %get-tuple-element.27, s32[32768]{0:T(1024)S(1)} %select_select_fusion), kind=kOutput, calls=%fused_computation.17 | convolution fusion | flops 1094713344 | bytes 8585216 | tf_op jit(solution)/shard_map/dot_general | solution.py:85
  233.3 27.6 %fusion.9 = f32[128,128]{1,0:T(8,128)S(1)} fusion(bf16[64,32768]{1,0:T(8,128)(2,1)S(1)} %copy-done.5, bf16[64,32768]{1,0:T(8,128)(2,1)S(1)} %get-tuple-element.29, s32[32768]{0:T(1024)S(1)} %compare_select_fusion.1), kind=kOutput, calls=%fused_computation.18 | convolution fusion | flops 1094713344 | bytes 8585216 | tf_op jit(solution)/shard_map/dot_general | solution.py:85
  260.8 27.6 %fusion.10 = f32[128,128]{1,0:T(8,128)S(1)} fusion(bf16[64,32768]{1,0:T(8,128)(2,1)S(1)} %copy-done.5, bf16[64,32768]{1,0:T(8,128)(2,1)S(1)} %get-tuple-element.28, s32[32768]{0:T(1024)S(1)} %compare_select_fusion), kind=kOutput, calls=%fused_computation.19 | convolution fusion | flops 1094713344 | bytes 8585216 | tf_op jit(solution)/shard_map/dot_general | solution.py:85
  288.9 6.2 %gather_fusion = f32[1024]{0:T(1024)S(1)} fusion(f32[16385]{0:T(1024)S(1)} %get-tuple-element.39, s32[1024]{0:T(1024)S(1)} %broadcast_clamp_fusion.1), kind=kCustom, calls=%fused_computation | custom fusion | bytes 12288 | tf_op jit(solution)/shard_map/gather | solution.py:97
  295.0 6.2 %gather_fusion.1 = f32[1024]{0:T(1024)S(1)} fusion(f32[16385]{0:T(1024)S(1)} %get-tuple-element.39, s32[1024]{0:T(1024)S(1)} %broadcast_clamp_fusion), kind=kCustom, calls=%fused_computation.1 | custom fusion | bytes 12288 | tf_op jit(solution)/shard_map/gather | solution.py:97
  301.2 6.2 %gather_fusion.2 = f32[1024]{0:T(1024)S(1)} fusion(f32[16385]{0:T(1024)S(1)} %get-tuple-element.38, s32[1024]{0:T(1024)S(1)} %broadcast_clamp_fusion.1), kind=kCustom, calls=%fused_computation.2 | custom fusion | bytes 12288 | tf_op jit(solution)/shard_map/gather | solution.py:98
  307.4 6.2 %gather_fusion.3 = f32[1024]{0:T(1024)S(1)} fusion(f32[16385]{0:T(1024)S(1)} %get-tuple-element.38, s32[1024]{0:T(1024)S(1)} %broadcast_clamp_fusion), kind=kCustom, calls=%fused_computation.3 | custom fusion | bytes 12288 | tf_op jit(solution)/shard_map/gather | solution.py:98
  313.8 6.2 %scatter_custom_fusion = f32[2,1536]{0,1:T(8,128)S(1)} fusion(s32[1024]{0:T(1024)S(1)} %bitcast.145, f32[1024,2]{1,0:T(8,128)S(1)} %copy.100, f32[]{:T(128)} %constant.20.clone.1), kind=kCustom, calls=%fused_computation.50 | custom fusion | flops 2048 | bytes 12292 | tf_op jit(solution)/shard_map/scatter-add | solution.py:109
  320.5 7.1 %all_to_all.10 = f32[8,1,384]{2,1,0:T(1,128)S(1)} all-to-all(f32[8,1,384]{2,1,0:T(1,128)S(1)} %reshape.328), channel_id=1, replica_groups=mesh['gx'=2,'gy'=4,'gz'=4] {'gx','gy'}, dimensions={0} | all-to-all | bytes 24576 | tf_op jit(solution)/shard_map/all_to_all | solution.py:115
  329.6 3.2 all-to-all-start.1
  333.7 4.7 %all-to-all-done.1 = f32[4,1,768]{2,1,0:T(1,128)S(1)} async-done(((f32[4,1,768]{2,1,0:T(1,128)}), f32[4,1,768]{2,1,0:T(1,128)S(1)}, u32[]{:S(2)}, u32[]{:S(2)}) %all-to-all-start.1) | async-done | bytes 12320 | tf_op jit(solution)/shard_map/all_to_all | solution.py:114
  339.5 8.8 %scatter_custom_fusion.1 = f32[384,2]{1,0:T(8,128)S(1)} fusion(s32[1536]{0:T(1024)S(1)} %reduce, f32[1536,2]{1,0:T(8,128)S(1)} %copy.104, f32[]{:T(128)} %constant.20.clone.1), kind=kCustom, calls=%fused_computation.70 | custom fusion | flops 3072 | bytes 3076 | tf_op jit(solution)/shard_map/scatter-add | solution.py:122
  (99 shorter events, 24.8 us)
Async XLA Ops:
  0.6 156.8 %copy-start = (bf16[27,32,32]{2,1,0:T(8,128)(2,1)S(1)}, bf16[27,32,32]{2,1,0:T(8,128)(2,1)}, u32[]{:S(2)}) copy-start(bf16[27,32,32]{2,1,0:T(8,128)(2,1)} %param.11) | copy-start | bytes 165892
  0.6 39.5 %copy-start.4 = (s32[2,128,128]{2,1,0:T(8,128)S(1)}, s32[2,128,128]{2,1,0:T(8,128)}, u32[]{:S(2)}) copy-start(s32[2,128,128]{2,1,0:T(8,128)} %param.15) | copy-start | bytes 393220
  1.8 38.7 %collective-permute-start = (bf16[32,2,1,128]{3,0,2,1:T(8,128)(2,1)S(1)}, bf16[32,2,1,128]{3,0,2,1:T(8,128)(2,1)S(1)}, u32[]{:S(2)}, u32[]{:S(2)}) collective-permute-start(bf16[32,2,1,128]{3,0,2,1:T(8,128)(2,1)S(1)} %copy.107), channel_id=1, source_target_pairs={{0,16},{1,17},{2,18},{3,19},{4,20},{5,21},{6,22},{7,23},{8,24},{9,... | collective-permute-start | bytes 49160 | tf_op jit(solution)/shard_map/ppermute | solution.py:14
  6.6 37.8 %collective-permute-start.1 = (bf16[32,2,1,128]{3,0,2,1:T(8,128)(2,1)S(1)}, bf16[32,2,1,128]{3,0,2,1:T(8,128)(2,1)S(1)}, u32[]{:S(2)}, u32[]{:S(2)}) collective-permute-start(bf16[32,2,1,128]{3,0,2,1:T(8,128)(2,1)S(1)} %copy.108), channel_id=1, source_target_pairs={{16,0},{17,1},{18,2},{19,3},{20,4},{21,5},{22,6},{23,7},{24,8},{25... | collective-permute-start | bytes 49160 | tf_op jit(solution)/shard_map/ppermute | solution.py:17
  8.8 57.5 %collective-permute-start.6 = (s32[128,128]{1,0:T(8,128)S(1)}, s32[128,128]{1,0:T(8,128)S(1)}, u32[]{:S(2)}, u32[]{:S(2)}) collective-permute-start(s32[128,128]{1,0:T(8,128)S(1)} %get-tuple-element.25), channel_id=1, source_target_pairs={{0,1},{1,2},{2,3},{4,5},{5,6},{6,7},{8,9},{9,10},{10,11},{12,13},{... | collective-permute-start | bytes 196616 | tf_op jit(solution)/shard_map/ppermute | solution.py:25
  13.0 27.1 %collective-permute-start.7 = (s32[2,128]{1,0:T(2,128)S(1)}, s32[2,128]{1,0:T(2,128)S(1)}, u32[]{:S(2)}, u32[]{:S(2)}) collective-permute-start(s32[2,128]{1,0:T(2,128)S(1)} %bitcast.148), channel_id=1, source_target_pairs={{0,16},{1,17},{2,18},{3,19},{4,20},{5,21},{6,22},{7,23},{8,24},{9,... | collective-permute-start | bytes 3080 | tf_op jit(solution)/shard_map/ppermute | solution.py:25
  18.6 21.7 %collective-permute-start.8 = (s32[2,128]{1,0:T(2,128)S(1)}, s32[2,128]{1,0:T(2,128)S(1)}, u32[]{:S(2)}, u32[]{:S(2)}) collective-permute-start(s32[2,128]{1,0:T(2,128)S(1)} %slice_reduce_fusion), channel_id=1, source_target_pairs={{0,4},{4,8},{8,12},{1,5},{5,9},{9,13},{2,6},{6,10},{10,14},{3,7},{... | collective-permute-start | bytes 3080 | tf_op jit(solution)/shard_map/ppermute | solution.py:25
  49.2 5.6 %collective-permute-start.2 = (bf16[32,2,130,1]{2,0,3,1:T(8,128)(2,1)S(1)}, bf16[32,2,130,1]{2,0,3,1:T(8,128)(2,1)S(1)}, u32[]{:S(2)}, u32[]{:S(2)}) collective-permute-start(bf16[32,2,130,1]{2,0,3,1:T(8,128)(2,1)S(1)} %get-tuple-element.14), channel_id=1, source_target_pairs={{0,4},{4,8},{8,12},{1,5},{5,9},{9,13},{2,6},{6,10},{10,14},{3,7},{... | collective-permute-start | bytes 49928 | tf_op jit(solution)/shard_map/ppermute | solution.py:14
  53.4 3.1 collective-permute-start.3
  54.8 60.3 %copy-start.2 = (bf16[32,2,1,128]{2,0,3,1:T(8,128)(2,1)S(1)}, bf16[32,2,1,128]{2,0,3,1:T(8,128)(2,1)}, u32[]{:S(2)}) copy-start(bf16[32,2,1,128]{2,0,3,1:T(8,128)(2,1)} %copy.87) | copy-start | bytes 49156
  54.8 60.3 %copy-start.3 = (bf16[32,2,1,128]{2,0,3,1:T(8,128)(2,1)S(1)}, bf16[32,2,1,128]{2,0,3,1:T(8,128)(2,1)}, u32[]{:S(2)}) copy-start(bf16[32,2,1,128]{2,0,3,1:T(8,128)(2,1)} %copy.89) | copy-start | bytes 49156
  61.2 49.0 %collective-permute-start.4 = (bf16[32,1,130,130]{2,0,3,1:T(8,128)(2,1)S(1)}, bf16[32,1,130,130]{2,0,3,1:T(8,128)(2,1)S(1)}, u32[]{:S(2)}, u32[]{:S(2)}) collective-permute-start(bf16[32,1,130,130]{2,0,3,1:T(8,128)(2,1)S(1)} %get-tuple-element.16), channel_id=1, source_target_pairs={{0,1},{1,2},{2,3},{4,5},{5,6},{6,7},{8,9},{9,10},{10,11},{12,13},{... | collective-permute-start | bytes 3244808 | tf_op jit(solution)/shard_map/ppermute | solution.py:14
  64.8 50.2 %collective-permute-start.5 = (bf16[32,1,130,130]{2,0,3,1:T(8,128)(2,1)S(1)}, bf16[32,1,130,130]{2,0,3,1:T(8,128)(2,1)S(1)}, u32[]{:S(2)}, u32[]{:S(2)}) collective-permute-start(bf16[32,1,130,130]{2,0,3,1:T(8,128)(2,1)S(1)} %get-tuple-element.17), channel_id=1, source_target_pairs={{1,0},{2,1},{3,2},{5,4},{6,5},{7,6},{9,8},{10,9},{11,10},{13,12},{... | collective-permute-start | bytes 3244808 | tf_op jit(solution)/shard_map/ppermute | solution.py:17
  131.6 25.9 %copy-start.10 = (pred[8,17]{0,1:T(8,128)(4,1)S(1)}, pred[8,17]{0,1:T(8,128)(4,1)}, u32[]{:S(2)}) copy-start(pred[8,17]{0,1:T(8,128)(4,1)} %constant.67) | copy-start | bytes 412
  186.4 13.4 %copy-start.7 = (bf16[3,32]{1,0:T(4,128)(2,1)S(1)}, bf16[3,32]{1,0:T(4,128)(2,1)}, u32[]{:S(2)}) copy-start(bf16[3,32]{1,0:T(4,128)(2,1)} %param.13) | copy-start | bytes 580
  186.4 13.4 %copy-start.8 = (f32[32]{0:T(128)S(1)}, f32[32]{0:T(128)}, u32[]{:S(2)}) copy-start(f32[32]{0:T(128)} %param.12) | copy-start | bytes 388
  186.4 13.4 %copy-start.9 = (f32[3]{0:T(128)S(1)}, f32[3]{0:T(128)}, u32[]{:S(2)}) copy-start(f32[3]{0:T(128)} %param.14) | copy-start | bytes 40
  203.4 2.3 copy-start.5
  288.9 60.3 %copy-start.1 = (bf16[27,32,32]{2,1,0:T(8,128)(2,1)S(1)}, bf16[27,32,32]{2,1,0:T(8,128)(2,1)}, u32[]{:S(2)}) copy-start(bf16[27,32,32]{2,1,0:T(8,128)(2,1)} %param.11) | copy-start | bytes 165892
  295.0 37.8 %copy-start.6 = (s32[1,1536]{1,0:T(1,128)S(1)}, s32[1,1536]{1,0:T(1,128)}, u32[]{:S(2)}) copy-start(s32[1,1536]{1,0:T(1,128)} %param.19) | copy-start | bytes 18436
  329.6 8.8 %all-to-all-start.1 = ((f32[4,1,768]{2,1,0:T(1,128)}), f32[4,1,768]{2,1,0:T(1,128)S(1)}, u32[]{:S(2)}, u32[]{:S(2)}) async-start(f32[4,1,768]{2,1,0:T(1,128)} %reshape.330), calls=%async_computation.1 | async-start | bytes 24576 | tf_op jit(solution)/shard_map/all_to_all | solution.py:114
where the time goes:
time: 351 us; the launch traced here: 349 us
  matrix products  115 us (33%)
  local copies, waits for them, and re-layouts  94.2 us (27%)
  waiting for transfers between devices  54.9 us (16%)
  other arithmetic  47.3 us (13%)
  starting transfers between devices  29.2 us (8%)
  blocking collectives  7.06 us (2%)
    dot_general x3, matrix products, shards(): jnp.dot(left_side, partner_hot, preferred_element_type=jnp.float32)  82.7 us
    ppermute x3, waiting for transfers between devices, with_halo(): lax.ppermute(lax.slice_in_dim(block, block.shape[dim] - width, None, axis...  43.7 us
    conv_general_dilated x3, local copies, waits for them, and re-layouts, shards(): lax.conv_general_dilated(padded[None], kernel, (1, 1, 1), 'VALID', dimens...  39.3 us
    conv_general_dilated x1, matrix products, shards(): lax.conv_general_dilated(padded[None], kernel, (1, 1, 1), 'VALID', dimens...  29 us
    ppermute x3, starting transfers between devices, with_halo(): lax.ppermute(lax.slice_in_dim(block, block.shape[dim] - width, None, axis...  12.6 us
    gather x2, local copies, waits for them, and re-layouts, shards(): part_sum = (table_sum[edge_cells[0]] + table_sum[edge_cells[1]]) * live_mask  12.3 us
    broadcast_in_dim x1, local copies, waits for them, and re-layouts, shards(): padded[None]  9.53 us
    ppermute x3, starting transfers between devices, shifted(): return lax.ppermute(value, axis, pairs)  9.3 us
  transfers between devices with their start and end apart: 10, of which 4 were waited for; matrix products, arithmetic and copies ran while one was open for 11% of the time, Pallas kernels for 0%

commit v1 on v0

v1 whole, which is shorter than its diff:
```python
import jax
import jax.numpy as jnp
from jax import lax
from jax.experimental import pallas as pl
from jax.experimental.pallas import tpu as pltpu
from jax.sharding import PartitionSpec as P

F = 64
LANES = 128
BF = jnp.bfloat16
F32 = jnp.float32
VMEM = pl.BlockSpec(memory_space=pltpu.VMEM)
SMEM = pl.BlockSpec(memory_space=pltpu.SMEM)


def params():
    return pltpu.CompilerParams(vmem_limit_bytes=48 << 20)


def cost(flops, nbytes):
    return pl.CostEstimate(flops=flops, bytes_accessed=nbytes, transcendentals=0)


def exchange(up, down, axis):
    n = lax.axis_size(axis)
    if n == 1:
        return jnp.zeros_like(up), jnp.zeros_like(down)
    if n == 2 and up.shape == down.shape:
        first = lax.axis_index(axis) == 0
        got = lax.ppermute(jnp.where(first, up, down), axis, [(0, 1), (1, 0)])
        none = jnp.zeros_like(got)
        return jnp.where(first, none, got), jnp.where(first, got, none)
    forward = [(i, i + 1) for i in range(n - 1)]
    backward = [(i + 1, i) for i in range(n - 1)]
    return lax.ppermute(up, axis, forward), lax.ppermute(down, axis, backward)


def spread(stage, zi, src, row_low, row_high, col_low, col_high):
    lane = lax.broadcasted_iota(jnp.int32, (32, LANES), 1)
    is_first = lane == 0
    is_last = lane == LANES - 1

    def put(x, centre, low, high):
        stage[1, zi, x] = centre
        stage[0, zi, x] = jnp.where(is_first, low, pltpu.roll(centre, 1, 1))
        stage[2, zi, x] = jnp.where(is_last, high, pltpu.roll(centre, LANES - 1, 1))

    put(0, row_low, col_low[:, LANES:], pltpu.roll(col_high[:, LANES:], LANES - 1, 1))
    put(
        LANES + 1,
        row_high,
        pltpu.roll(col_low[:, LANES:], LANES - 1, 1),
        pltpu.roll(col_high[:, LANES:], LANES - 2, 1),
    )
    low0 = col_low[:, :LANES]
    high0 = pltpu.roll(col_high[:, :LANES], LANES - 1, 1)

    def body(t, carry):
        low, high = carry
        block = jnp.swapaxes(src[:, pl.ds(pl.multiple_of(16 * t, 16), 16), :], 0, 1)
        for j in range(16):
            put(16 * t + j + 1, block[j], low, high)
            low = pltpu.roll(low, LANES - 1, 1)
            high = pltpu.roll(high, LANES - 1, 1)
        return low, high

    lax.fori_loop(0, 8, body, (low0, high0))


def toeplitz(weight_ref, out_ref, planes):
    quarter = lax.broadcasted_iota(jnp.int32, (32, LANES), 1) // 32
    zero = jnp.zeros((32, LANES), BF)
    for zo in range(2):
        for xo in range(4):
            row = 32 * (4 * zo + xo)
            for chunk in range(9):
                tile = zero
                for q in range(4):
                    place = 4 * chunk + q
                    dy, rest = divmod(place, 12)
                    plane, xi = divmod(rest, 6)
                    dz, dx = planes[plane] - zo, xi - 1 - xo
                    if abs(dz) <= 1 and abs(dx) <= 1:
                        weight = weight_ref[9 * (dz + 1) + 3 * (dx + 1) + dy]
                        tile = jnp.where(quarter == q, weight, tile)
                out_ref[row : row + 32, LANES * chunk : LANES * (chunk + 1)] = tile


def window(stage, x):
    return jnp.concatenate(
        [
            stage[:, :, pl.ds(x, 6)].reshape(1152, LANES),
            stage[:, :, pl.ds(x + 4, 6)].reshape(1152, LANES),
        ],
        axis=1,
    )


def own_planes_kernel(feat, rows, cols, weight, bias, acc, outer_weight, stage, inner_weight):
    toeplitz(weight, inner_weight, (0, 1))
    toeplitz(weight, outer_weight, (-1, 2))
    for z in range(2):
        spread(
            stage,
            z,
            feat.at[:, z],
            rows[0, 32 * z : 32 * z + 32],
            rows[1, 32 * z : 32 * z + 32],
            cols[0, 32 * z : 32 * z + 32],
            cols[1, 32 * z : 32 * z + 32],
        )
    bias_block = jnp.broadcast_to(bias[...], (256, 2 * LANES))

    def body(p, _):
        acc[p] = bias_block + jnp.dot(
            inner_weight[...], window(stage, 8 * p), preferred_element_type=F32
        )
        return 0

    lax.fori_loop(0, 16, body, 0)


def row_of(ref, z, x, copies):
    one = jnp.broadcast_to(ref[z, pl.ds(x, 1), :], (16, LANES)).astype(BF)
    return jnp.concatenate([one] * copies, axis=0)


def outer_product(left, right):
    return lax.dot_general(left, right, (((1,), (1,)), ((), ())), preferred_element_type=F32)


def table_rows(t, frag, ycode, weight_row, own_hot, pair_hot, extra):
    one = jnp.ones((F, LANES), BF)
    none = jnp.zeros((F, LANES), BF)
    iota = lax.broadcasted_iota(jnp.int32, (F, LANES), 0).astype(F32).astype(BF)
    iota2 = lax.broadcasted_iota(jnp.int32, (2 * F, LANES), 0).astype(F32).astype(BF)
    none2 = jnp.zeros((2 * F, LANES), BF)
    for j in range(16):
        x = 16 * t + j
        spot = slice(LANES * j, LANES * (j + 1))
        before = jnp.maximum(x - 1, 0)
        live = jnp.where(x > 0, 0.0, -1.0).astype(F32)
        hot = [row_of(frag, z, x, 4) == iota for z in range(2)]
        for z in range(2):
            own_hot[z, :, spot] = jnp.where(hot[z], one, none)
            earlier = jnp.broadcast_to(
                jnp.where(live < 0, live, frag[z, pl.ds(before, 1), :]), (16, LANES)
            ).astype(BF)
            earlier = jnp.concatenate([earlier] * 4, axis=0) == iota
            pair_hot[z, 0:F, spot] = jnp.where(earlier, weight_row(1, z, x, 4), none)
            pair_hot[z, F : 3 * F, spot] = jnp.where(
                row_of(ycode, z, x, 8) == iota2, weight_row(2, z, x, 8), none2
            )
        pair_hot[1, 3 * F : 4 * F, spot] = jnp.where(hot[0], weight_row(0, 1, x, 4), none)
        extra(x, spot, iota, none)


def first_line(frag, xcode, weight_row):
    none = jnp.zeros((F, LANES), BF)
    iota = lax.broadcasted_iota(jnp.int32, (F, LANES), 0).astype(F32).astype(BF)
    one = jnp.ones((F, LANES), BF)
    left = [jnp.where(row_of(frag, z, 0, 4) == iota, one, none) for z in range(2)]
    right = [
        jnp.where(row_of(xcode, z, 0, 4) == iota, weight_row(1, z, 0, 4), none) for z in range(2)
    ]
    return outer_product(jnp.concatenate(left, axis=1), jnp.concatenate(right, axis=1))


def count_kernel(frag, ycode, xcode, out, own_hot, pair_hot):
    def ones(d, z, x, copies):
        return jnp.ones((16 * copies, LANES), BF)

    def body(t, carry):
        low, high = carry
        table_rows(t, frag, ycode, ones, own_hot, pair_hot, lambda *_: None)
        low = low + outer_product(own_hot[0], pair_hot[0, : 3 * F])
        high = high + outer_product(own_hot[1], pair_hot[1, : 4 * F])
        return low, high

    low, high = lax.fori_loop(
        0, 8, body, (jnp.zeros((F, 3 * F), F32), jnp.zeros((F, 4 * F), F32))
    )
    both = low + high[:, : 3 * F]
    own = both[:, :F] + both[:, F : 2 * F] + high[:, 3 * F :]
    out[...] = jnp.concatenate(
        [own, jnp.zeros((F, F), F32), first_line(frag, xcode, ones), both[:, 2 * F :]], axis=1
    )


def rank_kernel(owner, out):
    slots = owner.shape[1]
    devices = out.shape[0]
    hot = lax.broadcasted_iota(jnp.int32, (devices, slots), 0) == owner[...]
    before = (
        lax.broadcasted_iota(jnp.int32, (slots, slots), 0)
        < lax.broadcasted_iota(jnp.int32, (slots, slots), 1)
    )
    earlier = jnp.dot(
        jnp.where(hot, 1.0, 0.0).astype(BF),
        jnp.where(before, 1.0, 0.0).astype(BF),
        preferred_element_type=F32,
    )
    rank = jnp.sum(jnp.where(hot, earlier, 0.0), axis=0, keepdims=True)
    out[...] = jnp.broadcast_to(rank, out.shape)


def halves(value):
    high = value.astype(BF)
    return high, (value - high.astype(F32)).astype(BF)


def finish_kernel(
    acc,
    below,
    above,
    ring_low,
    ring_high,
    outer_weight,
    head,
    head_bias,
    frag,
    ycode,
    xcode,
    zlive,
    counts,
    cells,
    owner,
    rank,
    edge_count,
    affinity,
    outgoing,
    stage,
    kept,
    own_hot,
    pair_hot,
    zcode,
):
    for i, (plane, ring) in enumerate(((below, ring_low), (above, ring_high))):
        spread(
            stage,
            i,
            plane,
            ring[0:32],
            ring[32:64],
            jnp.concatenate([ring[64:96], ring[96:128]], axis=1),
            jnp.concatenate([ring[128:160], ring[160:192]], axis=1),
        )
    zcode[0] = jnp.where(zlive[...] > 0, ring_low[192:320].astype(F32), -1.0)
    bias_block = jnp.broadcast_to(head_bias[...], (48, LANES))
    top_half = (lax.broadcasted_iota(jnp.int32, (48, LANES), 0) % 8) < 4

    def weight_row(d, z, x, copies):
        return row_of(kept, 2 * d + z, x, copies)

    def z_outer(x, spot, iota, none):
        hot = row_of(zcode, 0, x, 4) == iota
        pair_hot[0, 3 * F : 4 * F, spot] = jnp.where(hot, weight_row(0, 0, x, 4), none)
        pair_hot[0, 4 * F :, spot] = jnp.where(hot, jnp.ones((F, LANES), BF), none)

    def body(t, carry):
        low, high = carry
        for half in range(2):
            p = 2 * t + half
            total = acc[p] + jnp.dot(
                outer_weight[...], window(stage, 8 * p), preferred_element_type=F32
            )
            hidden = jnp.maximum(total, 0.0).astype(BF)
            logits = jnp.dot(head[...], hidden, preferred_element_type=F32)
            logits = jnp.where(top_half, logits[:, :LANES], logits[:, LANES:]) + bias_block
            value = jax.nn.sigmoid(logits).astype(BF).astype(F32)
            for i in range(6):
                kept[i, pl.ds(pl.multiple_of(8 * p, 8), 8), :] = value[8 * i : 8 * i + 8]
        lines = pl.ds(pl.multiple_of(16 * t, 16), 16)
        for i in range(6):
            affinity[i // 2, i % 2, lines, :] = kept[i, lines, :].astype(BF)
        table_rows(t, frag, ycode, weight_row, own_hot, pair_hot, z_outer)
        low = low + outer_product(own_hot[0], pair_hot[0])
        high = high + outer_product(own_hot[1], pair_hot[1, : 4 * F])
        return low, high

    low, high = lax.fori_loop(
        0, 8, body, (jnp.zeros((F, 5 * F), F32), jnp.zeros((F, 4 * F), F32))
    )
    both = low[:, : 3 * F] + high[:, : 3 * F]
    own = both[:, :F] + both[:, F : 2 * F] + high[:, 3 * F :]
    sums = jnp.concatenate(
        [own, low[:, 3 * F : 4 * F], first_line(frag, xcode, weight_row), both[:, 2 * F :]], axis=1
    )
    tally = counts[...] + jnp.concatenate(
        [jnp.zeros((F, F), F32), low[:, 4 * F :], jnp.zeros((F, 2 * F), F32)], axis=1
    )
    slots = cells.shape[1]
    code = jnp.concatenate([cells[0:1, :], cells[1:2, :]], axis=1)
    column = (code & (4 * F - 1)).astype(F32)
    line = code >> 8
    column_hot = jnp.where(
        lax.broadcasted_iota(jnp.int32, (4 * F, 2 * slots), 0).astype(F32) == column, 1.0, 0.0
    ).astype(BF)
    picked = jnp.dot(
        jnp.concatenate(halves(sums) + halves(tally), axis=0),
        column_hot,
        preferred_element_type=F32,
    )
    line_hot = lax.broadcasted_iota(jnp.int32, (F, 2 * slots), 0) == line
    alive = lax.broadcasted_iota(jnp.int32, (1, slots), 1) < edge_count[0]

    def part(value):
        total = jnp.sum(jnp.where(line_hot, value, 0.0), axis=0, keepdims=True)
        return jnp.where(alive, total[:, :slots] + total[:, slots:], 0.0)

    part_sum = part(picked[:F] + picked[F : 2 * F])
    part_count = part(picked[2 * F : 3 * F] + picked[3 * F :])
    devices = outgoing.shape[0]
    to_owner = lax.broadcasted_iota(jnp.int32, (devices, slots), 0) == owner[...]
    lanes = lax.broadcasted_iota(jnp.int32, (LANES, slots), 0)
    place = rank[0:1, :].astype(jnp.int32)
    low_hot = jnp.where(lanes == place, 1.0, 0.0).astype(BF)
    high_hot = jnp.where(lanes == place + F, 1.0, 0.0).astype(BF)
    left = [
        jnp.where(to_owner, piece.astype(F32), 0.0).astype(BF)
        for piece in halves(part_sum) + halves(part_count)
    ]
    sent = outer_product(
        jnp.concatenate(left, axis=1),
        jnp.concatenate([low_hot, low_hot, high_hot, high_hot], axis=1),
    )
    outgoing[...] = sent.reshape(outgoing.shape)


def settle_kernel(received, slot, out, left, right):
    devices = received.shape[0]
    groups = out.shape[1] // LANES
    iota = lax.broadcasted_iota(jnp.int32, (LANES, LANES), 0)
    row = lax.broadcasted_iota(jnp.int32, (16, LANES), 0)
    lane = lax.broadcasted_iota(jnp.int32, (16, LANES), 1)
    of_count = row >= 2 * groups
    inner = jnp.where(of_count, row - 2 * groups, row)
    is_low = inner >= groups
    group = jnp.where(is_low, inner - groups, inner)
    group = jnp.where((lane >= F) == of_count, group, -1)
    group = jnp.where(row < 4 * groups, group, -1)

    def body(p, _):
        spot = pl.ds(pl.multiple_of(p * LANES, LANES), LANES)
        code = slot[pl.ds(p, 1), :]
        value = received[p]
        high = value.astype(BF).astype(F32)
        piece = jnp.where(is_low, value - high, high)
        left[:, spot] = jnp.where((code >> 7) == group, piece, 0.0).astype(BF)
        right[:, spot] = jnp.where((code & (LANES - 1)) == iota, 1.0, 0.0).astype(BF)
        return 0

    lax.fori_loop(0, devices, body, 0, unroll=8)
    total = outer_product(left[...], right[...])
    for g in range(groups):
        total_sum = total[g : g + 1] + total[groups + g : groups + g + 1]
        total_count = total[2 * groups + g : 2 * groups + g + 1] + total[3 * groups + g : 3 * groups + g + 1]
        out[:, LANES * g : LANES * (g + 1)] = total_sum / jnp.maximum(total_count, 1.0)


def shards(
    features,
    conv_weight,
    conv_bias,
    head_weight,
    head_bias,
    fragments,
    edge_cells,
    edge_owner,
    edge_count,
    recv_slot,
):
    axes = ("gx", "gy", "gz")
    devices = lax.axis_size("gx") * lax.axis_size("gy") * lax.axis_size("gz")
    capacity = recv_slot.shape[1] // devices
    slots = edge_cells.shape[1]
    own_slots = devices * capacity // 4
    frag_bf = fragments.astype(BF)
    frag = fragments.astype(F32)

    below, above = exchange(features[:, 1], features[:, 0], "gz")

    def packed(value):
        return value.transpose(1, 0, 2).reshape(64, LANES)

    def rows16(value):
        return jnp.pad(value, ((0, 16 - value.shape[0]), (0, 0)))

    x_up = jnp.concatenate([packed(features[:, :, -1, :]), rows16(frag_bf[:, -1, :])], 0)
    x_down = jnp.concatenate([packed(features[:, :, 0, :]), jnp.zeros((16, LANES), BF)], 0)
    x_low, x_high = exchange(x_up, x_down, "gx")
    rows = jnp.stack([x_low[:64], x_high[:64]])

    def columns(at, last):
        main = jnp.concatenate([packed(features[:, :, :, at]), last], 0)
        ends = jnp.concatenate([rows[0, :, at, None], rows[1, :, at, None]], 1)
        return jnp.concatenate([main, jnp.pad(ends, ((0, 16), (0, LANES - 2)))], 1)

    y_low, y_high = exchange(
        columns(-1, rows16(frag_bf[:, :, -1])), columns(0, jnp.zeros((16, LANES), BF)), "gy"
    )
    cols = jnp.stack([y_low[:64], y_high[:64]])

    def ring(z):
        lines = slice(32 * z, 32 * z + 32)
        return [
            rows[0, lines],
            rows[1, lines],
            cols[0, lines, :LANES],
            cols[0, lines, LANES:],
            cols[1, lines, :LANES],
            cols[1, lines, LANES:],
        ]

    ring_low, ring_high = exchange(
        jnp.concatenate(ring(1) + [frag_bf[1]], 0), jnp.concatenate(ring(0), 0), "gz"
    )

    first_x = lax.axis_index("gx") > 0
    first_y = lax.axis_index("gy") > 0
    first_z = lax.axis_index("gz") > 0
    xcode = jnp.where(first_x, x_low[64:66].astype(F32), -1.0)[:, None, :]
    y_outer = jnp.where(first_y, y_low[64:66, :LANES].astype(F32) + F, -1.0)[:, :, None]
    ycode = jnp.concatenate([y_outer, frag[:, :, :-1]], 2)
    zlive = jnp.broadcast_to(first_z.astype(F32), (1, LANES))

    weight4 = jnp.tile(conv_weight, (1, 1, 4))
    bias_col = jnp.tile(conv_bias, 8)[:, None]
    line = jnp.arange(48)
    step = jnp.arange(256)
    match = ((line[:, None] // 8) % 2 == step[None, :] // 128) & (
        line[:, None] % 4 == (step[None, :] // 32) % 4
    )
    head = jnp.where(match, jnp.tile(jnp.repeat(head_weight, 16, axis=0), (1, 8)), 0).astype(BF)
    head_col = jnp.repeat(head_bias, 16)[:, None]

    acc, outer_weight = pl.pallas_call(
        own_planes_kernel,
        out_shape=(
            jax.ShapeDtypeStruct((16, 256, 256), F32),
            jax.ShapeDtypeStruct((256, 1152), BF),
        ),
        in_specs=[VMEM] * 5,
        out_specs=(VMEM, VMEM),
        scratch_shapes=[pltpu.VMEM((3, 2, 130, 32, LANES), BF), pltpu.VMEM((256, 1152), BF)],
        compiler_params=params(),
        cost_estimate=cost(10_000_000_000, 8 << 20),
        name="own_planes",
    )(features, rows, cols, weight4, bias_col)

    counts = pl.pallas_call(
        count_kernel,
        out_shape=jax.ShapeDtypeStruct((F, 4 * F), F32),
        in_specs=[VMEM] * 3,
        out_specs=VMEM,
        scratch_shapes=[pltpu.VMEM((2, F, 2048), BF), pltpu.VMEM((2, 4 * F, 2048), BF)],
        compiler_params=params(),
        cost_estimate=cost(5_000_000_000, 1 << 20),
        name="pair_counts",
    )(frag, ycode, xcode)

    owner = edge_owner.reshape(1, slots)
    rank = pl.pallas_call(
        rank_kernel,
        out_shape=jax.ShapeDtypeStruct((devices, slots), F32),
        in_specs=[VMEM],
        out_specs=VMEM,
        compiler_params=params(),
        cost_estimate=cost(1_000_000_000, 1 << 20),
        name="owner_rank",
    )(owner)

    affinity, outgoing = pl.pallas_call(
        finish_kernel,
        out_shape=(
            jax.ShapeDtypeStruct((3, 2, LANES, LANES), BF),
            jax.ShapeDtypeStruct((devices, 1, LANES), F32),
        ),
        in_specs=[VMEM] * 16 + [SMEM],
        out_specs=(VMEM, VMEM),
        scratch_shapes=[
            pltpu.VMEM((3, 2, 130, 32, LANES), BF),
            pltpu.VMEM((6, LANES, LANES), F32),
            pltpu.VMEM((2, F, 2048), BF),
            pltpu.VMEM((2, 5 * F, 2048), BF),
            pltpu.VMEM((1, LANES, LANES), F32),
        ],
        compiler_params=params(),
        cost_estimate=cost(10_000_000_000, 8 << 20),
        name="finish",
    )(
        acc,
        below,
        above,
        ring_low,
        ring_high,
        outer_weight,
        head,
        head_col,
        frag,
        ycode,
        xcode,
        zlive,
        counts,
        edge_cells,
        owner,
        rank,
        edge_count,
    )

    received = lax.all_to_all(outgoing, axes, split_axis=0, concat_axis=0, tiled=True)

    slot = recv_slot.reshape(devices, capacity)
    slot = jnp.pad(slot, ((0, 0), (0, F - capacity)), constant_values=-256)
    slot = jnp.concatenate([slot, slot], 1)
    edge_mean = pl.pallas_call(
        settle_kernel,
        out_shape=jax.ShapeDtypeStruct((1, own_slots), F32),
        in_specs=[VMEM] * 2,
        out_specs=VMEM,
        scratch_shapes=[
            pltpu.VMEM((16, devices * LANES), BF),
            pltpu.VMEM((LANES, devices * LANES), BF),
        ],
        compiler_params=params(),
        name="settle",
    )(received, slot)
    return affinity, edge_mean


def solution(mesh):
    in_specs = (
        P(None, "gz", "gx", "gy"),
        P(),
        P(),
        P(),
        P(),
        P("gz", "gx", "gy"),
        P(None, ("gx", "gy", "gz")),
        P(("gx", "gy", "gz"), None),
        P(("gx", "gy", "gz")),
        P(("gx", "gy", "gz"), None),
    )
    out_specs = (P(None, "gz", "gx", "gy"), P(("gx", "gy", "gz"), None))
    return jax.shard_map(shards, mesh=mesh, in_specs=in_specs, out_specs=out_specs, check_vma=False)
```

time: 351 us -> 123 us (0.35)
  matrix products: 115 us -> 0 us
  local copies, waits for them, and re-layouts: 94.2 us -> 16 us
  Pallas kernels: 0 us -> 69.9 us
  waiting for transfers between devices: 54.9 us -> 7.94 us
  other arithmetic: 47.3 us -> 1.41 us
  blocking collectives: 7.06 us -> 0 us
    dot_general x4 -> x0, matrix products: 85.6 us -> none  [the longest x3 82.7 us: shards(): jnp.dot(left_side, partner_hot, preferred_element_type=jnp.float32)]
    pallas_call x0 -> x5, Pallas kernels: none -> 69.9 us  [the longest x1 36.8 us: shards(): pl.pallas_call(finish_kernel, out_shape=(jax.ShapeDtypeStruct((3, 2, LANE...]
    ppermute x9 -> x7, waiting for transfers between devices: 50.2 us -> 0.85 us  [the longest x6 0.84 us: exchange(): return (lax.ppermute(up, axis, forward), lax.ppermute(down, axis, backward))]
    conv_general_dilated x3 -> x0, local copies, waits for them, and re-layouts: 39.3 us -> none  [shards(): lax.conv_general_dilated(padded[None], kernel, (1, 1, 1), 'VALID', dimens...]
    conv_general_dilated x1 -> x0, matrix products: 29 us -> none  [shards(): lax.conv_general_dilated(padded[None], kernel, (1, 1, 1), 'VALID', dimens...]
    gather x4 -> x0, local copies, waits for them, and re-layouts: 24.6 us -> none  [the longest x2 12.3 us: shards(): part_sum = (table_sum[edge_cells[0]] + table_sum[edge_cells[1]]) * live_mask]
    scatter-add x2 -> x0, other arithmetic: 15 us -> none  [the longest x1 8.8 us: shards(): jax.ops.segment_sum(received.T, recv_slot[0], num_segments=own_slots)]
    broadcast_in_dim x2 -> x4, local copies, waits for them, and re-layouts: 9.66 us -> 0.21 us  [the longest x1 0.13 us: shards(): jnp.where(first_y, y_low[64:66, :LANES].astype(F32) + F, -1.0)[:, :, None]]
  transfers between devices with their start and end apart: 10 -> 8, of which waited for: 4 -> 2; matrix products, arithmetic and copies ran while one was open for 11% -> 12% of each run, Pallas kernels for 0% -> 26%
where the time goes in v1:
time: 123 us
  Pallas kernels  69.9 us (57%)
  starting transfers between devices  26 us (21%)
  local copies, waits for them, and re-layouts  16 us (13%)
  waiting for transfers between devices  7.94 us (6%)
  between operations  1.75 us (1%)
  other arithmetic  1.41 us (1%)
    pallas_call x1, Pallas kernels, shards(): pl.pallas_call(finish_kernel, out_shape=(jax.ShapeDtypeStruct((3, 2, LANE...  36.8 us
    pallas_call x1, Pallas kernels, shards(): pl.pallas_call(own_planes_kernel, out_shape=(jax.ShapeDtypeStruct((16, 25...  25.2 us
    ppermute x6, starting transfers between devices, exchange(): return (lax.ppermute(up, axis, forward), lax.ppermute(down, axis, backward))  17 us
    all_to_all x1, waiting for transfers between devices, shards(): lax.all_to_all(outgoing, axes, split_axis=0, concat_axis=0, tiled=True)  7.1 us
    pallas_call x1, Pallas kernels, shards(): pl.pallas_call(count_kernel, out_shape=jax.ShapeDtypeStruct((F, 4 * F), F...  6.06 us
    all_to_all x1, starting transfers between devices, shards(): lax.all_to_all(outgoing, axes, split_axis=0, concat_axis=0, tiled=True)  6.01 us
    unnamed x27, local copies, waits for them, and re-layouts  4.13 us
    another operation x2, local copies, waits for them, and re-layouts, shards(): weight4 = jnp.tile(conv_weight, (1, 1, 4))  3.26 us
  transfers between devices with their start and end apart: 8, of which 2 were waited for; matrix products, arithmetic and copies ran while one was open for 12% of the time, Pallas kernels for 26%

profile of v1, /device:TPU:0, one launch (start us, length us, event | category | flops | bytes accessed | tf_op | source)
XLA Modules:
  0.0 123.0 jit_solution(2318525859895839828)
XLA Ops:
  0.6 1.0 copy_convert_fusion
  1.7 1.0 fusion.17
  2.8 3.0 %collective-permute-start = (bf16[80,128]{1,0:T(8,128)(2,1)S(1)}, bf16[80,128]{1,0:T(8,128)(2,1)S(1)}, u32[]{:S(2)}, u32[]{:S(2)}) collective-permute-start(bf16[80,128]{1,0:T(8,128)(2,1)S(1)} %fusion.11), channel_id=1, source_target_pairs={{0,16},{16,0},{1,17},{17,1},{2,18},{18,2},{3,19},{19,3},{4,20},{20... | collective-permute-start | bytes 61448 | tf_op jit(solution)/shard_map/ppermute | solution.py:30
  5.8 3.2 %slice_bitcast_fusion = (bf16[32,128,128]{2,1,0:T(8,128)(2,1)}, bf16[32,128,128]{2,1,0:T(8,128)(2,1)}) fusion(bf16[32,2,128,128]{3,2,1,0:T(8,128)(2,1)} %feat.1), kind=kLoop, calls=%fused_computation | loop fusion | bytes 4194304 | tf_op jit(solution)/shard_map/squeeze | solution.py:381
  8.9 1.3 %collective-permute-start.4 = (bf16[32,128,128]{2,1,0:T(8,128)(2,1)}, bf16[32,128,128]{2,1,0:T(8,128)(2,1)}, u32[]{:S(2)}, u32[]{:S(2)}) collective-permute-start(bf16[32,128,128]{2,1,0:T(8,128)(2,1)} %get-tuple-element.14), channel_id=1, source_target_pairs={{1,0},{2,1},{3,2},{5,4},{6,5},{7,6},{9,8},{10,9},{11,10},{13,12},{... | collective-permute-start | bytes 3145736 | tf_op jit(solution)/shard_map/ppermute | solution.py:35
  10.2 5.5 %collective-permute-start.3 = (bf16[32,128,128]{2,1,0:T(8,128)(2,1)}, bf16[32,128,128]{2,1,0:T(8,128)(2,1)}, u32[]{:S(2)}, u32[]{:S(2)}) collective-permute-start(bf16[32,128,128]{2,1,0:T(8,128)(2,1)} %get-tuple-element.15), channel_id=1, source_target_pairs={{0,1},{1,2},{2,3},{4,5},{5,6},{6,7},{8,9},{9,10},{10,11},{12,13},{... | collective-permute-start | bytes 3145736 | tf_op jit(solution)/shard_map/ppermute | solution.py:35
  15.8 2.8 %fusion.16 = (bf16[32,2,128,1]{3,2,1,0:T(8,128)(2,1)}, bf16[32,2,128,1]{3,2,1,0:T(8,128)(2,1)}) fusion(bf16[32,2,128,128]{3,2,1,0:T(8,128)(2,1)S(1)} %copy-done), kind=kLoop, calls=%fused_computation.85 | loop fusion | bytes 65536 | tf_op jit(solution)/shard_map/slice | solution.py:395
  18.6 0.1 tile.30
  18.9 0.4 owner_rank.1.rank
  19.4 0.1 slice.131
  20.6 0.1 broadcast_in_dim_tile.4.bias
  20.8 1.4 %tile.12 = bf16[27,32,4,32]{3,2,1,0:T(4,128)(2,1)} broadcast(bf16[27,32,32]{2,1,0:T(8,128)(2,1)S(1)} %copy-done.4), dimensions={0,1,3} | broadcast | bytes 276480 | tf_op jit(solution)/shard_map/tile | solution.py:427
  22.2 1.9 %tile.26.weight = bf16[27,32,128]{2,1,0:T(8,128)(2,1)S(1)} reshape(bf16[27,32,4,32]{3,2,1,0:T(4,128)(2,1)} %tile.12) | data formatting | bytes 442368 | tf_op jit(solution)/shard_map/tile | solution.py:427
  24.0 2.0 %copy.57 = bf16[32,2,128,1]{2,0,3,1:T(8,128)(2,1)S(1)} copy(bf16[32,2,128,1]{3,2,1,0:T(8,128)(2,1)} %get-tuple-element.16) | data formatting | bytes 32768
  26.0 2.0 %copy.58 = bf16[32,2,128,1]{2,0,3,1:T(8,128)(2,1)S(1)} copy(bf16[32,2,128,1]{3,2,1,0:T(8,128)(2,1)} %get-tuple-element.17) | data formatting | bytes 32768
  28.1 0.2 slice_reduce_fusion.3
  28.3 0.2 slice_reduce_fusion.2
  28.5 0.1 copy.48
  28.6 0.1 copy.46
  28.7 1.3 %collective-permute-start.2 = (bf16[80,256]{1,0:T(8,128)(2,1)S(1)}, bf16[80,256]{1,0:T(8,128)(2,1)S(1)}, u32[]{:S(2)}, u32[]{:S(2)}) collective-permute-start(bf16[80,256]{1,0:T(8,128)(2,1)S(1)} %fusion.8), channel_id=1, source_target_pairs={{4,0},{8,4},{12,8},{5,1},{9,5},{13,9},{6,2},{10,6},{14,10},{7,3},{... | collective-permute-start | bytes 122888 | tf_op jit(solution)/shard_map/ppermute | solution.py:35
  30.1 3.0 %collective-permute-start.1 = (bf16[80,256]{1,0:T(8,128)(2,1)S(1)}, bf16[80,256]{1,0:T(8,128)(2,1)S(1)}, u32[]{:S(2)}, u32[]{:S(2)}) collective-permute-start(bf16[80,256]{1,0:T(8,128)(2,1)S(1)} %fusion.7), channel_id=1, source_target_pairs={{0,4},{4,8},{8,12},{1,5},{5,9},{9,13},{2,6},{6,10},{10,14},{3,7},{... | collective-permute-start | bytes 122888 | tf_op jit(solution)/shard_map/ppermute | solution.py:35
  33.2 0.8 collective-permute-done.1
  34.1 1.3 %collective-permute-start.6 = (bf16[192,128]{1,0:T(8,128)(2,1)S(1)}, bf16[192,128]{1,0:T(8,128)(2,1)S(1)}, u32[]{:S(2)}, u32[]{:S(2)}) collective-permute-start(bf16[192,128]{1,0:T(8,128)(2,1)S(1)} %get-tuple-element.20), channel_id=1, source_target_pairs={{1,0},{2,1},{3,2},{5,4},{6,5},{7,6},{9,8},{10,9},{11,10},{13,12},{... | collective-permute-start | bytes 147464 | tf_op jit(solution)/shard_map/ppermute | solution.py:35
  35.4 4.6 %collective-permute-start.5 = (bf16[320,128]{1,0:T(8,128)(2,1)S(1)}, bf16[320,128]{1,0:T(8,128)(2,1)S(1)}, u32[]{:S(2)}, u32[]{:S(2)}) collective-permute-start(bf16[320,128]{1,0:T(8,128)(2,1)S(1)} %bitcast_dynamic-update-slice_fusion), channel_id=1, source_target_pairs={{0,1},{1,2},{2,3},{4,5},{5,6},{6,7},{8,9},{9,10},{10,11},{12,13},{... | collective-permute-start | bytes 245768 | tf_op jit(solution)/shard_map/ppermute | solution.py:35
  39.9 0.1 copy.52
  40.1 0.1 pad_maximum_fusion.ycode
  40.2 25.2 %own_planes.1 = (f32[16,256,256]{2,1,0:T(8,128)}, bf16[256,1152]{1,0:T(8,128)(2,1)S(1)}) custom-call(bf16[32,2,128,128]{3,2,1,0:T(8,128)(2,1)S(1)} %copy-done, bf16[2,64,128]{2,1,0:T(8,128)(2,1)S(1)} %pad_maximum_fusion.2.rows, bf16[2,64,256]{2,1,0:T(8,128)(2,1)S(1)} %pad_maximum_fusion.1.cols, bf16[27,32,128]{2,1,0:T(8,128)(2,1)S(1)} %tile.26.weight, ...), custom_call_target="tpu_custom_call" | custom-call | flops 10000000000 | bytes 8388608 | tf_op jit(solution)/shard_map/own_planes/pallas_call | solution.py:437
  65.4 6.1 %pair_counts.1.counts = f32[64,256]{1,0:T(8,128)S(1)} custom-call(f32[2,128,128]{2,1,0:T(8,128)S(1)} %convert_element_type.24.frag, f32[2,128,128]{2,1,0:T(8,128)S(1)} %pad_maximum_fusion.ycode, f32[2,1,128]{2,1,0:T(1,128)S(1)} %bitcast.100), custom_call_target="tpu_custom_call" | custom-call | flops 5000000000 | bytes 1048576 | tf_op jit(solution)/shard_map/pair_counts/pallas_call | solution.py:451
  71.5 36.8 %finish.1 = (bf16[3,2,128,128]{3,2,1,0:T(8,128)(2,1)}, f32[32,1,128]{2,1,0:T(1,128)}) custom-call(f32[16,256,256]{2,1,0:T(8,128)} %get-tuple-element.6.acc, bf16[32,128,128]{2,1,0:T(8,128)(2,1)} %collective-permute-done.3.below, bf16[32,128,128]{2,1,0:T(8,128)(2,1)} %collective-permute-done.4.above, bf16[320,128]{1,0:T(8,128)(2,1)S(1)} %collective-permute-done.5.ring_low, ...), custom_call_target="tpu_custom_call" | custom-call | flops 10000000000 | bytes 8388608 | tf_op jit(solution)/shard_map/finish/pallas_call | solution.py:473
  108.4 6.0 %all-to-all-start = ((f32[32,1,128]{2,1,0:T(1,128)}), f32[32,1,128]{2,1,0:T(1,128)S(1)}, u32[]{:S(2)}, u32[]{:S(2)}) async-start(f32[32,1,128]{2,1,0:T(1,128)} %get-tuple-element.9), calls=%async_computation | async-start | bytes 32768 | tf_op jit(solution)/shard_map/all_to_all | solution.py:511
  114.5 7.1 %all-to-all-done.received = f32[32,1,128]{2,1,0:T(1,128)S(1)} async-done(((f32[32,1,128]{2,1,0:T(1,128)}), f32[32,1,128]{2,1,0:T(1,128)S(1)}, u32[]{:S(2)}, u32[]{:S(2)}) %all-to-all-start) | async-done | bytes 16416 | tf_op jit(solution)/shard_map/all_to_all | solution.py:511
  121.6 1.5 %settle.1 = f32[1,384]{1,0:T(1,128)} custom-call(f32[32,1,128]{2,1,0:T(1,128)S(1)} %all-to-all-done.received, s32[32,128]{1,0:T(8,128)S(1)} %pad_add_fusion.slot), custom_call_target="tpu_custom_call" | custom-call | tf_op jit(solution)/shard_map/settle/pallas_call | solution.py:516
  (63 shorter events, 0.9 us)
Async XLA Ops:
  2.7 13.0 %copy-start = (bf16[32,2,128,128]{3,2,1,0:T(8,128)(2,1)S(1)}, bf16[32,2,128,128]{3,2,1,0:T(8,128)(2,1)}, u32[]{:S(2)}) copy-start(bf16[32,2,128,128]{3,2,1,0:T(8,128)(2,1)} %feat.1) | copy-start | bytes 6291460
  2.8 25.3 %collective-permute-start = (bf16[80,128]{1,0:T(8,128)(2,1)S(1)}, bf16[80,128]{1,0:T(8,128)(2,1)S(1)}, u32[]{:S(2)}, u32[]{:S(2)}) collective-permute-start(bf16[80,128]{1,0:T(8,128)(2,1)S(1)} %fusion.11), channel_id=1, source_target_pairs={{0,16},{16,0},{1,17},{17,1},{2,18},{18,2},{3,19},{19,3},{4,20},{20... | collective-permute-start | bytes 61448 | tf_op jit(solution)/shard_map/ppermute | solution.py:30
  8.9 62.6 %collective-permute-start.4 = (bf16[32,128,128]{2,1,0:T(8,128)(2,1)}, bf16[32,128,128]{2,1,0:T(8,128)(2,1)}, u32[]{:S(2)}, u32[]{:S(2)}) collective-permute-start(bf16[32,128,128]{2,1,0:T(8,128)(2,1)} %get-tuple-element.14), channel_id=1, source_target_pairs={{1,0},{2,1},{3,2},{5,4},{6,5},{7,6},{9,8},{10,9},{11,10},{13,12},{... | collective-permute-start | bytes 3145736 | tf_op jit(solution)/shard_map/ppermute | solution.py:35
  10.2 61.3 %collective-permute-start.3 = (bf16[32,128,128]{2,1,0:T(8,128)(2,1)}, bf16[32,128,128]{2,1,0:T(8,128)(2,1)}, u32[]{:S(2)}, u32[]{:S(2)}) collective-permute-start(bf16[32,128,128]{2,1,0:T(8,128)(2,1)} %get-tuple-element.15), channel_id=1, source_target_pairs={{0,1},{1,2},{2,3},{4,5},{5,6},{6,7},{8,9},{9,10},{10,11},{12,13},{... | collective-permute-start | bytes 3145736 | tf_op jit(solution)/shard_map/ppermute | solution.py:35
  15.7 2.9 %copy-start.6 = (bf16[3,32]{1,0:T(4,128)(2,1)S(1)}, bf16[3,32]{1,0:T(4,128)(2,1)}, u32[]{:S(2)}) copy-start(bf16[3,32]{1,0:T(4,128)(2,1)} %param.13) | copy-start | bytes 580
  15.8 3.1 %copy-start.2 = (s32[1024,1]{0,1:T(1,128)S(1)}, s32[1024,1]{0,1:T(1,128)}, u32[]{:S(2)}) copy-start(s32[1024,1]{0,1:T(1,128)} %param.17) | copy-start | bytes 12292
  18.6 0.9 copy-start.3
  18.9 1.4 %copy-start.5 = (s32[1,1536]{1,0:T(1,128)S(1)}, s32[1,1536]{1,0:T(1,128)}, u32[]{:S(2)}) copy-start(s32[1,1536]{1,0:T(1,128)} %param.19) | copy-start | bytes 18436
  18.9 1.5 %copy-start.7 = (f32[3]{0:T(128)S(1)}, f32[3]{0:T(128)}, u32[]{:S(2)}) copy-start(f32[3]{0:T(128)} %param.14) | copy-start | bytes 40
  18.9 1.7 %copy-start.8 = (f32[32]{0:T(128)S(1)}, f32[32]{0:T(128)}, u32[]{:S(2)}) copy-start(f32[32]{0:T(128)} %param.12) | copy-start | bytes 388
  18.9 1.9 %copy-start.4 = (bf16[27,32,32]{2,1,0:T(8,128)(2,1)S(1)}, bf16[27,32,32]{2,1,0:T(8,128)(2,1)}, u32[]{:S(2)}) copy-start(bf16[27,32,32]{2,1,0:T(8,128)(2,1)} %param.11) | copy-start | bytes 165892
  28.7 4.4 %collective-permute-start.2 = (bf16[80,256]{1,0:T(8,128)(2,1)S(1)}, bf16[80,256]{1,0:T(8,128)(2,1)S(1)}, u32[]{:S(2)}, u32[]{:S(2)}) collective-permute-start(bf16[80,256]{1,0:T(8,128)(2,1)S(1)} %fusion.8), channel_id=1, source_target_pairs={{4,0},{8,4},{12,8},{5,1},{9,5},{13,9},{6,2},{10,6},{14,10},{7,3},{... | collective-permute-start | bytes 122888 | tf_op jit(solution)/shard_map/ppermute | solution.py:35
  30.1 3.9 %collective-permute-start.1 = (bf16[80,256]{1,0:T(8,128)(2,1)S(1)}, bf16[80,256]{1,0:T(8,128)(2,1)S(1)}, u32[]{:S(2)}, u32[]{:S(2)}) collective-permute-start(bf16[80,256]{1,0:T(8,128)(2,1)S(1)} %fusion.7), channel_id=1, source_target_pairs={{0,4},{4,8},{8,12},{1,5},{5,9},{9,13},{2,6},{6,10},{10,14},{3,7},{... | collective-permute-start | bytes 122888 | tf_op jit(solution)/shard_map/ppermute | solution.py:35
  34.1 37.4 %collective-permute-start.6 = (bf16[192,128]{1,0:T(8,128)(2,1)S(1)}, bf16[192,128]{1,0:T(8,128)(2,1)S(1)}, u32[]{:S(2)}, u32[]{:S(2)}) collective-permute-start(bf16[192,128]{1,0:T(8,128)(2,1)S(1)} %get-tuple-element.20), channel_id=1, source_target_pairs={{1,0},{2,1},{3,2},{5,4},{6,5},{7,6},{9,8},{10,9},{11,10},{13,12},{... | collective-permute-start | bytes 147464 | tf_op jit(solution)/shard_map/ppermute | solution.py:35
  35.4 36.1 %collective-permute-start.5 = (bf16[320,128]{1,0:T(8,128)(2,1)S(1)}, bf16[320,128]{1,0:T(8,128)(2,1)S(1)}, u32[]{:S(2)}, u32[]{:S(2)}) collective-permute-start(bf16[320,128]{1,0:T(8,128)(2,1)S(1)} %bitcast_dynamic-update-slice_fusion), channel_id=1, source_target_pairs={{0,1},{1,2},{2,3},{4,5},{5,6},{6,7},{8,9},{9,10},{10,11},{12,13},{... | collective-permute-start | bytes 245768 | tf_op jit(solution)/shard_map/ppermute | solution.py:35
  65.4 6.1 %copy-start.1 = (s32[2,1024]{1,0:T(2,128)S(1)}, s32[2,1024]{1,0:T(2,128)}, u32[]{:S(2)}) copy-start(s32[2,1024]{1,0:T(2,128)} %cells.1) | copy-start | bytes 24580
  108.4 13.2 %all-to-all-start = ((f32[32,1,128]{2,1,0:T(1,128)}), f32[32,1,128]{2,1,0:T(1,128)S(1)}, u32[]{:S(2)}, u32[]{:S(2)}) async-start(f32[32,1,128]{2,1,0:T(1,128)} %get-tuple-element.9), calls=%async_computation | async-start | bytes 32768 | tf_op jit(solution)/shard_map/all_to_all | solution.py:511

commit v2 on v0

v2 whole, which is shorter than its diff:
```python
import jax
import jax.numpy as jnp
from jax import lax
from jax.experimental import pallas as pl
from jax.experimental.pallas import tpu as pltpu
from jax.sharding import PartitionSpec as P

F = 64
LANES = 128
GROUPS = 32
TILES = GROUPS + 1
WIDE = TILES * LANES
STACK = 8
STEP = LANES + 8
EDGE = 48
BF = jnp.bfloat16
F32 = jnp.float32
VMEM = pl.BlockSpec(memory_space=pltpu.VMEM)
SMEM = pl.BlockSpec(memory_space=pltpu.SMEM)


def call(kernel, name, out_shape, args, smem, scratch=(), flops=1_000_000):
    return pl.pallas_call(
        kernel,
        out_shape=out_shape,
        in_specs=[VMEM] * (len(args) - smem) + [SMEM] * smem,
        out_specs=jax.tree.map(lambda _: VMEM, out_shape),
        scratch_shapes=list(scratch),
        compiler_params=pltpu.CompilerParams(vmem_limit_bytes=48 << 20),
        cost_estimate=pl.CostEstimate(flops=flops, bytes_accessed=1 << 20, transcendentals=0),
        name=name,
    )(*args)


def shape(dims, dtype):
    return jax.ShapeDtypeStruct(dims, dtype)


def iota(dims, axis):
    return lax.broadcasted_iota(jnp.int32, dims, axis)


def outer_product(left, right):
    return lax.dot_general(left, right, (((1,), (1,)), ((), ())), preferred_element_type=F32)


def halves(value):
    high = value.astype(BF)
    return high, (value - high.astype(F32)).astype(BF)


def layout_kernel(feat, frag, flags, low, high, x_up, x_down, edge, first_col, rows):
    first = flags[0] == 0
    zero = jnp.zeros((32, LANES), BF)
    for z, plane in ((1, high), (0, low)):
        last = zero
        for t in range(8):
            block = jnp.swapaxes(feat[:, z, 16 * t : 16 * t + 16, :], 0, 1).reshape(512, LANES)
            turned = jnp.concatenate([last, block[:480]], axis=0).T
            last = block[480:]
            plane[:, 512 * t : 512 * t + 512] = turned
            for side, line in ((0, turned[112:128].astype(F32)[15:16]), (1, turned[0:16].astype(F32)[0:1])):
                for q in range(4):
                    spot = 4 * t + q
                    rows[2 * side + z, spot : spot + 1, :] = line[:, LANES * q : LANES * (q + 1)]
            if t == 0:
                tile_zero = turned[:, :LANES]
        end = jnp.concatenate([last, zero, zero, zero], axis=0).T
        plane[:, WIDE - LANES : WIDE] = end
        rows[z, TILES - 1 : TILES, :] = end[112:128].astype(F32)[15:16]
        rows[2 + z, TILES - 1 : TILES, :] = end[0:16].astype(F32)[0:1]
        x_up[LANES * z : LANES * (z + 1), :] = jnp.where(first, end, tile_zero)
        x_down[LANES * z : LANES * (z + 1), :] = tile_zero
        turned = frag[z].astype(F32).T
        first_col[z : z + 1, :] = turned[0:1]
        for side in range(2):
            rows[2 * side + z, TILES:EDGE, :] = jnp.broadcast_to(turned[127:128], (EDGE - TILES, LANES))
            edge[2 * side + z] = rows[2 * side + z].astype(BF)
    high[:, WIDE:] = frag[1].astype(F32).astype(BF)
    lines = [jnp.broadcast_to(frag[z, 127:128, :], (8, LANES)).astype(F32) for z in range(2)]
    x_up[2 * LANES :, :] = jnp.concatenate(lines, axis=0).astype(BF)
    x_down[2 * LANES :, :] = jnp.zeros((16, LANES), BF)


def x_face_kernel(low, high, edge, flags, face, x_code, y_up, y_down):
    has_low, has_high = flags[0] > 0, flags[1] > 0
    lane = iota((LANES, LANES), 1)
    is_low = (lane < 32) & has_low
    is_high = (lane >= 32) & (lane < 64) & has_high
    none = jnp.zeros((LANES, LANES), BF)
    for z in range(2):
        lines = slice(LANES * z, LANES * (z + 1))
        tile = jnp.where(is_low, low[lines, :], jnp.where(is_high, high[lines, :], none))
        face[z] = tile
        for side, out in ((0, y_up), (1, y_down)):
            near = (tile[112:128].astype(F32)[15:16], tile[0:16].astype(F32)[0:1])[side]
            line = edge[2 * side + z].astype(F32)
            row, place = iota((EDGE, LANES), 0), iota((EDGE, LANES), 1)
            ends = ((row == 0) & (place < 32)) | ((row == TILES - 1) & (place >= 32) & (place < 64))
            out[z] = jnp.where(ends, jnp.broadcast_to(near, (EDGE, LANES)), line).astype(BF)
        other = low[2 * LANES :, :].astype(F32)[8 * z : 8 * z + 1]
        x_code[z] = jnp.where(has_low, other, -1.0)


def ring_kernel(face, y_low, y_high, up, down):
    for z, out in ((1, up), (0, down)):
        out[:LANES, :] = face[z]
        out[LANES : LANES + EDGE, :] = y_low[z]
        out[LANES + EDGE :, :] = y_high[z]


def banded(weight, z_off, dy, slot, quarter):
    tile = jnp.zeros((32, LANES), BF)
    if abs(z_off) <= 1:
        for q in range(4):
            dx = slot - 1 - q
            if abs(dx) <= 1:
                tile = jnp.where(quarter == q, weight[9 * (z_off + 1) + 3 * (dx + 1) + dy], tile)
    return tile


def own_kernel(low, high, conv_weight, conv_bias, acc, inner, outer, weight, scr):
    quarter = iota((32, LANES), 1) // 32
    for k in range(27):
        one = conv_weight[k].astype(F32).T.astype(BF)
        weight[k] = jnp.concatenate([one] * 4, axis=1)
    for dy in range(3):
        for slot in range(8):
            for z in range(2):
                line = slice(256 * z + 32 * slot, 256 * z + 32 * slot + 32)
                for zo in range(2):
                    inner[dy, line, LANES * zo : LANES * (zo + 1)] = banded(weight, z - zo, dy, slot, quarter)
                outer[z, 32 * slot : 32 * slot + 32, LANES * dy : LANES * (dy + 1)] = banded(
                    weight, 2 * z - 1, dy, slot, quarter
                )
    bias = jnp.concatenate([conv_bias[...]] * 8, axis=1)
    for g in range(STACK):
        scr[STEP * g + 7 : STEP * g + 8, :] = jnp.zeros((1, 768), F32)
        scr[STEP * g + STEP : STEP * g + STEP + 1, :] = jnp.zeros((1, 768), F32)

    def body(s, _):
        base = s * STACK
        left = jnp.concatenate(
            [
                jnp.concatenate(
                    [plane[:, pl.ds(pl.multiple_of((base + g) * LANES, LANES), 2 * LANES)] for g in range(STACK)],
                    axis=0,
                )
                for plane in (low, high)
            ],
            axis=1,
        )
        for dy in range(3):
            part = jnp.dot(left, inner[dy], preferred_element_type=F32)
            for g in range(STACK):
                scr[STEP * g + 8 : STEP * g + STEP, 256 * dy : 256 * dy + 256] = part[LANES * g : LANES * (g + 1)]
        for g in range(STACK):
            o = STEP * g
            acc[base + g] = (
                scr[o + 7 : o + 135, 0:256] + scr[o + 8 : o + 136, 256:512] + scr[o + 9 : o + 137, 512:768] + bias
            )
        return 0

    lax.fori_loop(0, GROUPS // STACK, body, 0)


def line_windows(chunks):
    wide = chunks.astype(F32)
    return jnp.concatenate([wide[:GROUPS], wide[1:TILES]], axis=1).astype(BF)


def edge_kernel(face, y_low, y_high, inner, lines, ends):
    for side, (dy, source) in enumerate(((0, y_low), (2, y_high))):
        left = jnp.concatenate([line_windows(source[z]) for z in range(2)], axis=1)
        lines[side] = jnp.dot(left, inner[dy], preferred_element_type=F32)
    row = iota((LANES, 256), 0)
    lane = iota((LANES, LANES), 1)
    none = jnp.zeros((LANES, LANES), BF)
    for end in range(2):
        keep = lane < 32 if end == 0 else lane >= 32
        tiles = [jnp.where(keep, face[z], none) for z in range(2)]
        parts = []
        for dy in range(3):
            right = [inner[dy, 256 * z + LANES * end : 256 * z + LANES * end + LANES, :] for z in range(2)]
            parts.append(
                jnp.dot(
                    jnp.concatenate(tiles, axis=1), jnp.concatenate(right, axis=0), preferred_element_type=F32
                )
            )
        ends[end] = (
            jnp.where(row == 0, 0.0, pltpu.roll(parts[0], 1, 0))
            + parts[1]
            + jnp.where(row == LANES - 1, 0.0, pltpu.roll(parts[2], LANES - 1, 0))
        )


def spread(row, copies):
    one = jnp.broadcast_to(row, (16, LANES)).astype(BF)
    return jnp.concatenate([one] * copies, axis=0)


def numbers(rows):
    return iota((rows, LANES), 0).astype(F32).astype(BF)


def table_rows(t, frag, y_code, weight_row, own_hot, pair_hot, outer_z):
    one = jnp.ones((F, LANES), BF)
    none = jnp.zeros((F, LANES), BF)
    names = numbers(F)
    for j in range(16):
        x = 16 * t + j
        line = pl.ds(x, 1)
        before = pl.ds(jnp.maximum(x - 1, 0), 1)
        hot = [spread(frag[z, line, :], 4) == names for z in range(2)]
        spot = slice(LANES * j, LANES * (j + 1))
        for z in range(2):
            own_hot[z, :, spot] = jnp.where(hot[z], one, none)
            earlier = frag[z, before, :] + (jnp.where(x > 0, 0.0, -128.0) if j == 0 else 0.0)
            pair_hot[z, 0:F, spot] = jnp.where(spread(earlier, 4) == names, weight_row(1, z, x), none)
            pair_hot[z, F : 2 * F, spot] = jnp.where(
                spread(y_code[z, line, :], 4) == names, weight_row(2, z, x), none
            )
        pair_hot[1, 2 * F : 3 * F, spot] = jnp.where(hot[0], weight_row(0, 1, x), none)
        outer_z(line, x, spot, names, one, none)


def faces_product(own, partner, weight):
    names = numbers(F)
    one, none = jnp.ones((F, LANES), BF), jnp.zeros((F, LANES), BF)
    left = [jnp.where(spread(row, 4) == names, one, none) for row in own]
    right = [jnp.where(spread(row, 4) == names, spread(value, 4), none) for row, value in zip(partner, weight)]
    return outer_product(jnp.concatenate(left, axis=1), jnp.concatenate(right, axis=1))


def load_numbers(frag, plain, y_code):
    lane = iota((LANES, LANES), 1)
    for z in range(2):
        value = frag[z].astype(F32)
        plain[z] = value
        y_code[z] = jnp.where(lane == 0, -1.0, pltpu.roll(value, 1, 1))


def y_partner(y_low, z, has_low):
    return jnp.where(has_low, y_low[z, TILES - 1 :, :].astype(F32)[8:9], -1.0)


def count_kernel(frag, x_code, y_low, first_col, flags, out, own_hot, pair_hot, plain, y_code):
    load_numbers(frag, plain, y_code)
    unit = jnp.ones((F, LANES), BF)

    def body(t, carry):
        low, high = carry
        table_rows(t, plain, y_code, lambda *_: unit, own_hot, pair_hot, lambda *_: None)
        low = low + outer_product(own_hot[0], pair_hot[0, : 2 * F])
        high = high + outer_product(own_hot[1], pair_hot[1])
        return low, high

    low, high = lax.fori_loop(0, 8, body, (jnp.zeros((F, 2 * F), F32), jnp.zeros((F, 3 * F), F32)))
    own = low[:, :F] + low[:, F:] + high[:, :F] + high[:, F : 2 * F] + high[:, 2 * F :]
    ones = [jnp.ones((1, LANES), F32)] * 2
    x_outer = faces_product([plain[z, 0:1, :] for z in range(2)], [x_code[z] for z in range(2)], ones)
    y_outer = faces_product(
        [first_col[z : z + 1, :] for z in range(2)], [y_partner(y_low, z, flags[2] > 0) for z in range(2)], ones
    )
    out[...] = jnp.concatenate([own, jnp.zeros((F, F), F32), x_outer, y_outer], axis=1)


def slots_kernel(owner, recv, rank, place):
    slots = owner.shape[1]
    devices = place.shape[0]
    capacity = recv.shape[1] // devices
    hot = iota((devices, slots), 0) == owner[...]
    before = iota((slots, slots), 0) < iota((slots, slots), 1)
    earlier = jnp.dot(
        jnp.where(hot, 1.0, 0.0).astype(BF), jnp.where(before, 1.0, 0.0).astype(BF), preferred_element_type=F32
    )
    rank[...] = jnp.sum(jnp.where(hot, earlier, 0.0), axis=0, keepdims=True).astype(jnp.int32)
    place[...] = jnp.full(place.shape, -4 * LANES, jnp.int32)
    for p in range(devices):
        piece = recv[:, capacity * p : capacity * (p + 1)]
        place[p : p + 1, 0:capacity] = piece
        place[p : p + 1, F : F + capacity] = piece


def finish_kernel(
    acc,
    below,
    above,
    ring_low,
    ring_high,
    inner_lines,
    inner_ends,
    outer,
    head_weight,
    frag,
    x_code,
    y_low,
    first_col,
    counts,
    cells,
    owner,
    rank,
    head_bias,
    flags,
    edge_count,
    affinity,
    outgoing,
    planes,
    scr,
    lines,
    kept,
    own_hot,
    pair_hot,
    plain,
    y_code,
    z_code,
):
    load_numbers(frag, plain, y_code)
    z_code[...] = jnp.where(flags[3] > 0, below[:, WIDE:].astype(F32), -1.0)
    lane = iota((LANES, LANES), 1)
    for i, (plane, ring) in enumerate(((below, ring_low), (above, ring_high))):
        planes[i, :, LANES : WIDE - LANES] = plane[:, LANES : WIDE - LANES]
        face = ring[:LANES, :]
        planes[i, :, :LANES] = jnp.where(lane < 32, face, plane[:, :LANES])
        planes[i, :, WIDE - LANES :] = jnp.where(
            (lane >= 32) & (lane < 64), face, plane[:, WIDE - LANES : WIDE]
        )
        half = slice(LANES * i, LANES * (i + 1))
        for side, dy in ((0, 0), (1, 2)):
            chunks = ring[LANES + EDGE * side : LANES + EDGE * (side + 1), :]
            lines[side, :, half] = inner_lines[side, :, half] + jnp.dot(
                line_windows(chunks), outer[i, :, LANES * dy : LANES * (dy + 1)], preferred_element_type=F32
            )
    line, spot = iota((8, 256), 0), iota((8, 256), 1)
    head = []
    for d in range(3):
        weights = jnp.concatenate([head_weight[d : d + 1, :].astype(F32)] * 8, axis=1)
        for z in range(2):
            match = (spot // LANES == z) & ((spot // 32) % 4 == line % 4)
            head.append(jnp.where(match, jnp.broadcast_to(weights, (8, 256)), 0.0))
    head = jnp.concatenate(head, axis=0).astype(BF)
    top_half = iota((8, LANES), 0) < 4

    def weight_row(d, z, x):
        return spread(kept[2 * d + z, pl.ds(x, 1), :], 4)

    def outer_z(at, x, place, names, one, none):
        hot = spread(z_code[at, :], 4) == names
        pair_hot[0, 2 * F : 3 * F, place] = jnp.where(hot, weight_row(0, 0, x), none)
        pair_hot[0, 3 * F :, place] = jnp.where(hot, one, none)

    def body(s, carry):
        low, high = carry
        base = s * STACK
        for i in range(2):
            left = jnp.concatenate(
                [
                    planes[i, :, pl.ds(pl.multiple_of((base + g) * LANES, LANES), 2 * LANES)]
                    for g in range(STACK)
                ],
                axis=0,
            )
            part = jnp.dot(left, outer[i], preferred_element_type=F32)
            half = slice(LANES * i, LANES * (i + 1))
            ends = [lines[side, pl.ds(pl.multiple_of(base, 8), STACK), half] for side in range(2)]
            for g in range(STACK):
                o = STEP * g
                scr[i, o + 8 : o + STEP, :] = part[LANES * g : LANES * (g + 1)]
                scr[i, o + 7 : o + 8, 0:LANES] = ends[0][g : g + 1]
                scr[i, o + STEP : o + STEP + 1, 2 * LANES :] = ends[1][g : g + 1]
        hidden = []
        for g in range(STACK):
            o = STEP * g
            outside = [
                scr[i, o + 7 : o + 135, 0:LANES]
                + scr[i, o + 8 : o + 136, LANES : 2 * LANES]
                + scr[i, o + 9 : o + 137, 2 * LANES :]
                for i in range(2)
            ]
            total = acc[base + g] + jnp.concatenate(outside, axis=1)
            if g == 0:
                total = total + jnp.where(s == 0, inner_ends[0], 0.0)
            if g == STACK - 1:
                total = total + jnp.where(s == GROUPS // STACK - 1, inner_ends[1], 0.0)
            hidden.append(jnp.maximum(total, 0.0).astype(BF))
        logits = outer_product(head, jnp.concatenate(hidden, axis=0))
        for i in range(6):
            for pair in range(STACK // 2):
                at = 2 * LANES * pair
                both = logits[8 * i : 8 * i + 8]
                value = jnp.where(top_half, both[:, at : at + LANES], both[:, at + LANES : at + 2 * LANES])
                value = jax.nn.sigmoid(value + head_bias[i // 2]).astype(BF).astype(F32)
                kept[i, pl.ds(pl.multiple_of(4 * STACK * s + 8 * pair, 8), 8), :] = value
            all_lines = pl.ds(pl.multiple_of(4 * STACK * s, 16), 4 * STACK)
            affinity[i // 2, i % 2, all_lines, :] = kept[i, all_lines, :].astype(BF)
        for t in range(STACK // 4):
            table_rows(STACK // 4 * s + t, plain, y_code, weight_row, own_hot, pair_hot, outer_z)
            low = low + outer_product(own_hot[0], pair_hot[0])
            high = high + outer_product(own_hot[1], pair_hot[1, : 3 * F])
        return low, high

    low, high = lax.fori_loop(
        0, GROUPS // STACK, body, (jnp.zeros((F, 4 * F), F32), jnp.zeros((F, 3 * F), F32))
    )
    own = low[:, :F] + low[:, F : 2 * F] + high[:, :F] + high[:, F : 2 * F] + high[:, 2 * F :]
    x_outer = faces_product(
        [plain[z, 0:1, :] for z in range(2)],
        [x_code[z] for z in range(2)],
        [kept[2 + z, 0:1, :] for z in range(2)],
    )
    y_outer = faces_product(
        [first_col[z : z + 1, :] for z in range(2)],
        [y_partner(y_low, z, flags[2] > 0) for z in range(2)],
        [kept[4 + z].T[0:1, :] for z in range(2)],
    )
    sums = jnp.concatenate([own, low[:, 2 * F : 3 * F], x_outer, y_outer], axis=1)
    tally = counts[...] + jnp.concatenate(
        [jnp.zeros((F, F), F32), low[:, 3 * F :], jnp.zeros((F, 2 * F), F32)], axis=1
    )
    slots = cells.shape[1]
    code = jnp.concatenate([cells[0:1, :], cells[1:2, :]], axis=1)
    column_hot = jnp.where(iota((4 * F, 2 * slots), 0) == (code & (4 * F - 1)), 1.0, 0.0).astype(BF)
    picked = jnp.dot(
        jnp.concatenate(halves(sums) + halves(tally), axis=0), column_hot, preferred_element_type=F32
    )
    line_hot = iota((F, 2 * slots), 0) == (code >> 8)
    alive = iota((1, slots), 1) < edge_count[0]

    def part_of(value):
        total = jnp.sum(jnp.where(line_hot, value, 0.0), axis=0, keepdims=True)
        return jnp.where(alive, total[:, :slots] + total[:, slots:], 0.0)

    part_sum = part_of(picked[:F] + picked[F : 2 * F])
    part_count = part_of(picked[2 * F : 3 * F] + picked[3 * F :])
    to_owner = iota((outgoing.shape[0], slots), 0) == owner[...]
    lanes = iota((LANES, slots), 0)
    low_hot = jnp.where(lanes == rank[...], 1.0, 0.0).astype(BF)
    high_hot = jnp.where(lanes == rank[...] + F, 1.0, 0.0).astype(BF)
    left = [
        jnp.where(to_owner, piece.astype(F32), 0.0).astype(BF) for piece in halves(part_sum) + halves(part_count)
    ]
    sent = outer_product(
        jnp.concatenate(left, axis=1), jnp.concatenate([low_hot, low_hot, high_hot, high_hot], axis=1)
    )
    outgoing[...] = sent.reshape(outgoing.shape)


def settle_kernel(received, slot, out, left, right):
    devices = received.shape[0]
    groups = out.shape[1] // LANES
    names = iota((LANES, LANES), 0)
    row, lane = iota((16, LANES), 0), iota((16, LANES), 1)
    of_count = row >= 2 * groups
    inner = jnp.where(of_count, row - 2 * groups, row)
    is_low = inner >= groups
    group = jnp.where(is_low, inner - groups, inner)
    group = jnp.where((lane >= F) == of_count, group, -1)
    group = jnp.where(row < 4 * groups, group, -1)

    def body(p, _):
        spot = pl.ds(pl.multiple_of(p * LANES, LANES), LANES)
        code = slot[pl.ds(p, 1), :]
        value = received[p]
        high = value.astype(BF).astype(F32)
        piece = jnp.where(is_low, value - high, high)
        left[:, spot] = jnp.where((code >> 7) == group, piece, 0.0).astype(BF)
        right[:, spot] = jnp.where((code & (LANES - 1)) == names, 1.0, 0.0).astype(BF)
        return 0

    lax.fori_loop(0, devices, body, 0, unroll=8)
    total = outer_product(left[...], right[...])
    for g in range(groups):
        total_sum = total[g : g + 1] + total[groups + g : groups + g + 1]
        total_count = total[2 * groups + g : 2 * groups + g + 1] + total[3 * groups + g : 3 * groups + g + 1]
        out[:, LANES * g : LANES * (g + 1)] = total_sum / jnp.maximum(total_count, 1.0)


def exchange(up, down, axis):
    n = lax.axis_size(axis)
    if n == 1:
        return jnp.zeros_like(up), jnp.zeros_like(down)
    forward = [(i, i + 1) for i in range(n - 1)]
    backward = [(i + 1, i) for i in range(n - 1)]
    return lax.ppermute(up, axis, forward), lax.ppermute(down, axis, backward)


def shards(
    features,
    conv_weight,
    conv_bias,
    head_weight,
    head_bias,
    fragments,
    edge_cells,
    edge_owner,
    edge_count,
    recv_slot,
):
    axes = ("gx", "gy", "gz")
    size = {axis: lax.axis_size(axis) for axis in axes}
    at = {axis: lax.axis_index(axis) for axis in axes}
    devices = size["gx"] * size["gy"] * size["gz"]
    capacity = recv_slot.shape[1] // devices
    slots = edge_cells.shape[1]
    own_slots = devices * capacity // 4
    flags = jnp.stack([at["gx"], size["gx"] - 1 - at["gx"], at["gy"], at["gz"]]).astype(jnp.int32)
    pair = size["gx"] == 2
    send_up = flags if pair else jnp.zeros_like(flags)

    xt_low, xt_high, x_up, x_down, edge, first_col = call(
        layout_kernel,
        "layout",
        (
            shape((LANES, WIDE), BF),
            shape((LANES, WIDE + LANES), BF),
            shape((2 * LANES + 16, LANES), BF),
            shape((2 * LANES + 16, LANES), BF),
            shape((4, EDGE, LANES), BF),
            shape((2, LANES), F32),
        ),
        (features, fragments, send_up),
        1,
        [pltpu.VMEM((4, EDGE, LANES), F32)],
    )
    below, above = exchange(xt_high, xt_low, "gz")
    if pair:
        x_low = x_high = lax.ppermute(x_up, "gx", [(0, 1), (1, 0)])
    else:
        x_low, x_high = exchange(x_up, x_down, "gx")

    acc, inner, outer = call(
        own_kernel,
        "own_planes",
        (shape((GROUPS, LANES, 256), F32), shape((3, 512, 256), BF), shape((2, 256, 3 * LANES), BF)),
        (xt_low, xt_high, conv_weight, conv_bias.reshape(1, -1)),
        0,
        [pltpu.VMEM((27, 32, LANES), BF), pltpu.VMEM((STEP * STACK + 8, 768), F32)],
        flops=5_000_000_000,
    )
    owner = edge_owner.reshape(1, slots)
    rank, place = call(
        slots_kernel,
        "slots",
        (shape((1, slots), jnp.int32), shape((devices, LANES), jnp.int32)),
        (owner, recv_slot),
        0,
    )
    face, x_code, y_up, y_down = call(
        x_face_kernel,
        "x_face",
        (
            shape((2, LANES, LANES), BF),
            shape((2, 1, LANES), F32),
            shape((2, EDGE, LANES), BF),
            shape((2, EDGE, LANES), BF),
        ),
        (x_low, x_high, edge, flags),
        1,
    )
    y_low, y_high = exchange(y_up, y_down, "gy")
    ring_up, ring_down = call(
        ring_kernel, "ring", (shape((LANES + 2 * EDGE, LANES), BF),) * 2, (face, y_low, y_high), 0
    )
    ring_low, ring_high = exchange(ring_up, ring_down, "gz")

    lines, ends = call(
        edge_kernel,
        "edges",
        (shape((2, GROUPS, 256), F32), shape((2, LANES, 256), F32)),
        (face, y_low, y_high, inner),
        0,
        flops=500_000_000,
    )
    counts = call(
        count_kernel,
        "pair_counts",
        shape((F, 4 * F), F32),
        (fragments, x_code, y_low, first_col, flags),
        1,
        [
            pltpu.VMEM((2, F, 2048), BF),
            pltpu.VMEM((2, 3 * F, 2048), BF),
            pltpu.VMEM((2, LANES, LANES), F32),
            pltpu.VMEM((2, LANES, LANES), F32),
        ],
        flops=4_000_000_000,
    )
    affinity, outgoing = call(
        finish_kernel,
        "finish",
        (shape((3, 2, LANES, LANES), BF), shape((devices, 1, LANES), F32)),
        (
            acc,
            below,
            above,
            ring_low,
            ring_high,
            lines,
            ends,
            outer,
            head_weight,
            fragments,
            x_code,
            y_low,
            first_col,
            counts,
            edge_cells,
            owner,
            rank,
            head_bias,
            flags,
            edge_count,
        ),
        3,
        [
            pltpu.VMEM((2, LANES, WIDE), BF),
            pltpu.VMEM((2, STEP * STACK + 8, 3 * LANES), F32),
            pltpu.VMEM((2, GROUPS, 256), F32),
            pltpu.VMEM((6, LANES, LANES), F32),
            pltpu.VMEM((2, F, 2048), BF),
            pltpu.VMEM((2, 4 * F, 2048), BF),
            pltpu.VMEM((2, LANES, LANES), F32),
            pltpu.VMEM((2, LANES, LANES), F32),
            pltpu.VMEM((LANES, LANES), F32),
        ],
        flops=8_000_000_000,
    )
    received = lax.all_to_all(outgoing, axes, split_axis=0, concat_axis=0, tiled=True)
    edge_mean = call(
        settle_kernel,
        "settle",
        shape((1, own_slots), F32),
        (received, place),
        0,
        [pltpu.VMEM((16, devices * LANES), BF), pltpu.VMEM((LANES, devices * LANES), BF)],
    )
    return affinity, edge_mean


def solution(mesh):
    in_specs = (
        P(None, "gz", "gx", "gy"),
        P(),
        P(),
        P(),
        P(),
        P("gz", "gx", "gy"),
        P(None, ("gx", "gy", "gz")),
        P(("gx", "gy", "gz"), None),
        P(("gx", "gy", "gz")),
        P(("gx", "gy", "gz"), None),
    )
    out_specs = (P(None, "gz", "gx", "gy"), P(("gx", "gy", "gz"), None))
    return jax.shard_map(shards, mesh=mesh, in_specs=in_specs, out_specs=out_specs, check_vma=False)
```

time: 351 us -> 72.1 us (0.21)
  matrix products: 115 us -> 0 us
  local copies, waits for them, and re-layouts: 94.2 us -> 2.79 us
  waiting for transfers between devices: 54.9 us -> 2.83 us
  other arithmetic: 47.3 us -> 0.08 us
  Pallas kernels: 0 us -> 31.3 us
  starting transfers between devices: 29.2 us -> 16.3 us
  blocking collectives: 7.06 us -> 16.9 us
    dot_general x4 -> x0, matrix products: 85.6 us -> none  [the longest x3 82.7 us: shards(): jnp.dot(left_side, partner_hot, preferred_element_type=jnp.float32)]
    ppermute x9 -> x7, waiting for transfers between devices: 50.2 us -> 2.83 us  [the longest x1 2.82 us: shards(): x_low = x_high = lax.ppermute(x_up, 'gx', [(0, 1), (1, 0)])]
    conv_general_dilated x3 -> x0, local copies, waits for them, and re-layouts: 39.3 us -> none  [shards(): lax.conv_general_dilated(padded[None], kernel, (1, 1, 1), 'VALID', dimens...]
    pallas_call x0 -> x9, Pallas kernels: none -> 31.3 us  [call(): pl.pallas_call(kernel, out_shape=out_shape, in_specs=[VMEM] * (len(args)...]
    conv_general_dilated x1 -> x0, matrix products: 29 us -> none  [shards(): lax.conv_general_dilated(padded[None], kernel, (1, 1, 1), 'VALID', dimens...]
    gather x4 -> x0, local copies, waits for them, and re-layouts: 24.6 us -> none  [the longest x2 12.3 us: shards(): part_sum = (table_sum[edge_cells[0]] + table_sum[edge_cells[1]]) * live_mask]
    scatter-add x2 -> x0, other arithmetic: 15 us -> none  [the longest x1 8.8 us: shards(): jax.ops.segment_sum(received.T, recv_slot[0], num_segments=own_slots)]
    all_to_all x1, blocking collectives: 7.06 us -> 16.9 us  [shards(): lax.all_to_all(outgoing, axes, split_axis=0, concat_axis=0, tiled=True)]
  transfers between devices with their start and end apart: 10 -> 7, of which waited for: 4 -> 1; matrix products, arithmetic and copies ran while one was open for 11% -> 0% of each run, Pallas kernels for 0% -> 19%
where the time goes in v2:
time: 72.1 us; the launch traced here: 71.7 us
  Pallas kernels  31.3 us (43%)
  blocking collectives  16.9 us (23%)
  starting transfers between devices  16.3 us (23%)
  waiting for transfers between devices  2.83 us (4%)
  local copies, waits for them, and re-layouts  2.79 us (4%)
  between operations  1.51 us (2%)
    pallas_call x9, Pallas kernels, call(): pl.pallas_call(kernel, out_shape=out_shape, in_specs=[VMEM] * (len(args)...  31.3 us
    all_to_all x1, blocking collectives, shards(): lax.all_to_all(outgoing, axes, split_axis=0, concat_axis=0, tiled=True)  16.9 us
    ppermute x6, starting transfers between devices, exchange(): return (lax.ppermute(up, axis, forward), lax.ppermute(down, axis, backward))  14.7 us
    ppermute x1, waiting for transfers between devices, shards(): x_low = x_high = lax.ppermute(x_up, 'gx', [(0, 1), (1, 0)])  2.82 us
    unnamed x20, local copies, waits for them, and re-layouts  2.79 us
    ppermute x1, starting transfers between devices, shards(): x_low = x_high = lax.ppermute(x_up, 'gx', [(0, 1), (1, 0)])  1.56 us
  transfers between devices with their start and end apart: 7, of which 1 were waited for; matrix products, arithmetic and copies ran while one was open for 0% of the time, Pallas kernels for 19%

profile of v2, /device:TPU:0, one launch (start us, length us, event | category | flops | bytes accessed | tf_op | source)
XLA Modules:
  0.0 71.7 jit_solution(18087285301989739724)
XLA Ops:
  0.6 0.1 pad_add_fusion.flags
  0.7 1.6 %copy-done = bf16[32,2,128,128]{3,2,1,0:T(8,128)(2,1)S(1)} copy-done((bf16[32,2,128,128]{3,2,1,0:T(8,128)(2,1)S(1)}, bf16[32,2,128,128]{3,2,1,0:T(8,128)(2,1)}, u32[]{:S(2)}) %copy-start) | copy-done | bytes 2097176
  2.3 0.9 %copy-done.1 = s32[2,128,128]{2,1,0:T(8,128)S(1)} copy-done((s32[2,128,128]{2,1,0:T(8,128)S(1)}, s32[2,128,128]{2,1,0:T(8,128)}, u32[]{:S(2)}) %copy-start.1) | copy-done | bytes 131096
  3.2 1.7 %layout.1 = (bf16[128,4224]{1,0:T(8,128)(2,1)S(1)}, bf16[128,4352]{1,0:T(8,128)(2,1)S(1)}, bf16[272,128]{1,0:T(8,128)(2,1)S(1)}, bf16[272,128]{1,0:T(8,128)(2,1)...) custom-call(bf16[32,2,128,128]{3,2,1,0:T(8,128)(2,1)S(1)} %copy-done, s32[2,128,128]{2,1,0:T(8,128)S(1)} %copy-done.1, ...), custom_call_target="tpu_custom_call" | custom-call | flops 1000000 | bytes 1048576 | tf_op jit(solution)/shard_map/layout/pallas_call | solution.py:23
  4.9 5.0 %collective-permute-start = (bf16[128,4352]{1,0:T(8,128)(2,1)S(1)}, bf16[128,4352]{1,0:T(8,128)(2,1)S(1)}, u32[]{:S(2)}, u32[]{:S(2)}) collective-permute-start(bf16[128,4352]{1,0:T(8,128)(2,1)S(1)} %get-tuple-element.23.high), channel_id=1, source_target_pairs={{0,1},{1,2},{2,3},{4,5},{5,6},{6,7},{8,9},{9,10},{10,11},{12,13},{... | collective-permute-start | bytes 3342344 | tf_op jit(solution)/shard_map/ppermute | solution.py:484
  9.9 1.3 %collective-permute-start.1 = (bf16[128,4224]{1,0:T(8,128)(2,1)S(1)}, bf16[128,4224]{1,0:T(8,128)(2,1)S(1)}, u32[]{:S(2)}, u32[]{:S(2)}) collective-permute-start(bf16[128,4224]{1,0:T(8,128)(2,1)S(1)} %get-tuple-element.22.low), channel_id=1, source_target_pairs={{1,0},{2,1},{3,2},{5,4},{6,5},{7,6},{9,8},{10,9},{11,10},{13,12},{... | collective-permute-start | bytes 3244040 | tf_op jit(solution)/shard_map/ppermute | solution.py:484
  11.2 1.6 %collective-permute-start.2 = (bf16[272,128]{1,0:T(8,128)(2,1)S(1)}, bf16[272,128]{1,0:T(8,128)(2,1)S(1)}, u32[]{:S(2)}, u32[]{:S(2)}) collective-permute-start(bf16[272,128]{1,0:T(8,128)(2,1)S(1)} %get-tuple-element.25), channel_id=1, source_target_pairs={{0,16},{16,0},{1,17},{17,1},{2,18},{18,2},{3,19},{19,3},{4,20},{20... | collective-permute-start | bytes 208904 | tf_op jit(solution)/shard_map/ppermute | solution.py:527
  12.7 2.8 %collective-permute-done.2.low.high = bf16[272,128]{1,0:T(8,128)(2,1)S(1)} collective-permute-done((bf16[272,128]{1,0:T(8,128)(2,1)S(1)}, bf16[272,128]{1,0:T(8,128)(2,1)S(1)}, u32[]{:S(2)}, u32[]{:S(2)}) %collective-permute-start.2) | collective-permute-done | bytes 69664 | tf_op jit(solution)/shard_map/ppermute | solution.py:527
  15.6 0.6 x_face.1
  16.1 1.3 %collective-permute-start.3 = (bf16[2,48,128]{2,1,0:T(8,128)(2,1)S(1)}, bf16[2,48,128]{2,1,0:T(8,128)(2,1)S(1)}, u32[]{:S(2)}, u32[]{:S(2)}) collective-permute-start(bf16[2,48,128]{2,1,0:T(8,128)(2,1)S(1)} %get-tuple-element.28), channel_id=1, source_target_pairs={{0,4},{4,8},{8,12},{1,5},{5,9},{9,13},{2,6},{6,10},{10,14},{3,7},{... | collective-permute-start | bytes 73736 | tf_op jit(solution)/shard_map/ppermute | solution.py:484
  17.4 1.3 %collective-permute-start.4 = (bf16[2,48,128]{2,1,0:T(8,128)(2,1)S(1)}, bf16[2,48,128]{2,1,0:T(8,128)(2,1)S(1)}, u32[]{:S(2)}, u32[]{:S(2)}) collective-permute-start(bf16[2,48,128]{2,1,0:T(8,128)(2,1)S(1)} %get-tuple-element.29), channel_id=1, source_target_pairs={{4,0},{8,4},{12,8},{5,1},{9,5},{13,9},{6,2},{10,6},{14,10},{7,3},{... | collective-permute-start | bytes 73736 | tf_op jit(solution)/shard_map/ppermute | solution.py:484
  18.8 0.0 copy-start.3
  18.8 0.0 copy-start.4
  18.8 0.0 copy-start.2
  18.8 6.5 %own_planes.1 = (f32[32,128,256]{2,1,0:T(8,128)}, bf16[3,512,256]{2,1,0:T(8,128)(2,1)S(1)}, bf16[2,256,384]{2,1,0:T(8,128)(2,1)S(1)}) custom-call(bf16[128,4224]{1,0:T(8,128)(2,1)S(1)} %get-tuple-element.22.low, bf16[128,4352]{1,0:T(8,128)(2,1)S(1)} %get-tuple-element.23.high, bf16[27,32,32]{2,1,0:T(8,128)(2,1)S(1)} %copy-done.5, f32[1,32]{1,0:T(1,128)S(1)} %bitcast.8), custom_call_target="tpu_custom_call" | custom-call | flops 5000000000 | bytes 1048576 | tf_op jit(solution)/shard_map/own_planes/pallas_call | solution.py:23
  26.0 0.4 slots.1
  26.4 0.0 collective-permute-done.3.y_low
  26.4 0.0 collective-permute-done.4.y_high
  26.4 4.6 %collective-permute-start.5 = (bf16[224,128]{1,0:T(8,128)(2,1)S(1)}, bf16[224,128]{1,0:T(8,128)(2,1)S(1)}, u32[]{:S(2)}, u32[]{:S(2)}) collective-permute-start(bf16[224,128]{1,0:T(8,128)(2,1)S(1)} %get-tuple-element.30), channel_id=1, source_target_pairs={{0,1},{1,2},{2,3},{4,5},{5,6},{6,7},{8,9},{9,10},{10,11},{12,13},{... | collective-permute-start | bytes 172040 | tf_op jit(solution)/shard_map/ppermute | solution.py:484
  31.0 1.3 %collective-permute-start.6 = (bf16[224,128]{1,0:T(8,128)(2,1)S(1)}, bf16[224,128]{1,0:T(8,128)(2,1)S(1)}, u32[]{:S(2)}, u32[]{:S(2)}) collective-permute-start(bf16[224,128]{1,0:T(8,128)(2,1)S(1)} %get-tuple-element.31), channel_id=1, source_target_pairs={{1,0},{2,1},{3,2},{5,4},{6,5},{7,6},{9,8},{10,9},{11,10},{13,12},{... | collective-permute-start | bytes 172040 | tf_op jit(solution)/shard_map/ppermute | solution.py:484
  32.3 5.9 %pair_counts.1.counts = f32[64,256]{1,0:T(8,128)S(1)} custom-call(s32[2,128,128]{2,1,0:T(8,128)S(1)} %copy-done.2, f32[2,1,128]{2,1,0:T(1,128)S(1)} %get-tuple-element.36.x_code, bf16[2,48,128]{2,1,0:T(8,128)(2,1)S(1)} %collective-permute-done.3.y_low, f32[2,128]{1,0:T(2,128)S(1)} %get-tuple-element.37.first_col, s32[4]{0:T(128)S(1)} %pad_add_fusion.flags), custom_call_target="tpu_custom_call" | custom-call | flops 4000000000 | bytes 1048576 | tf_op jit(solution)/shard_map/pair_counts/pallas_call | solution.py:23
  38.2 0.0 copy-start.6
  38.2 0.0 copy-start.7
  38.2 0.0 copy-start.9
  38.2 0.4 edges.1
  38.6 0.0 collective-permute-done.5.ring_low
  38.6 0.0 collective-permute-done.1.above
  38.6 0.0 collective-permute-done.below
  38.6 0.3 copy-done.6
  38.9 14.5 %finish.1 = (bf16[3,2,128,128]{3,2,1,0:T(8,128)(2,1)}, f32[32,1,128]{2,1,0:T(1,128)S(1)}) custom-call(f32[32,128,256]{2,1,0:T(8,128)} %get-tuple-element.24.acc, bf16[128,4352]{1,0:T(8,128)(2,1)S(1)} %collective-permute-done.below, bf16[128,4224]{1,0:T(8,128)(2,1)S(1)} %collective-permute-done.1.above, bf16[224,128]{1,0:T(8,128)(2,1)S(1)} %collective-permute-done.5.ring_low, ...), custom_call_target="tpu_custom_call" | custom-call | flops 8000000000 | bytes 1048576 | tf_op jit(solution)/shard_map/finish/pallas_call | solution.py:23
  53.3 16.9 %all_to_all.5.received = f32[32,1,128]{2,1,0:T(1,128)S(1)} all-to-all(f32[32,1,128]{2,1,0:T(1,128)S(1)} %get-tuple-element.40), channel_id=1, replica_groups=mesh['gx'=2,'gy'=4,'gz'=4] {'gx','gy','gz'}, dimensions={0} | all-to-all | bytes 32768 | tf_op jit(solution)/shard_map/all_to_all | solution.py:628
  70.2 1.5 %settle.1 = f32[1,384]{1,0:T(1,128)} custom-call(f32[32,1,128]{2,1,0:T(1,128)S(1)} %all_to_all.5.received, s32[32,128]{1,0:T(8,128)S(1)} %get-tuple-element.41.slot), custom_call_target="tpu_custom_call" | custom-call | flops 1000000 | bytes 1048576 | tf_op jit(solution)/shard_map/settle/pallas_call | solution.py:23
  (13 shorter events, 0.0 us)
Async XLA Ops:
  0.7 1.6 %copy-start = (bf16[32,2,128,128]{3,2,1,0:T(8,128)(2,1)S(1)}, bf16[32,2,128,128]{3,2,1,0:T(8,128)(2,1)}, u32[]{:S(2)}) copy-start(bf16[32,2,128,128]{3,2,1,0:T(8,128)(2,1)} %feat.1) | copy-start | bytes 6291460
  2.3 0.9 %copy-start.1 = (s32[2,128,128]{2,1,0:T(8,128)S(1)}, s32[2,128,128]{2,1,0:T(8,128)}, u32[]{:S(2)}) copy-start(s32[2,128,128]{2,1,0:T(8,128)} %frag.5) | copy-start | bytes 393220
  3.2 15.5 %copy-start.5 = (bf16[27,32,32]{2,1,0:T(8,128)(2,1)S(1)}, bf16[27,32,32]{2,1,0:T(8,128)(2,1)}, u32[]{:S(2)}) copy-start(bf16[27,32,32]{2,1,0:T(8,128)(2,1)} %conv_weight.1) | copy-start | bytes 165892
  3.2 15.5 %copy-start.8 = (f32[32]{0:T(128)S(1)}, f32[32]{0:T(128)}, u32[]{:S(2)}) copy-start(f32[32]{0:T(128)} %param.12) | copy-start | bytes 388
  4.9 33.7 %collective-permute-start = (bf16[128,4352]{1,0:T(8,128)(2,1)S(1)}, bf16[128,4352]{1,0:T(8,128)(2,1)S(1)}, u32[]{:S(2)}, u32[]{:S(2)}) collective-permute-start(bf16[128,4352]{1,0:T(8,128)(2,1)S(1)} %get-tuple-element.23.high), channel_id=1, source_target_pairs={{0,1},{1,2},{2,3},{4,5},{5,6},{6,7},{8,9},{9,10},{10,11},{12,13},{... | collective-permute-start | bytes 3342344 | tf_op jit(solution)/shard_map/ppermute | solution.py:484
  9.9 28.7 %collective-permute-start.1 = (bf16[128,4224]{1,0:T(8,128)(2,1)S(1)}, bf16[128,4224]{1,0:T(8,128)(2,1)S(1)}, u32[]{:S(2)}, u32[]{:S(2)}) collective-permute-start(bf16[128,4224]{1,0:T(8,128)(2,1)S(1)} %get-tuple-element.22.low), channel_id=1, source_target_pairs={{1,0},{2,1},{3,2},{5,4},{6,5},{7,6},{9,8},{10,9},{11,10},{13,12},{... | collective-permute-start | bytes 3244040 | tf_op jit(solution)/shard_map/ppermute | solution.py:484
  11.2 4.4 %collective-permute-start.2 = (bf16[272,128]{1,0:T(8,128)(2,1)S(1)}, bf16[272,128]{1,0:T(8,128)(2,1)S(1)}, u32[]{:S(2)}, u32[]{:S(2)}) collective-permute-start(bf16[272,128]{1,0:T(8,128)(2,1)S(1)} %get-tuple-element.25), channel_id=1, source_target_pairs={{0,16},{16,0},{1,17},{17,1},{2,18},{18,2},{3,19},{19,3},{4,20},{20... | collective-permute-start | bytes 208904 | tf_op jit(solution)/shard_map/ppermute | solution.py:527
  16.1 10.3 %collective-permute-start.3 = (bf16[2,48,128]{2,1,0:T(8,128)(2,1)S(1)}, bf16[2,48,128]{2,1,0:T(8,128)(2,1)S(1)}, u32[]{:S(2)}, u32[]{:S(2)}) collective-permute-start(bf16[2,48,128]{2,1,0:T(8,128)(2,1)S(1)} %get-tuple-element.28), channel_id=1, source_target_pairs={{0,4},{4,8},{8,12},{1,5},{5,9},{9,13},{2,6},{6,10},{10,14},{3,7},{... | collective-permute-start | bytes 73736 | tf_op jit(solution)/shard_map/ppermute | solution.py:484
  17.4 9.0 %collective-permute-start.4 = (bf16[2,48,128]{2,1,0:T(8,128)(2,1)S(1)}, bf16[2,48,128]{2,1,0:T(8,128)(2,1)S(1)}, u32[]{:S(2)}, u32[]{:S(2)}) collective-permute-start(bf16[2,48,128]{2,1,0:T(8,128)(2,1)S(1)} %get-tuple-element.29), channel_id=1, source_target_pairs={{4,0},{8,4},{12,8},{5,1},{9,5},{13,9},{6,2},{10,6},{14,10},{7,3},{... | collective-permute-start | bytes 73736 | tf_op jit(solution)/shard_map/ppermute | solution.py:484
  18.8 7.2 %copy-start.3 = (s32[1,1536]{1,0:T(1,128)S(1)}, s32[1,1536]{1,0:T(1,128)}, u32[]{:S(2)}) copy-start(s32[1,1536]{1,0:T(1,128)} %recv.1) | copy-start | bytes 18436
  18.8 7.2 %copy-start.4 = (s32[1024,1]{0,1:T(1,128)S(1)}, s32[1024,1]{0,1:T(1,128)}, u32[]{:S(2)}) copy-start(s32[1024,1]{0,1:T(1,128)} %param.17) | copy-start | bytes 12292
  18.8 13.5 %copy-start.2 = (s32[2,128,128]{2,1,0:T(8,128)S(1)}, s32[2,128,128]{2,1,0:T(8,128)}, u32[]{:S(2)}) copy-start(s32[2,128,128]{2,1,0:T(8,128)} %frag.5) | copy-start | bytes 393220
  26.4 12.2 %collective-permute-start.5 = (bf16[224,128]{1,0:T(8,128)(2,1)S(1)}, bf16[224,128]{1,0:T(8,128)(2,1)S(1)}, u32[]{:S(2)}, u32[]{:S(2)}) collective-permute-start(bf16[224,128]{1,0:T(8,128)(2,1)S(1)} %get-tuple-element.30), channel_id=1, source_target_pairs={{0,1},{1,2},{2,3},{4,5},{5,6},{6,7},{8,9},{9,10},{10,11},{12,13},{... | collective-permute-start | bytes 172040 | tf_op jit(solution)/shard_map/ppermute | solution.py:484
  31.0 7.6 %collective-permute-start.6 = (bf16[224,128]{1,0:T(8,128)(2,1)S(1)}, bf16[224,128]{1,0:T(8,128)(2,1)S(1)}, u32[]{:S(2)}, u32[]{:S(2)}) collective-permute-start(bf16[224,128]{1,0:T(8,128)(2,1)S(1)} %get-tuple-element.31), channel_id=1, source_target_pairs={{1,0},{2,1},{3,2},{5,4},{6,5},{7,6},{9,8},{10,9},{11,10},{13,12},{... | collective-permute-start | bytes 172040 | tf_op jit(solution)/shard_map/ppermute | solution.py:484
  38.2 0.7 copy-start.6
  38.2 0.7 copy-start.7
  38.2 0.7 copy-start.9

commit v3 on v2

--- a/solution.py
+++ b/solution.py
@@ -15,6 +15,7 @@
 EDGE = 48
 BF = jnp.bfloat16
 F32 = jnp.float32
+F8 = jnp.float8_e4m3fn
 VMEM = pl.BlockSpec(memory_space=pltpu.VMEM)
 SMEM = pl.BlockSpec(memory_space=pltpu.SMEM)
 
@@ -26,7 +27,7 @@
         in_specs=[VMEM] * (len(args) - smem) + [SMEM] * smem,
         out_specs=jax.tree.map(lambda _: VMEM, out_shape),
         scratch_shapes=list(scratch),
-        compiler_params=pltpu.CompilerParams(vmem_limit_bytes=48 << 20),
+        compiler_params=pltpu.CompilerParams(vmem_limit_bytes=28 << 20),
         cost_estimate=pl.CostEstimate(flops=flops, bytes_accessed=1 << 20, transcendentals=0),
         name=name,
     )(*args)
@@ -40,6 +41,9 @@
     return lax.broadcasted_iota(jnp.int32, dims, axis)
 
 
+X_LOW, X_HIGH, X_ODD, Y_LOW, Y_HIGH, Y_ODD, Z_LOW, Z_HIGH, Z_ODD, LIVE = range(10)
+
+
 def outer_product(left, right):
     return lax.dot_general(left, right, (((1,), (1,)), ((), ())), preferred_element_type=F32)
 
@@ -49,64 +53,95 @@
     return high, (value - high.astype(F32)).astype(BF)
 
 
-def layout_kernel(feat, frag, flags, low, high, x_up, x_down, edge, first_col, rows):
-    first = flags[0] == 0
+def layout_kernel(flags, feat_hbm, frag, low, high, z_one, z_two, x_one, x_two, edge, first_col, rows, feat, sems):
+    copies = []
+    for t in range(8):
+        lines = slice(16 * t, 16 * t + 16)
+        copies.append(pltpu.make_async_copy(feat_hbm.at[:, :, lines, :], feat.at[:, :, lines, :], sems.at[t]))
+        copies[-1].start()
+    x_odd, z_odd = flags[X_ODD] > 0, flags[Z_ODD] > 0
     zero = jnp.zeros((32, LANES), BF)
-    for z, plane in ((1, high), (0, low)):
-        last = zero
-        for t in range(8):
-            block = jnp.swapaxes(feat[:, z, 16 * t : 16 * t + 16, :], 0, 1).reshape(512, LANES)
-            turned = jnp.concatenate([last, block[:480]], axis=0).T
-            last = block[480:]
-            plane[:, 512 * t : 512 * t + 512] = turned
+    last = [zero, zero]
+    tile_zero = [None, None]
+    for t in range(9):
+        if t < 8:
+            copies[t].wait()
+        both = []
+        for z, plane in ((0, low), (1, high)):
+            if t < 8:
+                block = jnp.swapaxes(feat[:, z, 16 * t : 16 * t + 16, :], 0, 1).reshape(512, LANES)
+                turned = jnp.concatenate([last[z], block[:480]], axis=0).T
+                last[z] = block[480:]
+            else:
+                turned = jnp.concatenate([last[z], zero, zero, zero], axis=0).T
+            wide = turned.shape[1]
+            plane[:, 512 * t : 512 * t + wide] = turned
+            both.append(turned)
             for side, line in ((0, turned[112:128].astype(F32)[15:16]), (1, turned[0:16].astype(F32)[0:1])):
-                for q in range(4):
+                for q in range(wide // LANES):
                     spot = 4 * t + q
                     rows[2 * side + z, spot : spot + 1, :] = line[:, LANES * q : LANES * (q + 1)]
             if t == 0:
-                tile_zero = turned[:, :LANES]
-        end = jnp.concatenate([last, zero, zero, zero], axis=0).T
-        plane[:, WIDE - LANES : WIDE] = end
-        rows[z, TILES - 1 : TILES, :] = end[112:128].astype(F32)[15:16]
-        rows[2 + z, TILES - 1 : TILES, :] = end[0:16].astype(F32)[0:1]
-        x_up[LANES * z : LANES * (z + 1), :] = jnp.where(first, end, tile_zero)
-        x_down[LANES * z : LANES * (z + 1), :] = tile_zero
+                tile_zero[z] = turned[:, :LANES]
+            if t == 8:
+                lines = slice(LANES * z, LANES * (z + 1))
+                x_one[lines, :] = jnp.where(x_odd, tile_zero[z], turned)
+                x_two[lines, :] = jnp.where(x_odd, turned, tile_zero[z])
+        z_one[:, 512 * t : 512 * t + wide] = jnp.where(z_odd, both[0], both[1])
+        z_two[:, 512 * t : 512 * t + wide] = jnp.where(z_odd, both[1], both[0])
+    for z in range(2):
         turned = frag[z].astype(F32).T
         first_col[z : z + 1, :] = turned[0:1]
         for side in range(2):
             rows[2 * side + z, TILES:EDGE, :] = jnp.broadcast_to(turned[127:128], (EDGE - TILES, LANES))
             edge[2 * side + z] = rows[2 * side + z].astype(BF)
-    high[:, WIDE:] = frag[1].astype(F32).astype(BF)
+    top = frag[1].astype(F32).astype(BF)
     lines = [jnp.broadcast_to(frag[z, 127:128, :], (8, LANES)).astype(F32) for z in range(2)]
-    x_up[2 * LANES :, :] = jnp.concatenate(lines, axis=0).astype(BF)
-    x_down[2 * LANES :, :] = jnp.zeros((16, LANES), BF)
-
-
-def x_face_kernel(low, high, edge, flags, face, x_code, y_up, y_down):
-    has_low, has_high = flags[0] > 0, flags[1] > 0
+    lines = jnp.concatenate(lines, axis=0).astype(BF)
+    for out in (z_one, z_two):
+        out[:, WIDE:] = top
+    for out in (x_one, x_two):
+        out[2 * LANES :, :] = lines
+
+
+def x_face_kernel(got_one, got_two, edge, flags, face, x_code, y_one, y_two):
+    has_low, has_high, odd = flags[X_LOW] > 0, flags[X_HIGH] > 0, flags[X_ODD] > 0
+    y_odd = flags[Y_ODD] > 0
     lane = iota((LANES, LANES), 1)
     is_low = (lane < 32) & has_low
     is_high = (lane >= 32) & (lane < 64) & has_high
     none = jnp.zeros((LANES, LANES), BF)
+    row, place = iota((EDGE, LANES), 0), iota((EDGE, LANES), 1)
+    ends = ((row == 0) & (place < 32)) | ((row == TILES - 1) & (place >= 32) & (place < 64))
+    other = jnp.where(odd, got_one[2 * LANES :, :], got_two[2 * LANES :, :]).astype(F32)
     for z in range(2):
         lines = slice(LANES * z, LANES * (z + 1))
-        tile = jnp.where(is_low, low[lines, :], jnp.where(is_high, high[lines, :], none))
+        low = jnp.where(odd, got_one[lines, :], got_two[lines, :])
+        high = jnp.where(odd, got_two[lines, :], got_one[lines, :])
+        tile = jnp.where(is_low, low, jnp.where(is_high, high, none))
         face[z] = tile
-        for side, out in ((0, y_up), (1, y_down)):
+        patched = []
+        for side in range(2):
             near = (tile[112:128].astype(F32)[15:16], tile[0:16].astype(F32)[0:1])[side]
             line = edge[2 * side + z].astype(F32)
-            row, place = iota((EDGE, LANES), 0), iota((EDGE, LANES), 1)
-            ends = ((row == 0) & (place < 32)) | ((row == TILES - 1) & (place >= 32) & (place < 64))
-            out[z] = jnp.where(ends, jnp.broadcast_to(near, (EDGE, LANES)), line).astype(BF)
-        other = low[2 * LANES :, :].astype(F32)[8 * z : 8 * z + 1]
-        x_code[z] = jnp.where(has_low, other, -1.0)
-
-
-def ring_kernel(face, y_low, y_high, up, down):
-    for z, out in ((1, up), (0, down)):
-        out[:LANES, :] = face[z]
-        out[LANES : LANES + EDGE, :] = y_low[z]
-        out[LANES + EDGE :, :] = y_high[z]
+            patched.append(jnp.where(ends, jnp.broadcast_to(near, (EDGE, LANES)), line).astype(BF))
+        y_one[z] = jnp.where(y_odd, patched[1], patched[0])
+        y_two[z] = jnp.where(y_odd, patched[0], patched[1])
+        x_code[z] = jnp.where(has_low, other[8 * z : 8 * z + 1], -1.0)
+
+
+def ring_kernel(face, got_one, got_two, flags, y_low, y_high, z_one, z_two):
+    odd, z_odd = flags[Y_ODD] > 0, flags[Z_ODD] > 0
+    none = jnp.zeros((EDGE, LANES), BF)
+    rings = []
+    for z in range(2):
+        low = jnp.where(flags[Y_LOW] > 0, jnp.where(odd, got_one[z], got_two[z]), none)
+        high = jnp.where(flags[Y_HIGH] > 0, jnp.where(odd, got_two[z], got_one[z]), none)
+        y_low[z] = low
+        y_high[z] = high
+        rings.append(jnp.concatenate([face[z], low, high], axis=0))
+    z_one[...] = jnp.where(z_odd, rings[0], rings[1])
+    z_two[...] = jnp.where(z_odd, rings[1], rings[0])
 
 
 def banded(weight, z_off, dy, slot, quarter):
@@ -203,25 +238,15 @@
     return iota((rows, LANES), 0).astype(F32).astype(BF)
 
 
-def table_rows(t, frag, y_code, weight_row, own_hot, pair_hot, outer_z):
-    one = jnp.ones((F, LANES), BF)
-    none = jnp.zeros((F, LANES), BF)
+def line_partners(frag, y_code, x, first, hot_before):
     names = numbers(F)
-    for j in range(16):
-        x = 16 * t + j
-        line = pl.ds(x, 1)
-        before = pl.ds(jnp.maximum(x - 1, 0), 1)
-        hot = [spread(frag[z, line, :], 4) == names for z in range(2)]
-        spot = slice(LANES * j, LANES * (j + 1))
-        for z in range(2):
-            own_hot[z, :, spot] = jnp.where(hot[z], one, none)
-            earlier = frag[z, before, :] + (jnp.where(x > 0, 0.0, -128.0) if j == 0 else 0.0)
-            pair_hot[z, 0:F, spot] = jnp.where(spread(earlier, 4) == names, weight_row(1, z, x), none)
-            pair_hot[z, F : 2 * F, spot] = jnp.where(
-                spread(y_code[z, line, :], 4) == names, weight_row(2, z, x), none
-            )
-        pair_hot[1, 2 * F : 3 * F, spot] = jnp.where(hot[0], weight_row(0, 1, x), none)
-        outer_z(line, x, spot, names, one, none)
+    line = pl.ds(x, 1)
+    hot = [spread(frag[z, line, :], 4) == names for z in range(2)]
+    if hot_before is None:
+        before = [frag[z, pl.ds(jnp.maximum(x - 1, 0), 1), :] + first for z in range(2)]
+        hot_before = [spread(row, 4) == names for row in before]
+    y_hot = [spread(y_code[z, line, :], 4) == names for z in range(2)]
+    return hot, hot_before, y_hot
 
 
 def faces_product(own, partner, weight):
@@ -246,21 +271,31 @@
 
 def count_kernel(frag, x_code, y_low, first_col, flags, out, own_hot, pair_hot, plain, y_code):
     load_numbers(frag, plain, y_code)
-    unit = jnp.ones((F, LANES), BF)
-
-    def body(t, carry):
-        low, high = carry
-        table_rows(t, plain, y_code, lambda *_: unit, own_hot, pair_hot, lambda *_: None)
-        low = low + outer_product(own_hot[0], pair_hot[0, : 2 * F])
-        high = high + outer_product(own_hot[1], pair_hot[1])
-        return low, high
-
-    low, high = lax.fori_loop(0, 8, body, (jnp.zeros((F, 2 * F), F32), jnp.zeros((F, 3 * F), F32)))
-    own = low[:, :F] + low[:, F:] + high[:, :F] + high[:, F : 2 * F] + high[:, 2 * F :]
+    one = jnp.ones((F, LANES), BF)
+    none = jnp.zeros((F, LANES), BF)
+
+    def body(t, total):
+        hot_before = None
+        first = jnp.where(t > 0, 0.0, -128.0)
+        for j in range(32):
+            spot = slice(LANES * j, LANES * (j + 1))
+            hot, x_hot, y_hot = line_partners(plain, y_code, 32 * t + j, first, hot_before)
+            hot_before = hot
+            for z in range(2):
+                own_hot[z, :, spot] = jnp.where(hot[z], one, none).astype(F8)
+                pairs = jnp.where(x_hot[z], one, none) + jnp.where(y_hot[z], one, none)
+                if z == 1:
+                    pairs = pairs + jnp.where(hot[0], one, none)
+                pair_hot[z, :, spot] = pairs.astype(F8)
+        for z in range(2):
+            total = total + outer_product(own_hot[z], pair_hot[z])
+        return total
+
+    own = lax.fori_loop(0, 4, body, jnp.zeros((F, F), F32))
     ones = [jnp.ones((1, LANES), F32)] * 2
     x_outer = faces_product([plain[z, 0:1, :] for z in range(2)], [x_code[z] for z in range(2)], ones)
     y_outer = faces_product(
-        [first_col[z : z + 1, :] for z in range(2)], [y_partner(y_low, z, flags[2] > 0) for z in range(2)], ones
+        [first_col[z : z + 1, :] for z in range(2)], [y_partner(y_low, z, flags[Y_LOW] > 0) for z in range(2)], ones
     )
     out[...] = jnp.concatenate([own, jnp.zeros((F, F), F32), x_outer, y_outer], axis=1)
 
@@ -284,10 +319,10 @@
 
 def finish_kernel(
     acc,
-    below,
-    above,
-    ring_low,
-    ring_high,
+    plane_one,
+    plane_two,
+    ring_one,
+    ring_two,
     inner_lines,
     inner_ends,
     outer,
@@ -302,7 +337,6 @@
     rank,
     head_bias,
     flags,
-    edge_count,
     affinity,
     outgoing,
     planes,
@@ -316,21 +350,27 @@
     z_code,
 ):
     load_numbers(frag, plain, y_code)
-    z_code[...] = jnp.where(flags[3] > 0, below[:, WIDE:].astype(F32), -1.0)
+    odd = flags[Z_ODD]
+    below = jnp.where(odd > 0, plane_one[:, WIDE:], plane_two[:, WIDE:])
+    z_code[...] = jnp.where(flags[Z_LOW] > 0, below.astype(F32), -1.0)
     lane = iota((LANES, LANES), 1)
-    for i, (plane, ring) in enumerate(((below, ring_low), (above, ring_high))):
+    for plane, ring, i in ((plane_one, ring_one, 1 - odd), (plane_two, ring_two, odd)):
+        live = jnp.where(i > 0, flags[Z_HIGH], flags[Z_LOW]) > 0
         planes[i, :, LANES : WIDE - LANES] = plane[:, LANES : WIDE - LANES]
-        face = ring[:LANES, :]
+        around = jnp.where(live, ring[...], jnp.zeros(ring.shape, BF))
+        face = around[:LANES, :]
         planes[i, :, :LANES] = jnp.where(lane < 32, face, plane[:, :LANES])
         planes[i, :, WIDE - LANES :] = jnp.where(
             (lane >= 32) & (lane < 64), face, plane[:, WIDE - LANES : WIDE]
         )
-        half = slice(LANES * i, LANES * (i + 1))
         for side, dy in ((0, 0), (1, 2)):
-            chunks = ring[LANES + EDGE * side : LANES + EDGE * (side + 1), :]
-            lines[side, :, half] = inner_lines[side, :, half] + jnp.dot(
+            chunks = around[LANES + EDGE * side : LANES + EDGE * (side + 1), :]
+            lines[side, i] = jnp.dot(
                 line_windows(chunks), outer[i, :, LANES * dy : LANES * (dy + 1)], preferred_element_type=F32
             )
+    for i in range(2):
+        for side in range(2):
+            lines[side, i] = lines[side, i] + inner_lines[side, :, LANES * i : LANES * (i + 1)]
     line, spot = iota((8, 256), 0), iota((8, 256), 1)
     head = []
     for d in range(3):
@@ -344,10 +384,23 @@
     def weight_row(d, z, x):
         return spread(kept[2 * d + z, pl.ds(x, 1), :], 4)
 
-    def outer_z(at, x, place, names, one, none):
-        hot = spread(z_code[at, :], 4) == names
-        pair_hot[0, 2 * F : 3 * F, place] = jnp.where(hot, weight_row(0, 0, x), none)
-        pair_hot[0, 3 * F :, place] = jnp.where(hot, one, none)
+    def table_lines(x0, first, own_hot, pair_hot):
+        names, one, none = numbers(F), jnp.ones((F, LANES), BF), jnp.zeros((F, LANES), BF)
+        hot_before = None
+        for j in range(16):
+            x = x0 + j
+            spot = slice(LANES * j, LANES * (j + 1))
+            hot, x_hot, y_hot = line_partners(plain, y_code, x, first, hot_before)
+            hot_before = hot
+            for z in range(2):
+                own_hot[z, :, spot] = jnp.where(hot[z], one, none)
+                pair_hot[z, 0:F, spot] = jnp.where(x_hot[z], weight_row(1, z, x), none) + jnp.where(
+                    y_hot[z], weight_row(2, z, x), none
+                )
+            pair_hot[1, F : 2 * F, spot] = jnp.where(hot[0], weight_row(0, 1, x), none)
+            z_hot = spread(z_code[pl.ds(x, 1), :], 4) == names
+            pair_hot[0, F : 2 * F, spot] = jnp.where(z_hot, weight_row(0, 0, x), none)
+            pair_hot[0, 2 * F :, spot] = jnp.where(z_hot, one, none)
 
     def body(s, carry):
         low, high = carry
@@ -361,8 +414,7 @@
                 axis=0,
             )
             part = jnp.dot(left, outer[i], preferred_element_type=F32)
-            half = slice(LANES * i, LANES * (i + 1))
-            ends = [lines[side, pl.ds(pl.multiple_of(base, 8), STACK), half] for side in range(2)]
+            ends = [lines[side, i, pl.ds(pl.multiple_of(base, 8), STACK), :] for side in range(2)]
             for g in range(STACK):
                 o = STEP * g
                 scr[i, o + 8 : o + STEP, :] = part[LANES * g : LANES * (g + 1)]
@@ -393,16 +445,17 @@
                 kept[i, pl.ds(pl.multiple_of(4 * STACK * s + 8 * pair, 8), 8), :] = value
             all_lines = pl.ds(pl.multiple_of(4 * STACK * s, 16), 4 * STACK)
             affinity[i // 2, i % 2, all_lines, :] = kept[i, all_lines, :].astype(BF)
-        for t in range(STACK // 4):
-            table_rows(STACK // 4 * s + t, plain, y_code, weight_row, own_hot, pair_hot, outer_z)
-            low = low + outer_product(own_hot[0], pair_hot[0])
-            high = high + outer_product(own_hot[1], pair_hot[1, : 3 * F])
+        for t in range(2):
+            first = jnp.where(s > 0, 0.0, -128.0) if t == 0 else 0.0
+            table_lines(4 * STACK * s + 16 * t, first, own_hot.at[t], pair_hot.at[t])
+            low = low + outer_product(own_hot[t, 0], pair_hot[t, 0])
+            high = high + outer_product(own_hot[t, 1], pair_hot[t, 1, : 2 * F])
         return low, high
 
     low, high = lax.fori_loop(
-        0, GROUPS // STACK, body, (jnp.zeros((F, 4 * F), F32), jnp.zeros((F, 3 * F), F32))
-    )
-    own = low[:, :F] + low[:, F : 2 * F] + high[:, :F] + high[:, F : 2 * F] + high[:, 2 * F :]
+        0, GROUPS // STACK, body, (jnp.zeros((F, 3 * F), F32), jnp.zeros((F, 2 * F), F32))
+    )
+    own = low[:, :F] + high[:, :F] + high[:, F:]
     x_outer = faces_product(
         [plain[z, 0:1, :] for z in range(2)],
         [x_code[z] for z in range(2)],
@@ -410,12 +463,12 @@
     )
     y_outer = faces_product(
         [first_col[z : z + 1, :] for z in range(2)],
-        [y_partner(y_low, z, flags[2] > 0) for z in range(2)],
+        [y_partner(y_low, z, flags[Y_LOW] > 0) for z in range(2)],
         [kept[4 + z].T[0:1, :] for z in range(2)],
     )
-    sums = jnp.concatenate([own, low[:, 2 * F : 3 * F], x_outer, y_outer], axis=1)
+    sums = jnp.concatenate([own, low[:, F : 2 * F], x_outer, y_outer], axis=1)
     tally = counts[...] + jnp.concatenate(
-        [jnp.zeros((F, F), F32), low[:, 3 * F :], jnp.zeros((F, 2 * F), F32)], axis=1
+        [jnp.zeros((F, F), F32), low[:, 2 * F :], jnp.zeros((F, 2 * F), F32)], axis=1
     )
     slots = cells.shape[1]
     code = jnp.concatenate([cells[0:1, :], cells[1:2, :]], axis=1)
@@ -424,7 +477,7 @@
         jnp.concatenate(halves(sums) + halves(tally), axis=0), column_hot, preferred_element_type=F32
     )
     line_hot = iota((F, 2 * slots), 0) == (code >> 8)
-    alive = iota((1, slots), 1) < edge_count[0]
+    alive = iota((1, slots), 1) < flags[LIVE]
 
     def part_of(value):
         total = jnp.sum(jnp.where(line_hot, value, 0.0), axis=0, keepdims=True)
@@ -475,13 +528,20 @@
         out[:, LANES * g : LANES * (g + 1)] = total_sum / jnp.maximum(total_count, 1.0)
 
 
-def exchange(up, down, axis):
+def swap(one, two, axis, closed):
     n = lax.axis_size(axis)
     if n == 1:
-        return jnp.zeros_like(up), jnp.zeros_like(down)
-    forward = [(i, i + 1) for i in range(n - 1)]
-    backward = [(i + 1, i) for i in range(n - 1)]
-    return lax.ppermute(up, axis, forward), lax.ppermute(down, axis, backward)
+        return jnp.zeros_like(one), jnp.zeros_like(two)
+    rounds = [[(i, i + 1) for i in range(start, n - 1, 2)] for start in range(2)]
+    if n == 2:
+        got = lax.ppermute(one, axis, [(0, 1), (1, 0)])
+        return got, got
+    if closed and n % 2 == 0:
+        rounds[1].append((0, n - 1))
+    return tuple(
+        lax.ppermute(value, axis, [pair for a, b in pairs for pair in ((a, b), (b, a))])
+        for value, pairs in zip((one, two), rounds)
+    )
 
 
 def shards(
@@ -503,30 +563,36 @@
     capacity = recv_slot.shape[1] // devices
     slots = edge_cells.shape[1]
     own_slots = devices * capacity // 4
-    flags = jnp.stack([at["gx"], size["gx"] - 1 - at["gx"], at["gy"], at["gz"]]).astype(jnp.int32)
-    pair = size["gx"] == 2
-    send_up = flags if pair else jnp.zeros_like(flags)
-
-    xt_low, xt_high, x_up, x_down, edge, first_col = call(
+    flags = []
+    for axis in axes:
+        flags += [at[axis], size[axis] - 1 - at[axis], at[axis] % 2]
+    flags = jnp.stack(flags + [edge_count[0]]).astype(jnp.int32)
+
+    xt_low, xt_high, z_one, z_two, x_one, x_two, edge, first_col = pl.pallas_call(
         layout_kernel,
-        "layout",
-        (
+        out_shape=(
             shape((LANES, WIDE), BF),
+            shape((LANES, WIDE), BF),
+            shape((LANES, WIDE + LANES), BF),
             shape((LANES, WIDE + LANES), BF),
             shape((2 * LANES + 16, LANES), BF),
             shape((2 * LANES + 16, LANES), BF),
             shape((4, EDGE, LANES), BF),
             shape((2, LANES), F32),
         ),
-        (features, fragments, send_up),
-        1,
-        [pltpu.VMEM((4, EDGE, LANES), F32)],
-    )
-    below, above = exchange(xt_high, xt_low, "gz")
-    if pair:
-        x_low = x_high = lax.ppermute(x_up, "gx", [(0, 1), (1, 0)])
-    else:
-        x_low, x_high = exchange(x_up, x_down, "gx")
+        in_specs=[SMEM, pl.BlockSpec(memory_space=pl.ANY), VMEM],
+        out_specs=(VMEM,) * 8,
+        scratch_shapes=[
+            pltpu.VMEM((4, EDGE, LANES), F32),
+            pltpu.VMEM(features.shape, BF),
+            pltpu.SemaphoreType.DMA((8,)),
+        ],
+        compiler_params=pltpu.CompilerParams(vmem_limit_bytes=28 << 20),
+        cost_estimate=pl.CostEstimate(flops=1_000_000, bytes_accessed=1 << 20, transcendentals=0),
+        name="layout",
+    )(flags, features, fragments)
+    plane_one, plane_two = swap(z_one, z_two, "gz", False)
+    x_got = swap(x_one, x_two, "gx", True)
 
     acc, inner, outer = call(
         own_kernel,
@@ -545,7 +611,7 @@
         (owner, recv_slot),
         0,
     )
-    face, x_code, y_up, y_down = call(
+    face, x_code, y_one, y_two = call(
         x_face_kernel,
         "x_face",
         (
@@ -554,14 +620,17 @@
             shape((2, EDGE, LANES), BF),
             shape((2, EDGE, LANES), BF),
         ),
-        (x_low, x_high, edge, flags),
+        (*x_got, edge, flags),
         1,
     )
-    y_low, y_high = exchange(y_up, y_down, "gy")
-    ring_up, ring_down = call(
-        ring_kernel, "ring", (shape((LANES + 2 * EDGE, LANES), BF),) * 2, (face, y_low, y_high), 0
-    )
-    ring_low, ring_high = exchange(ring_up, ring_down, "gz")
+    y_low, y_high, ring_one, ring_two = call(
+        ring_kernel,
+        "ring",
+        (shape((2, EDGE, LANES), BF),) * 2 + (shape((LANES + 2 * EDGE, LANES), BF),) * 2,
+        (face, *swap(y_one, y_two, "gy", True), flags),
+        1,
+    )
+    ring_one, ring_two = swap(ring_one, ring_two, "gz", True)
 
     lines, ends = call(
         edge_kernel,
@@ -578,8 +647,8 @@
         (fragments, x_code, y_low, first_col, flags),
         1,
         [
-            pltpu.VMEM((2, F, 2048), BF),
-            pltpu.VMEM((2, 3 * F, 2048), BF),
+            pltpu.VMEM((2, F, 4096), F8),
+            pltpu.VMEM((2, F, 4096), F8),
             pltpu.VMEM((2, LANES, LANES), F32),
             pltpu.VMEM((2, LANES, LANES), F32),
         ],
@@ -591,10 +660,10 @@
         (shape((3, 2, LANES, LANES), BF), shape((devices, 1, LANES), F32)),
         (
             acc,
-            below,
-            above,
-            ring_low,
-            ring_high,
+            plane_one,
+            plane_two,
+            ring_one,
+            ring_two,
             lines,
             ends,
             outer,
@@ -609,16 +678,15 @@
             rank,
             head_bias,
             flags,
-            edge_count,
         ),
-        3,
+        2,
         [
             pltpu.VMEM((2, LANES, WIDE), BF),
             pltpu.VMEM((2, STEP * STACK + 8, 3 * LANES), F32),
-            pltpu.VMEM((2, GROUPS, 256), F32),
+            pltpu.VMEM((2, 2, GROUPS, LANES), F32),
             pltpu.VMEM((6, LANES, LANES), F32),
-            pltpu.VMEM((2, F, 2048), BF),
-            pltpu.VMEM((2, 4 * F, 2048), BF),
+            pltpu.VMEM((2, 2, F, 2048), BF),
+            pltpu.VMEM((2, 2, 3 * F, 2048), BF),
             pltpu.VMEM((2, LANES, LANES), F32),
             pltpu.VMEM((2, LANES, LANES), F32),
             pltpu.VMEM((LANES, LANES), F32),

time: 72.1 us -> 65 us (0.902)
  waiting for transfers between devices: 2.83 us -> 11 us
  Pallas kernels: 31.3 us -> 24.4 us
  blocking collectives: 16.9 us -> 12.9 us
  starting transfers between devices: 16.3 us -> 12.4 us
    pallas_call x9 -> x8, Pallas kernels: 31.3 us -> 21.5 us  [call(): pl.pallas_call(kernel, out_shape=out_shape, in_specs=[VMEM] * (len(args)...]
    ppermute x7, waiting for transfers between devices: 2.83 us -> 11 us  [the longest x6 8.22 us: swap(): lax.ppermute(value, axis, [pair for a, b in pairs for pair in ((a, b), (b...]
    all_to_all x1, blocking collectives: 16.9 us -> 12.9 us  [shards(): lax.all_to_all(outgoing, axes, split_axis=0, concat_axis=0, tiled=True)]
    ppermute x7, starting transfers between devices: 16.3 us -> 12.4 us  [the longest x6 10.8 us: swap(): lax.ppermute(value, axis, [pair for a, b in pairs for pair in ((a, b), (b...]
    pallas_call x0 -> x1, Pallas kernels: none -> 2.88 us  [shards(): pl.pallas_call(layout_kernel, out_shape=(shape((LANES, WIDE), BF), shape(...]
  transfers between devices with their start and end apart: 7 -> 7, of which waited for: 1 -> 3; matrix products, arithmetic and copies ran while one was open for 0% -> 0% of each run, Pallas kernels for 19% -> 14%
where the time goes in v3:
time: 65 us; the launch traced here: 64.8 us
  Pallas kernels  24.4 us (38%)
  blocking collectives  12.9 us (20%)
  starting transfers between devices  12.4 us (19%)
  waiting for transfers between devices  11 us (17%)
  local copies, waits for them, and re-layouts  2.63 us (4%)
  between operations  1.47 us (2%)
    pallas_call x8, Pallas kernels, call(): pl.pallas_call(kernel, out_shape=out_shape, in_specs=[VMEM] * (len(args)...  21.5 us
    all_to_all x1, blocking collectives, shards(): lax.all_to_all(outgoing, axes, split_axis=0, concat_axis=0, tiled=True)  12.9 us
    ppermute x6, starting transfers between devices, swap(): lax.ppermute(value, axis, [pair for a, b in pairs for pair in ((a, b), (b...  10.8 us
    ppermute x6, waiting for transfers between devices, swap(): lax.ppermute(value, axis, [pair for a, b in pairs for pair in ((a, b), (b...  8.22 us
    pallas_call x1, Pallas kernels, shards(): pl.pallas_call(layout_kernel, out_shape=(shape((LANES, WIDE), BF), shape(...  2.88 us
    ppermute x1, waiting for transfers between devices, swap(): got = lax.ppermute(one, axis, [(0, 1), (1, 0)])  2.82 us
    unnamed x20, local copies, waits for them, and re-layouts  2.54 us
    ppermute x1, starting transfers between devices, swap(): got = lax.ppermute(one, axis, [(0, 1), (1, 0)])  1.56 us
  transfers between devices with their start and end apart: 7, of which 3 were waited for; matrix products, arithmetic and copies ran while one was open for 0% of the time, Pallas kernels for 14%

profile of v3, /device:TPU:0, one launch (start us, length us, event | category | flops | bytes accessed | tf_op | source)
XLA Modules:
  0.0 64.8 jit_solution(13060399253708144955)
XLA Ops:
  1.3 0.1 stack.39.flags
  1.4 1.6 %copy-done = bf16[32,2,128,128]{3,2,1,0:T(8,128)(2,1)S(1)} copy-done((bf16[32,2,128,128]{3,2,1,0:T(8,128)(2,1)S(1)}, bf16[32,2,128,128]{3,2,1,0:T(8,128)(2,1)}, u32[]{:S(2)}) %copy-start) | copy-done | bytes 2097176
  3.0 0.9 %copy-done.1 = s32[2,128,128]{2,1,0:T(8,128)S(1)} copy-done((s32[2,128,128]{2,1,0:T(8,128)S(1)}, s32[2,128,128]{2,1,0:T(8,128)}, u32[]{:S(2)}) %copy-start.1) | copy-done | bytes 131096
  3.9 2.9 %layout.1 = (bf16[128,4224]{1,0:T(8,128)(2,1)S(1)}, bf16[128,4224]{1,0:T(8,128)(2,1)S(1)}, bf16[128,4352]{1,0:T(8,128)(2,1)S(1)}, bf16[128,4352]{1,0:T(8,128)(2,...) custom-call(s32[10]{0:T(128)S(1)} %stack.39.flags, ...), custom_call_target="tpu_custom_call" | custom-call | flops 1000000 | bytes 1048576 | tf_op jit(solution)/shard_map/layout/pallas_call | solution.py:571
  6.8 3.1 %collective-permute-start = (bf16[128,4352]{1,0:T(8,128)(2,1)S(1)}, bf16[128,4352]{1,0:T(8,128)(2,1)S(1)}, u32[]{:S(2)}, u32[]{:S(2)}) collective-permute-start(bf16[128,4352]{1,0:T(8,128)(2,1)S(1)} %get-tuple-element.29), channel_id=1, source_target_pairs={{0,1},{1,0},{2,3},{3,2},{4,5},{5,4},{6,7},{7,6},{8,9},{9,8},{10,11... | collective-permute-start | bytes 3342344 | tf_op jit(solution)/shard_map/ppermute | solution.py:542
  9.9 0.7 %collective-permute-start.1 = (bf16[128,4352]{1,0:T(8,128)(2,1)S(1)}, bf16[128,4352]{1,0:T(8,128)(2,1)S(1)}, u32[]{:S(2)}, u32[]{:S(2)}) collective-permute-start(bf16[128,4352]{1,0:T(8,128)(2,1)S(1)} %get-tuple-element.30), channel_id=1, source_target_pairs={{1,2},{2,1},{5,6},{6,5},{9,10},{10,9},{13,14},{14,13},{17,18},{18,... | collective-permute-start | bytes 3342344 | tf_op jit(solution)/shard_map/ppermute | solution.py:542
  10.6 1.6 %collective-permute-start.2 = (bf16[272,128]{1,0:T(8,128)(2,1)S(1)}, bf16[272,128]{1,0:T(8,128)(2,1)S(1)}, u32[]{:S(2)}, u32[]{:S(2)}) collective-permute-start(bf16[272,128]{1,0:T(8,128)(2,1)S(1)} %get-tuple-element.31), channel_id=1, source_target_pairs={{0,16},{16,0},{1,17},{17,1},{2,18},{18,2},{3,19},{19,3},{4,20},{20... | collective-permute-start | bytes 208904 | tf_op jit(solution)/shard_map/ppermute | solution.py:537
  12.2 2.8 %collective-permute-done.2.got_one.got_two = bf16[272,128]{1,0:T(8,128)(2,1)S(1)} collective-permute-done((bf16[272,128]{1,0:T(8,128)(2,1)S(1)}, bf16[272,128]{1,0:T(8,128)(2,1)S(1)}, u32[]{:S(2)}, u32[]{:S(2)}) %collective-permute-start.2) | collective-permute-done | bytes 69664 | tf_op jit(solution)/shard_map/ppermute | solution.py:537
  15.0 0.6 x_face.1
  15.6 0.1 collective-permute-start.3
  15.6 1.6 %collective-permute-start.4 = (bf16[2,48,128]{2,1,0:T(8,128)(2,1)S(1)}, bf16[2,48,128]{2,1,0:T(8,128)(2,1)S(1)}, u32[]{:S(2)}, u32[]{:S(2)}) collective-permute-start(bf16[2,48,128]{2,1,0:T(8,128)(2,1)S(1)} %get-tuple-element.35), channel_id=1, source_target_pairs={{4,8},{8,4},{0,12},{12,0},{5,9},{9,5},{1,13},{13,1},{6,10},{10,6},... | collective-permute-start | bytes 73736 | tf_op jit(solution)/shard_map/ppermute | solution.py:542
  17.3 0.0 copy-done.5
  17.3 0.0 copy-start.2
  17.3 4.6 %own_planes.1 = (f32[32,128,256]{2,1,0:T(8,128)S(1)}, bf16[3,512,256]{2,1,0:T(8,128)(2,1)S(1)}, bf16[2,256,384]{2,1,0:T(8,128)(2,1)S(1)}) custom-call(bf16[128,4224]{1,0:T(8,128)(2,1)S(1)} %get-tuple-element.26.low, bf16[128,4224]{1,0:T(8,128)(2,1)S(1)} %get-tuple-element.27.high, bf16[27,32,32]{2,1,0:T(8,128)(2,1)S(1)} %copy-done.5, f32[1,32]{1,0:T(1,128)S(1)} %bitcast.13), custom_call_target="tpu_custom_call" | custom-call | flops 5000000000 | bytes 1048576 | tf_op jit(solution)/shard_map/own_planes/pallas_call | solution.py:24
  21.9 0.4 slots.1
  22.3 0.0 collective-permute-done.3.got_one
  22.3 0.0 collective-permute-done.4.got_two
  22.4 0.6 ring.1
  22.9 4.4 %collective-permute-start.5 = (bf16[224,128]{1,0:T(8,128)(2,1)S(1)}, bf16[224,128]{1,0:T(8,128)(2,1)S(1)}, u32[]{:S(2)}, u32[]{:S(2)}) collective-permute-start(bf16[224,128]{1,0:T(8,128)(2,1)S(1)} %get-tuple-element.36), channel_id=1, source_target_pairs={{0,1},{1,0},{2,3},{3,2},{4,5},{5,4},{6,7},{7,6},{8,9},{9,8},{10,11... | collective-permute-start | bytes 172040 | tf_op jit(solution)/shard_map/ppermute | solution.py:542
  27.3 0.9 %collective-permute-start.6 = (bf16[224,128]{1,0:T(8,128)(2,1)S(1)}, bf16[224,128]{1,0:T(8,128)(2,1)S(1)}, u32[]{:S(2)}, u32[]{:S(2)}) collective-permute-start(bf16[224,128]{1,0:T(8,128)(2,1)S(1)} %get-tuple-element.37), channel_id=1, source_target_pairs={{1,2},{2,1},{0,3},{3,0},{5,6},{6,5},{4,7},{7,4},{9,10},{10,9},{8,1... | collective-permute-start | bytes 172040 | tf_op jit(solution)/shard_map/ppermute | solution.py:542
  28.2 2.3 %pair_counts.1.counts = f32[64,256]{1,0:T(8,128)S(1)} custom-call(s32[2,128,128]{2,1,0:T(8,128)S(1)} %copy-done.2, f32[2,1,128]{2,1,0:T(1,128)S(1)} %get-tuple-element.44.x_code, bf16[2,48,128]{2,1,0:T(8,128)(2,1)S(1)} %get-tuple-element.38.y_low, f32[2,128]{1,0:T(2,128)S(1)} %get-tuple-element.45.first_col, s32[10]{0:T(128)S(1)} %stack.39.flags), custom_call_target="tpu_custom_call" | custom-call | flops 4000000000 | bytes 1048576 | tf_op jit(solution)/shard_map/pair_counts/pallas_call | solution.py:24
  30.6 0.0 copy-start.6
  30.6 0.0 copy-start.7
  30.6 0.0 copy-start.9
  30.6 0.4 edges.1
  31.0 4.7 %collective-permute-done.5.ring_one = bf16[224,128]{1,0:T(8,128)(2,1)S(1)} collective-permute-done((bf16[224,128]{1,0:T(8,128)(2,1)S(1)}, bf16[224,128]{1,0:T(8,128)(2,1)S(1)}, u32[]{:S(2)}, u32[]{:S(2)}) %collective-permute-start.5) | collective-permute-done | bytes 57376 | tf_op jit(solution)/shard_map/ppermute | solution.py:542
  35.7 3.5 %collective-permute-done.6.ring_two = bf16[224,128]{1,0:T(8,128)(2,1)S(1)} collective-permute-done((bf16[224,128]{1,0:T(8,128)(2,1)S(1)}, bf16[224,128]{1,0:T(8,128)(2,1)S(1)}, u32[]{:S(2)}, u32[]{:S(2)}) %collective-permute-start.6) | collective-permute-done | bytes 57376 | tf_op jit(solution)/shard_map/ppermute | solution.py:542
  39.2 0.0 collective-permute-done.plane_one
  39.2 0.0 collective-permute-done.1.plane_two
  39.2 11.2 %finish.1 = (bf16[3,2,128,128]{3,2,1,0:T(8,128)(2,1)}, f32[32,1,128]{2,1,0:T(1,128)S(1)}) custom-call(f32[32,128,256]{2,1,0:T(8,128)S(1)} %get-tuple-element.28.acc, bf16[128,4352]{1,0:T(8,128)(2,1)S(1)} %collective-permute-done.plane_one, bf16[128,4352]{1,0:T(8,128)(2,1)S(1)} %collective-permute-done.1.plane_two, ...), custom_call_target="tpu_custom_call" | custom-call | flops 8000000000 | bytes 1048576 | tf_op jit(solution)/shard_map/finish/pallas_call | solution.py:24
  50.4 12.9 %all_to_all.5.received = f32[32,1,128]{2,1,0:T(1,128)S(1)} all-to-all(f32[32,1,128]{2,1,0:T(1,128)S(1)} %get-tuple-element.48), channel_id=1, replica_groups=mesh['gx'=2,'gy'=4,'gz'=4] {'gx','gy','gz'}, dimensions={0} | all-to-all | bytes 32768 | tf_op jit(solution)/shard_map/all_to_all | solution.py:696
  63.3 1.5 %settle.1 = f32[1,384]{1,0:T(1,128)} custom-call(f32[32,1,128]{2,1,0:T(1,128)S(1)} %all_to_all.5.received, s32[32,128]{1,0:T(8,128)S(1)} %get-tuple-element.49.slot), custom_call_target="tpu_custom_call" | custom-call | flops 1000000 | bytes 1048576 | tf_op jit(solution)/shard_map/settle/pallas_call | solution.py:24
  (13 shorter events, 0.0 us)
Async XLA Ops:
  1.4 1.6 %copy-start = (bf16[32,2,128,128]{3,2,1,0:T(8,128)(2,1)S(1)}, bf16[32,2,128,128]{3,2,1,0:T(8,128)(2,1)}, u32[]{:S(2)}) copy-start(bf16[32,2,128,128]{3,2,1,0:T(8,128)(2,1)} %feat_hbm.1) | copy-start | bytes 6291460
  3.0 0.9 %copy-start.1 = (s32[2,128,128]{2,1,0:T(8,128)S(1)}, s32[2,128,128]{2,1,0:T(8,128)}, u32[]{:S(2)}) copy-start(s32[2,128,128]{2,1,0:T(8,128)} %frag.5) | copy-start | bytes 393220
  3.9 13.4 %copy-start.5 = (bf16[27,32,32]{2,1,0:T(8,128)(2,1)S(1)}, bf16[27,32,32]{2,1,0:T(8,128)(2,1)}, u32[]{:S(2)}) copy-start(bf16[27,32,32]{2,1,0:T(8,128)(2,1)} %conv_weight.1) | copy-start | bytes 165892
  3.9 13.4 %copy-start.8 = (f32[32]{0:T(128)S(1)}, f32[32]{0:T(128)}, u32[]{:S(2)}) copy-start(f32[32]{0:T(128)} %param.12) | copy-start | bytes 388
  6.8 32.4 %collective-permute-start = (bf16[128,4352]{1,0:T(8,128)(2,1)S(1)}, bf16[128,4352]{1,0:T(8,128)(2,1)S(1)}, u32[]{:S(2)}, u32[]{:S(2)}) collective-permute-start(bf16[128,4352]{1,0:T(8,128)(2,1)S(1)} %get-tuple-element.29), channel_id=1, source_target_pairs={{0,1},{1,0},{2,3},{3,2},{4,5},{5,4},{6,7},{7,6},{8,9},{9,8},{10,11... | collective-permute-start | bytes 3342344 | tf_op jit(solution)/shard_map/ppermute | solution.py:542
  9.9 29.3 %collective-permute-start.1 = (bf16[128,4352]{1,0:T(8,128)(2,1)S(1)}, bf16[128,4352]{1,0:T(8,128)(2,1)S(1)}, u32[]{:S(2)}, u32[]{:S(2)}) collective-permute-start(bf16[128,4352]{1,0:T(8,128)(2,1)S(1)} %get-tuple-element.30), channel_id=1, source_target_pairs={{1,2},{2,1},{5,6},{6,5},{9,10},{10,9},{13,14},{14,13},{17,18},{18,... | collective-permute-start | bytes 3342344 | tf_op jit(solution)/shard_map/ppermute | solution.py:542
  10.6 4.4 %collective-permute-start.2 = (bf16[272,128]{1,0:T(8,128)(2,1)S(1)}, bf16[272,128]{1,0:T(8,128)(2,1)S(1)}, u32[]{:S(2)}, u32[]{:S(2)}) collective-permute-start(bf16[272,128]{1,0:T(8,128)(2,1)S(1)} %get-tuple-element.31), channel_id=1, source_target_pairs={{0,16},{16,0},{1,17},{17,1},{2,18},{18,2},{3,19},{19,3},{4,20},{20... | collective-permute-start | bytes 208904 | tf_op jit(solution)/shard_map/ppermute | solution.py:537
  15.6 6.8 %collective-permute-start.3 = (bf16[2,48,128]{2,1,0:T(8,128)(2,1)S(1)}, bf16[2,48,128]{2,1,0:T(8,128)(2,1)S(1)}, u32[]{:S(2)}, u32[]{:S(2)}) collective-permute-start(bf16[2,48,128]{2,1,0:T(8,128)(2,1)S(1)} %get-tuple-element.34), channel_id=1, source_target_pairs={{0,4},{4,0},{8,12},{12,8},{1,5},{5,1},{9,13},{13,9},{2,6},{6,2},{1... | collective-permute-start | bytes 73736 | tf_op jit(solution)/shard_map/ppermute | solution.py:542
  15.6 6.7 %collective-permute-start.4 = (bf16[2,48,128]{2,1,0:T(8,128)(2,1)S(1)}, bf16[2,48,128]{2,1,0:T(8,128)(2,1)S(1)}, u32[]{:S(2)}, u32[]{:S(2)}) collective-permute-start(bf16[2,48,128]{2,1,0:T(8,128)(2,1)S(1)} %get-tuple-element.35), channel_id=1, source_target_pairs={{4,8},{8,4},{0,12},{12,0},{5,9},{9,5},{1,13},{13,1},{6,10},{10,6},... | collective-permute-start | bytes 73736 | tf_op jit(solution)/shard_map/ppermute | solution.py:542
  17.3 4.6 %copy-start.3 = (s32[1,1536]{1,0:T(1,128)S(1)}, s32[1,1536]{1,0:T(1,128)}, u32[]{:S(2)}) copy-start(s32[1,1536]{1,0:T(1,128)} %recv.1) | copy-start | bytes 18436
  17.3 4.7 %copy-start.4 = (s32[1024,1]{0,1:T(1,128)S(1)}, s32[1024,1]{0,1:T(1,128)}, u32[]{:S(2)}) copy-start(s32[1024,1]{0,1:T(1,128)} %param.17) | copy-start | bytes 12292
  17.3 11.0 %copy-start.2 = (s32[2,128,128]{2,1,0:T(8,128)S(1)}, s32[2,128,128]{2,1,0:T(8,128)}, u32[]{:S(2)}) copy-start(s32[2,128,128]{2,1,0:T(8,128)} %frag.5) | copy-start | bytes 393220
  22.9 12.7 %collective-permute-start.5 = (bf16[224,128]{1,0:T(8,128)(2,1)S(1)}, bf16[224,128]{1,0:T(8,128)(2,1)S(1)}, u32[]{:S(2)}, u32[]{:S(2)}) collective-permute-start(bf16[224,128]{1,0:T(8,128)(2,1)S(1)} %get-tuple-element.36), channel_id=1, source_target_pairs={{0,1},{1,0},{2,3},{3,2},{4,5},{5,4},{6,7},{7,6},{8,9},{9,8},{10,11... | collective-permute-start | bytes 172040 | tf_op jit(solution)/shard_map/ppermute | solution.py:542
  27.3 11.9 %collective-permute-start.6 = (bf16[224,128]{1,0:T(8,128)(2,1)S(1)}, bf16[224,128]{1,0:T(8,128)(2,1)S(1)}, u32[]{:S(2)}, u32[]{:S(2)}) collective-permute-start(bf16[224,128]{1,0:T(8,128)(2,1)S(1)} %get-tuple-element.37), channel_id=1, source_target_pairs={{1,2},{2,1},{0,3},{3,0},{5,6},{6,5},{4,7},{7,4},{9,10},{10,9},{8,1... | collective-permute-start | bytes 172040 | tf_op jit(solution)/shard_map/ppermute | solution.py:542
  30.6 8.6 %copy-start.6 = (s32[2,1024]{1,0:T(2,128)S(1)}, s32[2,1024]{1,0:T(2,128)}, u32[]{:S(2)}) copy-start(s32[2,1024]{1,0:T(2,128)} %cells.1) | copy-start | bytes 24580
  30.6 8.6 %copy-start.7 = (bf16[3,32]{1,0:T(4,128)(2,1)S(1)}, bf16[3,32]{1,0:T(4,128)(2,1)}, u32[]{:S(2)}) copy-start(bf16[3,32]{1,0:T(4,128)(2,1)} %head_weight.1) | copy-start | bytes 580
  30.6 8.6 %copy-start.9 = (f32[3]{0:T(128)S(1)}, f32[3]{0:T(128)}, u32[]{:S(2)}) copy-start(f32[3]{0:T(128)} %head_bias.1) | copy-start | bytes 40

commit v4 on v3

--- a/solution.py
+++ b/solution.py
@@ -13,6 +13,10 @@
 STACK = 8
 STEP = LANES + 8
 EDGE = 48
+HEAD_STACKS = 3
+HEAD_GROUPS = HEAD_STACKS * STACK
+HEAD = (HEAD_GROUPS + 1) * LANES
+HEAD_LINES = 4 * HEAD_GROUPS
 BF = jnp.bfloat16
 F32 = jnp.float32
 F8 = jnp.float8_e4m3fn
@@ -53,19 +57,12 @@
     return high, (value - high.astype(F32)).astype(BF)
 
 
-def layout_kernel(flags, feat_hbm, frag, low, high, z_one, z_two, x_one, x_two, edge, first_col, rows, feat, sems):
-    copies = []
-    for t in range(8):
-        lines = slice(16 * t, 16 * t + 16)
-        copies.append(pltpu.make_async_copy(feat_hbm.at[:, :, lines, :], feat.at[:, :, lines, :], sems.at[t]))
-        copies[-1].start()
+def layout_kernel(flags, feat, frag, low, high, z_one, z_two, end_one, end_two, x_one, x_two, edge, first_col, rows):
     x_odd, z_odd = flags[X_ODD] > 0, flags[Z_ODD] > 0
     zero = jnp.zeros((32, LANES), BF)
     last = [zero, zero]
     tile_zero = [None, None]
     for t in range(9):
-        if t < 8:
-            copies[t].wait()
         both = []
         for z, plane in ((0, low), (1, high)):
             if t < 8:
@@ -87,8 +84,15 @@
                 lines = slice(LANES * z, LANES * (z + 1))
                 x_one[lines, :] = jnp.where(x_odd, tile_zero[z], turned)
                 x_two[lines, :] = jnp.where(x_odd, turned, tile_zero[z])
-        z_one[:, 512 * t : 512 * t + wide] = jnp.where(z_odd, both[0], both[1])
-        z_two[:, 512 * t : 512 * t + wide] = jnp.where(z_odd, both[1], both[0])
+        for head, end, value in (
+            (z_one, end_one, jnp.where(z_odd, both[0], both[1])),
+            (z_two, end_two, jnp.where(z_odd, both[1], both[0])),
+        ):
+            cut = min(max(HEAD - 512 * t, 0), wide)
+            if cut > 0:
+                head[:, 512 * t : 512 * t + cut] = value[:, :cut]
+            if cut < wide:
+                end[:, 512 * t + cut - HEAD : 512 * t + wide - HEAD] = value[:, cut:]
     for z in range(2):
         turned = frag[z].astype(F32).T
         first_col[z : z + 1, :] = turned[0:1]
@@ -99,7 +103,7 @@
     lines = [jnp.broadcast_to(frag[z, 127:128, :], (8, LANES)).astype(F32) for z in range(2)]
     lines = jnp.concatenate(lines, axis=0).astype(BF)
     for out in (z_one, z_two):
-        out[:, WIDE:] = top
+        out[:, HEAD:] = top
     for out in (x_one, x_two):
         out[2 * LANES :, :] = lines
 
@@ -269,7 +273,7 @@
     return jnp.where(has_low, y_low[z, TILES - 1 :, :].astype(F32)[8:9], -1.0)
 
 
-def count_kernel(frag, x_code, y_low, first_col, flags, out, own_hot, pair_hot, plain, y_code):
+def count_kernel(frag, x_code, y_low, first_col, flags, out, plain, y_code, own_hot, pair_hot):
     load_numbers(frag, plain, y_code)
     one = jnp.ones((F, LANES), BF)
     none = jnp.zeros((F, LANES), BF)
@@ -300,24 +304,112 @@
     out[...] = jnp.concatenate([own, jnp.zeros((F, F), F32), x_outer, y_outer], axis=1)
 
 
-def slots_kernel(owner, recv, rank, place):
+def slots_kernel(cells, owner, recv, rank_hot, column_hot, group, name_hot, place):
     slots = owner.shape[1]
-    devices = place.shape[0]
+    devices = group.shape[0]
     capacity = recv.shape[1] // devices
     hot = iota((devices, slots), 0) == owner[...]
     before = iota((slots, slots), 0) < iota((slots, slots), 1)
     earlier = jnp.dot(
         jnp.where(hot, 1.0, 0.0).astype(BF), jnp.where(before, 1.0, 0.0).astype(BF), preferred_element_type=F32
     )
-    rank[...] = jnp.sum(jnp.where(hot, earlier, 0.0), axis=0, keepdims=True).astype(jnp.int32)
+    rank = jnp.sum(jnp.where(hot, earlier, 0.0), axis=0, keepdims=True).astype(jnp.int32)
+    lanes = iota((LANES, slots), 0)
+    rank_hot[0] = jnp.where(lanes == rank, 1.0, 0.0).astype(BF)
+    rank_hot[1] = jnp.where(lanes == rank + F, 1.0, 0.0).astype(BF)
+    code = jnp.concatenate([cells[0:1, :], cells[1:2, :]], axis=1)
+    column_hot[...] = jnp.where(iota((4 * F, 2 * slots), 0) == (code & (4 * F - 1)), 1.0, 0.0).astype(BF)
     place[...] = jnp.full(place.shape, -4 * LANES, jnp.int32)
     for p in range(devices):
         piece = recv[:, capacity * p : capacity * (p + 1)]
         place[p : p + 1, 0:capacity] = piece
         place[p : p + 1, F : F + capacity] = piece
-
-
-def finish_kernel(
+    group[...] = place[...] >> 7
+    names = iota((LANES, LANES), 0)
+
+    def body(p, _):
+        spot = pl.ds(pl.multiple_of(p * LANES, LANES), LANES)
+        name_hot[:, spot] = jnp.where((place[pl.ds(p, 1), :] & (LANES - 1)) == names, 1.0, 0.0).astype(BF)
+        return 0
+
+    lax.fori_loop(0, devices, body, 0, unroll=8)
+
+
+def head_rows(head_weight):
+    line, spot = iota((8, 256), 0), iota((8, 256), 1)
+    head = []
+    for d in range(3):
+        weights = jnp.concatenate([head_weight[d : d + 1, :].astype(F32)] * 8, axis=1)
+        for z in range(2):
+            match = (spot // LANES == z) & ((spot // 32) % 4 == line % 4)
+            head.append(jnp.where(match, jnp.broadcast_to(weights, (8, 256)), 0.0))
+    return jnp.concatenate(head, axis=0).astype(BF)
+
+
+def stack_affinity(groups, tile, acc, add, planes, outer, lines, head, head_bias, scr, kept, kept_at):
+    for i in range(2):
+        left = jnp.concatenate(
+            [
+                planes[i, :, pl.ds(pl.multiple_of((tile + g) * LANES, LANES), 2 * LANES)]
+                for g in range(STACK)
+            ],
+            axis=0,
+        )
+        part = jnp.dot(left, outer[i], preferred_element_type=F32)
+        ends = [lines[side, i, groups, :] for side in range(2)]
+        for g in range(STACK):
+            o = STEP * g
+            scr[i, o + 8 : o + STEP, :] = part[LANES * g : LANES * (g + 1)]
+            scr[i, o + 7 : o + 8, 0:LANES] = ends[0][g : g + 1]
+            scr[i, o + STEP : o + STEP + 1, 2 * LANES :] = ends[1][g : g + 1]
+    hidden = []
+    for g in range(STACK):
+        o = STEP * g
+        outside = [
+            scr[i, o + 7 : o + 135, 0:LANES]
+            + scr[i, o + 8 : o + 136, LANES : 2 * LANES]
+            + scr[i, o + 9 : o + 137, 2 * LANES :]
+            for i in range(2)
+        ]
+        total = acc(g) + jnp.concatenate(outside, axis=1)
+        if add[g] is not None:
+            total = total + add[g]
+        hidden.append(jnp.maximum(total, 0.0).astype(BF))
+    logits = outer_product(head, jnp.concatenate(hidden, axis=0))
+    top_half = iota((8, LANES), 0) < 4
+    for i in range(6):
+        for pair in range(STACK // 2):
+            at = 2 * LANES * pair
+            both = logits[8 * i : 8 * i + 8]
+            value = jnp.where(top_half, both[:, at : at + LANES], both[:, at + LANES : at + 2 * LANES])
+            value = jax.nn.sigmoid(value + head_bias[i // 2]).astype(BF).astype(F32)
+            kept[i, pl.ds(pl.multiple_of(kept_at + 8 * pair, 8), 8), :] = value
+
+
+def stack_table(x0, kept_at, first, plain, y_code, z_code, kept, own_hot, pair_hot):
+    names, one, none = numbers(F), jnp.ones((F, LANES), BF), jnp.zeros((F, LANES), BF)
+    hot_before = None
+    for j in range(32):
+        t, x = j // 16, x0 + j
+        spot = slice(LANES * (j % 16), LANES * (j % 16 + 1))
+        weight = [spread(kept[i, pl.ds(kept_at + j, 1), :], 4) for i in range(6)]
+        hot, x_hot, y_hot = line_partners(plain, y_code, x, first, hot_before)
+        hot_before = hot
+        for z in range(2):
+            own_hot[t, z, :, spot] = jnp.where(hot[z], one, none)
+            pair_hot[t, z, 0:F, spot] = jnp.where(x_hot[z], weight[2 + z], none) + jnp.where(
+                y_hot[z], weight[4 + z], none
+            )
+        pair_hot[t, 1, F : 2 * F, spot] = jnp.where(hot[0], weight[1], none)
+        z_hot = spread(z_code[pl.ds(x, 1), :], 4) == names
+        pair_hot[t, 0, F : 2 * F, spot] = jnp.where(z_hot, weight[0], none)
+        pair_hot[t, 0, 2 * F :, spot] = jnp.where(z_hot, one, none)
+    low = outer_product(own_hot[0, 0], pair_hot[0, 0]) + outer_product(own_hot[1, 0], pair_hot[1, 0])
+    high = outer_product(own_hot[0, 1], pair_hot[0, 1, : 2 * F]) + outer_product(own_hot[1, 1], pair_hot[1, 1, : 2 * F])
+    return low, high
+
+
+def first_kernel(
     acc,
     plane_one,
     plane_two,
@@ -327,42 +419,37 @@
     inner_ends,
     outer,
     head_weight,
-    frag,
+    plain,
+    y_code,
     x_code,
-    y_low,
-    first_col,
-    counts,
-    cells,
-    owner,
-    rank,
     head_bias,
     flags,
     affinity,
-    outgoing,
+    kept_y,
+    low_out,
+    high_out,
+    x_outer,
+    lines,
+    z_code,
+    carry,
     planes,
     scr,
-    lines,
     kept,
     own_hot,
     pair_hot,
-    plain,
-    y_code,
-    z_code,
 ):
-    load_numbers(frag, plain, y_code)
     odd = flags[Z_ODD]
-    below = jnp.where(odd > 0, plane_one[:, WIDE:], plane_two[:, WIDE:])
+    below = jnp.where(odd > 0, plane_one[:, HEAD:], plane_two[:, HEAD:])
     z_code[...] = jnp.where(flags[Z_LOW] > 0, below.astype(F32), -1.0)
     lane = iota((LANES, LANES), 1)
     for plane, ring, i in ((plane_one, ring_one, 1 - odd), (plane_two, ring_two, odd)):
         live = jnp.where(i > 0, flags[Z_HIGH], flags[Z_LOW]) > 0
-        planes[i, :, LANES : WIDE - LANES] = plane[:, LANES : WIDE - LANES]
         around = jnp.where(live, ring[...], jnp.zeros(ring.shape, BF))
         face = around[:LANES, :]
+        planes[i, :, LANES:] = plane[:, LANES:HEAD]
         planes[i, :, :LANES] = jnp.where(lane < 32, face, plane[:, :LANES])
-        planes[i, :, WIDE - LANES :] = jnp.where(
-            (lane >= 32) & (lane < 64), face, plane[:, WIDE - LANES : WIDE]
-        )
+        carry[i] = plane[:, HEAD - LANES : HEAD]
+        carry[2 + i] = face
         for side, dy in ((0, 0), (1, 2)):
             chunks = around[LANES + EDGE * side : LANES + EDGE * (side + 1), :]
             lines[side, i] = jnp.dot(
@@ -371,111 +458,102 @@
     for i in range(2):
         for side in range(2):
             lines[side, i] = lines[side, i] + inner_lines[side, :, LANES * i : LANES * (i + 1)]
-    line, spot = iota((8, 256), 0), iota((8, 256), 1)
-    head = []
-    for d in range(3):
-        weights = jnp.concatenate([head_weight[d : d + 1, :].astype(F32)] * 8, axis=1)
-        for z in range(2):
-            match = (spot // LANES == z) & ((spot // 32) % 4 == line % 4)
-            head.append(jnp.where(match, jnp.broadcast_to(weights, (8, 256)), 0.0))
-    head = jnp.concatenate(head, axis=0).astype(BF)
-    top_half = iota((8, LANES), 0) < 4
-
-    def weight_row(d, z, x):
-        return spread(kept[2 * d + z, pl.ds(x, 1), :], 4)
-
-    def table_lines(x0, first, own_hot, pair_hot):
-        names, one, none = numbers(F), jnp.ones((F, LANES), BF), jnp.zeros((F, LANES), BF)
-        hot_before = None
-        for j in range(16):
-            x = x0 + j
-            spot = slice(LANES * j, LANES * (j + 1))
-            hot, x_hot, y_hot = line_partners(plain, y_code, x, first, hot_before)
-            hot_before = hot
-            for z in range(2):
-                own_hot[z, :, spot] = jnp.where(hot[z], one, none)
-                pair_hot[z, 0:F, spot] = jnp.where(x_hot[z], weight_row(1, z, x), none) + jnp.where(
-                    y_hot[z], weight_row(2, z, x), none
-                )
-            pair_hot[1, F : 2 * F, spot] = jnp.where(hot[0], weight_row(0, 1, x), none)
-            z_hot = spread(z_code[pl.ds(x, 1), :], 4) == names
-            pair_hot[0, F : 2 * F, spot] = jnp.where(z_hot, weight_row(0, 0, x), none)
-            pair_hot[0, 2 * F :, spot] = jnp.where(z_hot, one, none)
-
-    def body(s, carry):
-        low, high = carry
-        base = s * STACK
-        for i in range(2):
-            left = jnp.concatenate(
-                [
-                    planes[i, :, pl.ds(pl.multiple_of((base + g) * LANES, LANES), 2 * LANES)]
-                    for g in range(STACK)
-                ],
-                axis=0,
-            )
-            part = jnp.dot(left, outer[i], preferred_element_type=F32)
-            ends = [lines[side, i, pl.ds(pl.multiple_of(base, 8), STACK), :] for side in range(2)]
-            for g in range(STACK):
-                o = STEP * g
-                scr[i, o + 8 : o + STEP, :] = part[LANES * g : LANES * (g + 1)]
-                scr[i, o + 7 : o + 8, 0:LANES] = ends[0][g : g + 1]
-                scr[i, o + STEP : o + STEP + 1, 2 * LANES :] = ends[1][g : g + 1]
-        hidden = []
-        for g in range(STACK):
-            o = STEP * g
-            outside = [
-                scr[i, o + 7 : o + 135, 0:LANES]
-                + scr[i, o + 8 : o + 136, LANES : 2 * LANES]
-                + scr[i, o + 9 : o + 137, 2 * LANES :]
-                for i in range(2)
-            ]
-            total = acc[base + g] + jnp.concatenate(outside, axis=1)
-            if g == 0:
-                total = total + jnp.where(s == 0, inner_ends[0], 0.0)
-            if g == STACK - 1:
-                total = total + jnp.where(s == GROUPS // STACK - 1, inner_ends[1], 0.0)
-            hidden.append(jnp.maximum(total, 0.0).astype(BF))
-        logits = outer_product(head, jnp.concatenate(hidden, axis=0))
+    head = head_rows(head_weight)
+
+    def body(s, total):
+        base = pl.multiple_of(s * STACK, STACK)
+        x0 = pl.multiple_of(4 * STACK * s, 4 * STACK)
+        add = [None] * STACK
+        add[0] = jnp.where(s == 0, inner_ends[0], 0.0)
+        stack_affinity(
+            pl.ds(base, STACK), base, lambda g: acc[base + g], add, planes, outer, lines, head, head_bias, scr, kept, x0
+        )
+        all_lines = pl.ds(x0, 4 * STACK)
         for i in range(6):
-            for pair in range(STACK // 2):
-                at = 2 * LANES * pair
-                both = logits[8 * i : 8 * i + 8]
-                value = jnp.where(top_half, both[:, at : at + LANES], both[:, at + LANES : at + 2 * LANES])
-                value = jax.nn.sigmoid(value + head_bias[i // 2]).astype(BF).astype(F32)
-                kept[i, pl.ds(pl.multiple_of(4 * STACK * s + 8 * pair, 8), 8), :] = value
-            all_lines = pl.ds(pl.multiple_of(4 * STACK * s, 16), 4 * STACK)
             affinity[i // 2, i % 2, all_lines, :] = kept[i, all_lines, :].astype(BF)
-        for t in range(2):
-            first = jnp.where(s > 0, 0.0, -128.0) if t == 0 else 0.0
-            table_lines(4 * STACK * s + 16 * t, first, own_hot.at[t], pair_hot.at[t])
-            low = low + outer_product(own_hot[t, 0], pair_hot[t, 0])
-            high = high + outer_product(own_hot[t, 1], pair_hot[t, 1, : 2 * F])
-        return low, high
-
-    low, high = lax.fori_loop(
-        0, GROUPS // STACK, body, (jnp.zeros((F, 3 * F), F32), jnp.zeros((F, 2 * F), F32))
-    )
-    own = low[:, :F] + high[:, :F] + high[:, F:]
-    x_outer = faces_product(
+        first = jnp.where(s > 0, 0.0, -128.0)
+        low, high = stack_table(x0, x0, first, plain, y_code, z_code, kept, own_hot, pair_hot)
+        return total[0] + low, total[1] + high
+
+    low, high = lax.fori_loop(0, HEAD_STACKS, body, (jnp.zeros((F, 3 * F), F32), jnp.zeros((F, 2 * F), F32)))
+    low_out[...] = low
+    high_out[...] = high
+    kept_y[...] = kept[4:6]
+    x_outer[...] = faces_product(
         [plain[z, 0:1, :] for z in range(2)],
         [x_code[z] for z in range(2)],
         [kept[2 + z, 0:1, :] for z in range(2)],
     )
+
+
+def second_kernel(
+    acc,
+    plane_one,
+    plane_two,
+    inner_ends,
+    outer,
+    head_weight,
+    plain,
+    y_code,
+    y_low,
+    first_col,
+    counts,
+    affinity_head,
+    kept_y,
+    low_head,
+    high_head,
+    x_outer,
+    lines,
+    z_code,
+    carry,
+    cells,
+    owner,
+    rank_hot,
+    column_hot,
+    head_bias,
+    flags,
+    affinity,
+    outgoing,
+    planes,
+    scr,
+    kept,
+    own_hot,
+    pair_hot,
+):
+    odd = flags[Z_ODD]
+    lane = iota((LANES, LANES), 1)
+    wide = WIDE - HEAD
+    for i in range(2):
+        planes[i, :, :LANES] = carry[i]
+    for plane, i in ((plane_one, 1 - odd), (plane_two, odd)):
+        planes[i, :, LANES:wide] = plane[:, : wide - LANES]
+        planes[i, :, wide:] = jnp.where((lane >= 32) & (lane < 64), carry[2 + i], plane[:, wide - LANES :])
+    add = [None] * STACK
+    add[-1] = inner_ends[1]
+    groups = pl.ds(HEAD_GROUPS, STACK)
+    stack_affinity(
+        groups, 0, lambda g: acc[HEAD_GROUPS + g], add, planes, outer, lines, head_rows(head_weight), head_bias, scr, kept, 0
+    )
+    for i in range(6):
+        affinity[i // 2, i % 2, :HEAD_LINES, :] = affinity_head[i // 2, i % 2]
+        affinity[i // 2, i % 2, HEAD_LINES:, :] = kept[i].astype(BF)
+    low, high = stack_table(HEAD_LINES, 0, 0.0, plain, y_code, z_code, kept, own_hot, pair_hot)
+    low, high = low_head[...] + low, high_head[...] + high
+    own = low[:, :F] + high[:, :F] + high[:, F:]
     y_outer = faces_product(
         [first_col[z : z + 1, :] for z in range(2)],
         [y_partner(y_low, z, flags[Y_LOW] > 0) for z in range(2)],
-        [kept[4 + z].T[0:1, :] for z in range(2)],
-    )
-    sums = jnp.concatenate([own, low[:, F : 2 * F], x_outer, y_outer], axis=1)
+        [jnp.concatenate([kept_y[z], kept[4 + z]], axis=0).T[0:1, :] for z in range(2)],
+    )
+    sums = jnp.concatenate([own, low[:, F : 2 * F], x_outer[...], y_outer], axis=1)
     tally = counts[...] + jnp.concatenate(
         [jnp.zeros((F, F), F32), low[:, 2 * F :], jnp.zeros((F, 2 * F), F32)], axis=1
     )
     slots = cells.shape[1]
+    picked = jnp.dot(
+        jnp.concatenate(halves(sums) + halves(tally), axis=0), column_hot[...], preferred_element_type=F32
+    )
     code = jnp.concatenate([cells[0:1, :], cells[1:2, :]], axis=1)
-    column_hot = jnp.where(iota((4 * F, 2 * slots), 0) == (code & (4 * F - 1)), 1.0, 0.0).astype(BF)
-    picked = jnp.dot(
-        jnp.concatenate(halves(sums) + halves(tally), axis=0), column_hot, preferred_element_type=F32
-    )
     line_hot = iota((F, 2 * slots), 0) == (code >> 8)
     alive = iota((1, slots), 1) < flags[LIVE]
 
@@ -486,22 +564,19 @@
     part_sum = part_of(picked[:F] + picked[F : 2 * F])
     part_count = part_of(picked[2 * F : 3 * F] + picked[3 * F :])
     to_owner = iota((outgoing.shape[0], slots), 0) == owner[...]
-    lanes = iota((LANES, slots), 0)
-    low_hot = jnp.where(lanes == rank[...], 1.0, 0.0).astype(BF)
-    high_hot = jnp.where(lanes == rank[...] + F, 1.0, 0.0).astype(BF)
     left = [
         jnp.where(to_owner, piece.astype(F32), 0.0).astype(BF) for piece in halves(part_sum) + halves(part_count)
     ]
     sent = outer_product(
-        jnp.concatenate(left, axis=1), jnp.concatenate([low_hot, low_hot, high_hot, high_hot], axis=1)
+        jnp.concatenate(left, axis=1),
+        jnp.concatenate([rank_hot[0], rank_hot[0], rank_hot[1], rank_hot[1]], axis=1),
     )
     outgoing[...] = sent.reshape(outgoing.shape)
 
 
-def settle_kernel(received, slot, out, left, right):
+def settle_kernel(received, group_of, name_hot, out, left):
     devices = received.shape[0]
     groups = out.shape[1] // LANES
-    names = iota((LANES, LANES), 0)
     row, lane = iota((16, LANES), 0), iota((16, LANES), 1)
     of_count = row >= 2 * groups
     inner = jnp.where(of_count, row - 2 * groups, row)
@@ -512,16 +587,14 @@
 
     def body(p, _):
         spot = pl.ds(pl.multiple_of(p * LANES, LANES), LANES)
-        code = slot[pl.ds(p, 1), :]
         value = received[p]
         high = value.astype(BF).astype(F32)
         piece = jnp.where(is_low, value - high, high)
-        left[:, spot] = jnp.where((code >> 7) == group, piece, 0.0).astype(BF)
-        right[:, spot] = jnp.where((code & (LANES - 1)) == names, 1.0, 0.0).astype(BF)
+        left[:, spot] = jnp.where(group_of[pl.ds(p, 1), :] == group, piece, 0.0).astype(BF)
         return 0
 
     lax.fori_loop(0, devices, body, 0, unroll=8)
-    total = outer_product(left[...], right[...])
+    total = outer_product(left[...], name_hot[...])
     for g in range(groups):
         total_sum = total[g : g + 1] + total[groups + g : groups + g + 1]
         total_count = total[2 * groups + g : 2 * groups + g + 1] + total[3 * groups + g : 3 * groups + g + 1]
@@ -568,25 +641,23 @@
         flags += [at[axis], size[axis] - 1 - at[axis], at[axis] % 2]
     flags = jnp.stack(flags + [edge_count[0]]).astype(jnp.int32)
 
-    xt_low, xt_high, z_one, z_two, x_one, x_two, edge, first_col = pl.pallas_call(
+    xt_low, xt_high, z_one, z_two, end_one, end_two, x_one, x_two, edge, first_col = pl.pallas_call(
         layout_kernel,
         out_shape=(
             shape((LANES, WIDE), BF),
             shape((LANES, WIDE), BF),
-            shape((LANES, WIDE + LANES), BF),
-            shape((LANES, WIDE + LANES), BF),
+            shape((LANES, HEAD + LANES), BF),
+            shape((LANES, HEAD + LANES), BF),
+            shape((LANES, WIDE - HEAD), BF),
+            shape((LANES, WIDE - HEAD), BF),
             shape((2 * LANES + 16, LANES), BF),
             shape((2 * LANES + 16, LANES), BF),
             shape((4, EDGE, LANES), BF),
             shape((2, LANES), F32),
         ),
-        in_specs=[SMEM, pl.BlockSpec(memory_space=pl.ANY), VMEM],
-        out_specs=(VMEM,) * 8,
-        scratch_shapes=[
-            pltpu.VMEM((4, EDGE, LANES), F32),
-            pltpu.VMEM(features.shape, BF),
-            pltpu.SemaphoreType.DMA((8,)),
-        ],
+        in_specs=[SMEM, VMEM, VMEM],
+        out_specs=(VMEM,) * 10,
+        scratch_shapes=[pltpu.VMEM((4, EDGE, LANES), F32)],
         compiler_params=pltpu.CompilerParams(vmem_limit_bytes=28 << 20),
         cost_estimate=pl.CostEstimate(flops=1_000_000, bytes_accessed=1 << 20, transcendentals=0),
         name="layout",
@@ -604,12 +675,18 @@
         flops=5_000_000_000,
     )
     owner = edge_owner.reshape(1, slots)
-    rank, place = call(
+    rank_hot, column_hot, group, name_hot = call(
         slots_kernel,
         "slots",
-        (shape((1, slots), jnp.int32), shape((devices, LANES), jnp.int32)),
-        (owner, recv_slot),
+        (
+            shape((2, LANES, slots), BF),
+            shape((4 * F, 2 * slots), BF),
+            shape((devices, LANES), jnp.int32),
+            shape((LANES, devices * LANES), BF),
+        ),
+        (edge_cells, owner, recv_slot),
         0,
+        [pltpu.VMEM((devices, LANES), jnp.int32)],
     )
     face, x_code, y_one, y_two = call(
         x_face_kernel,
@@ -640,24 +717,40 @@
         0,
         flops=500_000_000,
     )
-    counts = call(
+    counts, plain, y_code = call(
         count_kernel,
         "pair_counts",
-        shape((F, 4 * F), F32),
+        (shape((F, 4 * F), F32), shape((2, LANES, LANES), F32), shape((2, LANES, LANES), F32)),
         (fragments, x_code, y_low, first_col, flags),
         1,
-        [
-            pltpu.VMEM((2, F, 4096), F8),
-            pltpu.VMEM((2, F, 4096), F8),
-            pltpu.VMEM((2, LANES, LANES), F32),
-            pltpu.VMEM((2, LANES, LANES), F32),
-        ],
+        [pltpu.VMEM((2, F, 4096), F8), pltpu.VMEM((2, F, 4096), F8)],
         flops=4_000_000_000,
     )
-    affinity, outgoing = call(
-        finish_kernel,
-        "finish",
-        (shape((3, 2, LANES, LANES), BF), shape((devices, 1, LANES), F32)),
+    end_one, end_two, counts = lax.optimization_barrier((end_one, end_two, counts))
+    end_one, end_two = swap(end_one, end_two, "gz", False)
+
+    def stack_scratch(tiles, kept_lines):
+        return [
+            pltpu.VMEM((2, LANES, tiles * LANES), BF),
+            pltpu.VMEM((2, STEP * STACK + 8, 3 * LANES), F32),
+            pltpu.VMEM((6, kept_lines, LANES), F32),
+            pltpu.VMEM((2, 2, F, 2048), BF),
+            pltpu.VMEM((2, 2, 3 * F, 2048), BF),
+        ]
+
+    done = call(
+        first_kernel,
+        "first_lines",
+        (
+            shape((3, 2, HEAD_LINES, LANES), BF),
+            shape((2, HEAD_LINES, LANES), F32),
+            shape((F, 3 * F), F32),
+            shape((F, 2 * F), F32),
+            shape((F, F), F32),
+            shape((2, 2, GROUPS, LANES), F32),
+            shape((LANES, LANES), F32),
+            shape((4, LANES, LANES), BF),
+        ),
         (
             acc,
             plane_one,
@@ -668,39 +761,52 @@
             ends,
             outer,
             head_weight,
-            fragments,
+            plain,
+            y_code,
             x_code,
-            y_low,
-            first_col,
-            counts,
-            edge_cells,
-            owner,
-            rank,
             head_bias,
             flags,
         ),
         2,
-        [
-            pltpu.VMEM((2, LANES, WIDE), BF),
-            pltpu.VMEM((2, STEP * STACK + 8, 3 * LANES), F32),
-            pltpu.VMEM((2, 2, GROUPS, LANES), F32),
-            pltpu.VMEM((6, LANES, LANES), F32),
-            pltpu.VMEM((2, 2, F, 2048), BF),
-            pltpu.VMEM((2, 2, 3 * F, 2048), BF),
-            pltpu.VMEM((2, LANES, LANES), F32),
-            pltpu.VMEM((2, LANES, LANES), F32),
-            pltpu.VMEM((LANES, LANES), F32),
-        ],
-        flops=8_000_000_000,
+        stack_scratch(HEAD_GROUPS + 1, HEAD_LINES),
+        flops=6_000_000_000,
+    )
+    affinity, outgoing = call(
+        second_kernel,
+        "last_lines",
+        (shape((3, 2, LANES, LANES), BF), shape((devices, 1, LANES), F32)),
+        (
+            acc,
+            end_one,
+            end_two,
+            ends,
+            outer,
+            head_weight,
+            plain,
+            y_code,
+            y_low,
+            first_col,
+            counts,
+            *done,
+            edge_cells,
+            owner,
+            rank_hot,
+            column_hot,
+            head_bias,
+            flags,
+        ),
+        2,
+        stack_scratch(TILES - HEAD_GROUPS, LANES - HEAD_LINES),
+        flops=3_000_000_000,
     )
     received = lax.all_to_all(outgoing, axes, split_axis=0, concat_axis=0, tiled=True)
     edge_mean = call(
         settle_kernel,
         "settle",
         shape((1, own_slots), F32),
-        (received, place),
+        (received, group, name_hot),
         0,
-        [pltpu.VMEM((16, devices * LANES), BF), pltpu.VMEM((LANES, devices * LANES), BF)],
+        [pltpu.VMEM((16, devices * LANES), BF)],
     )
     return affinity, edge_mean
 

time: 65 us -> 60.9 us (0.937)
  waiting for transfers between devices: 11 us -> 6.48 us
  blocking collectives: 12.9 us -> 11.8 us
  Pallas kernels: 24.4 us -> 25.3 us
    ppermute x1, waiting for transfers between devices: 2.82 us -> 0.01 us  [swap(): got = lax.ppermute(one, axis, [(0, 1), (1, 0)])]
    ppermute x6 -> x8, waiting for transfers between devices: 8.22 us -> 6.48 us  [swap(): lax.ppermute(value, axis, [pair for a, b in pairs for pair in ((a, b), (b...]
    pallas_call x8 -> x9, Pallas kernels: 21.5 us -> 23 us  [call(): pl.pallas_call(kernel, out_shape=out_shape, in_specs=[VMEM] * (len(args)...]
    ppermute x1, starting transfers between devices: 1.56 us -> 2.94 us  [swap(): got = lax.ppermute(one, axis, [(0, 1), (1, 0)])]
    all_to_all x1, blocking collectives: 12.9 us -> 11.8 us  [shards(): lax.all_to_all(outgoing, axes, split_axis=0, concat_axis=0, tiled=True)]
    ppermute x6 -> x8, starting transfers between devices: 10.8 us -> 10 us  [swap(): lax.ppermute(value, axis, [pair for a, b in pairs for pair in ((a, b), (b...]
  transfers between devices with their start and end apart: 7 -> 9, of which waited for: 3 -> 2; matrix products, arithmetic and copies ran while one was open for 0% -> 0% of each run, Pallas kernels for 14% -> 29%
where the time goes in v4:
time: 60.9 us; the launch traced here: 60.7 us
  Pallas kernels  25.3 us (42%)
  starting transfers between devices  13 us (21%)
  blocking collectives  11.8 us (19%)
  waiting for transfers between devices  6.48 us (11%)
  local copies, waits for them, and re-layouts  2.62 us (4%)
  between operations  1.5 us (2%)
    pallas_call x9, Pallas kernels, call(): pl.pallas_call(kernel, out_shape=out_shape, in_specs=[VMEM] * (len(args)...  23 us
    all_to_all x1, blocking collectives, shards(): lax.all_to_all(outgoing, axes, split_axis=0, concat_axis=0, tiled=True)  11.8 us
    ppermute x8, starting transfers between devices, swap(): lax.ppermute(value, axis, [pair for a, b in pairs for pair in ((a, b), (b...  10 us
    ppermute x8, waiting for transfers between devices, swap(): lax.ppermute(value, axis, [pair for a, b in pairs for pair in ((a, b), (b...  6.48 us
    ppermute x1, starting transfers between devices, swap(): got = lax.ppermute(one, axis, [(0, 1), (1, 0)])  2.94 us
    unnamed x20, local copies, waits for them, and re-layouts  2.53 us
    pallas_call x1, Pallas kernels, shards(): pl.pallas_call(layout_kernel, out_shape=(shape((LANES, WIDE), BF), shape(...  2.27 us
  transfers between devices with their start and end apart: 9, of which 2 were waited for; matrix products, arithmetic and copies ran while one was open for 0% of the time, Pallas kernels for 29%

profile of v4, /device:TPU:0, one launch (start us, length us, event | category | flops | bytes accessed | tf_op | source)
XLA Modules:
  0.0 60.7 jit_solution(18086638612512018160)
XLA Ops:
  1.3 0.1 stack.39.flags
  1.4 1.6 %copy-done = bf16[32,2,128,128]{3,2,1,0:T(8,128)(2,1)S(1)} copy-done((bf16[32,2,128,128]{3,2,1,0:T(8,128)(2,1)S(1)}, bf16[32,2,128,128]{3,2,1,0:T(8,128)(2,1)}, u32[]{:S(2)}) %copy-start) | copy-done | bytes 2097176
  3.0 0.9 %copy-done.1 = s32[2,128,128]{2,1,0:T(8,128)S(1)} copy-done((s32[2,128,128]{2,1,0:T(8,128)S(1)}, s32[2,128,128]{2,1,0:T(8,128)}, u32[]{:S(2)}) %copy-start.1) | copy-done | bytes 131096
  3.9 2.3 %layout.1 = (bf16[128,4224]{1,0:T(8,128)(2,1)S(1)}, bf16[128,4224]{1,0:T(8,128)(2,1)S(1)}, bf16[128,3328]{1,0:T(8,128)(2,1)S(1)}, bf16[128,3328]{1,0:T(8,128)(2,...) custom-call(s32[10]{0:T(128)S(1)} %stack.39.flags, ...), custom_call_target="tpu_custom_call" | custom-call | flops 1000000 | bytes 1048576 | tf_op jit(solution)/shard_map/layout/pallas_call | solution.py:644
  6.2 2.9 %collective-permute-start = (bf16[272,128]{1,0:T(8,128)(2,1)S(1)}, bf16[272,128]{1,0:T(8,128)(2,1)S(1)}, u32[]{:S(2)}, u32[]{:S(2)}) collective-permute-start(bf16[272,128]{1,0:T(8,128)(2,1)S(1)} %get-tuple-element.49), channel_id=1, source_target_pairs={{0,16},{16,0},{1,17},{17,1},{2,18},{18,2},{3,19},{19,3},{4,20},{20... | collective-permute-start | bytes 208904 | tf_op jit(solution)/shard_map/ppermute | solution.py:610
  9.1 1.6 %collective-permute-start.5 = (bf16[128,3328]{1,0:T(8,128)(2,1)S(1)}, bf16[128,3328]{1,0:T(8,128)(2,1)S(1)}, u32[]{:S(2)}, u32[]{:S(2)}) collective-permute-start(bf16[128,3328]{1,0:T(8,128)(2,1)S(1)} %get-tuple-element.67), channel_id=1, source_target_pairs={{0,1},{1,0},{2,3},{3,2},{4,5},{5,4},{6,7},{7,6},{8,9},{9,8},{10,11... | collective-permute-start | bytes 2555912 | tf_op jit(solution)/shard_map/ppermute | solution.py:615
  10.7 0.7 %collective-permute-start.6 = (bf16[128,3328]{1,0:T(8,128)(2,1)S(1)}, bf16[128,3328]{1,0:T(8,128)(2,1)S(1)}, u32[]{:S(2)}, u32[]{:S(2)}) collective-permute-start(bf16[128,3328]{1,0:T(8,128)(2,1)S(1)} %get-tuple-element.68), channel_id=1, source_target_pairs={{1,2},{2,1},{5,6},{6,5},{9,10},{10,9},{13,14},{14,13},{17,18},{18,... | collective-permute-start | bytes 2555912 | tf_op jit(solution)/shard_map/ppermute | solution.py:615
  11.4 0.0 collective-permute-done.got_one.got_two
  11.4 0.6 x_face.1
  12.0 0.1 collective-permute-start.1
  12.1 2.2 %collective-permute-start.2 = (bf16[2,48,128]{2,1,0:T(8,128)(2,1)S(1)}, bf16[2,48,128]{2,1,0:T(8,128)(2,1)S(1)}, u32[]{:S(2)}, u32[]{:S(2)}) collective-permute-start(bf16[2,48,128]{2,1,0:T(8,128)(2,1)S(1)} %get-tuple-element.54), channel_id=1, source_target_pairs={{4,8},{8,4},{0,12},{12,0},{5,9},{9,5},{1,13},{13,1},{6,10},{10,6},... | collective-permute-start | bytes 73736 | tf_op jit(solution)/shard_map/ppermute | solution.py:615
  14.2 0.0 copy-start.5
  14.3 0.0 copy-start.2
  14.3 4.6 %own_planes.1 = (f32[32,128,256]{2,1,0:T(8,128)S(1)}, bf16[3,512,256]{2,1,0:T(8,128)(2,1)S(1)}, bf16[2,256,384]{2,1,0:T(8,128)(2,1)S(1)}) custom-call(bf16[128,4224]{1,0:T(8,128)(2,1)S(1)} %get-tuple-element.44.low, bf16[128,4224]{1,0:T(8,128)(2,1)S(1)} %get-tuple-element.45.high, bf16[27,32,32]{2,1,0:T(8,128)(2,1)S(1)} %copy-done.6, f32[1,32]{1,0:T(1,128)S(1)} %bitcast.13), custom_call_target="tpu_custom_call" | custom-call | flops 5000000000 | bytes 1048576 | tf_op jit(solution)/shard_map/own_planes/pallas_call | solution.py:28
  18.9 1.2 %slots.1 = (bf16[2,128,1024]{2,1,0:T(8,128)(2,1)S(1)}, bf16[256,2048]{1,0:T(8,128)(2,1)S(1)}, s32[32,128]{1,0:T(8,128)S(1)}, bf16[128,4096]{1,0:T(8,128)(2,1)S(1)}) custom-call(s32[2,1024]{1,0:T(2,128)S(1)} %copy-done.3, s32[1,1024]{1,0:T(1,128)S(1)} %bitcast.11, s32[1,1536]{1,0:T(1,128)S(1)} %copy-done.4), custom_call_target="tpu_custom_call" | custom-call | flops 1000000 | bytes 1048576 | tf_op jit(solution)/shard_map/slots/pallas_call | solution.py:28
  20.2 0.0 collective-permute-done.2.got_two
  20.2 0.6 ring.1
  20.7 3.9 %collective-permute-start.7 = (bf16[224,128]{1,0:T(8,128)(2,1)S(1)}, bf16[224,128]{1,0:T(8,128)(2,1)S(1)}, u32[]{:S(2)}, u32[]{:S(2)}) collective-permute-start(bf16[224,128]{1,0:T(8,128)(2,1)S(1)} %get-tuple-element.69), channel_id=1, source_target_pairs={{0,1},{1,0},{2,3},{3,2},{4,5},{5,4},{6,7},{7,6},{8,9},{9,8},{10,11... | collective-permute-start | bytes 172040 | tf_op jit(solution)/shard_map/ppermute | solution.py:615
  24.6 0.9 %collective-permute-start.8 = (bf16[224,128]{1,0:T(8,128)(2,1)S(1)}, bf16[224,128]{1,0:T(8,128)(2,1)S(1)}, u32[]{:S(2)}, u32[]{:S(2)}) collective-permute-start(bf16[224,128]{1,0:T(8,128)(2,1)S(1)} %get-tuple-element.70), channel_id=1, source_target_pairs={{1,2},{2,1},{0,3},{3,0},{5,6},{6,5},{4,7},{7,4},{9,10},{10,9},{8,1... | collective-permute-start | bytes 172040 | tf_op jit(solution)/shard_map/ppermute | solution.py:615
  25.6 2.3 %pair_counts.1 = (f32[64,256]{1,0:T(8,128)S(1)}, f32[2,128,128]{2,1,0:T(8,128)S(1)}, f32[2,128,128]{2,1,0:T(8,128)S(1)}) custom-call(s32[2,128,128]{2,1,0:T(8,128)S(1)} %copy-done.2, f32[2,1,128]{2,1,0:T(1,128)S(1)} %get-tuple-element.51.x_code, bf16[2,48,128]{2,1,0:T(8,128)(2,1)S(1)} %get-tuple-element.55.y_low, f32[2,128]{1,0:T(2,128)S(1)} %get-tuple-element.56.first_col, ...), custom_call_target="tpu_custom_call" | custom-call | flops 4000000000 | bytes 1048576 | tf_op jit(solution)/shard_map/pair_counts/pallas_call | solution.py:28
  27.9 0.1 collective-permute-start.3
  28.0 0.4 edges.1
  28.3 3.1 %collective-permute-done.7.ring_one = bf16[224,128]{1,0:T(8,128)(2,1)S(1)} collective-permute-done((bf16[224,128]{1,0:T(8,128)(2,1)S(1)}, bf16[224,128]{1,0:T(8,128)(2,1)S(1)}, u32[]{:S(2)}, u32[]{:S(2)}) %collective-permute-start.7) | collective-permute-done | bytes 57376 | tf_op jit(solution)/shard_map/ppermute | solution.py:615
  31.5 0.7 %collective-permute-start.4 = (bf16[128,1024]{1,0:T(8,128)(2,1)S(1)}, bf16[128,1024]{1,0:T(8,128)(2,1)S(1)}, u32[]{:S(2)}, u32[]{:S(2)}) collective-permute-start(bf16[128,1024]{1,0:T(8,128)(2,1)S(1)} %get-tuple-element.59), channel_id=1, source_target_pairs={{1,2},{2,1},{5,6},{6,5},{9,10},{10,9},{13,14},{14,13},{17,18},{18,... | collective-permute-start | bytes 786440 | tf_op jit(solution)/shard_map/ppermute | solution.py:615
  32.1 3.3 %collective-permute-done.8.ring_two = bf16[224,128]{1,0:T(8,128)(2,1)S(1)} collective-permute-done((bf16[224,128]{1,0:T(8,128)(2,1)S(1)}, bf16[224,128]{1,0:T(8,128)(2,1)S(1)}, u32[]{:S(2)}, u32[]{:S(2)}) %collective-permute-start.8) | collective-permute-done | bytes 57376 | tf_op jit(solution)/shard_map/ppermute | solution.py:615
  35.5 0.0 collective-permute-done.5.plane_one
  35.5 0.0 collective-permute-done.6.plane_two
  35.5 7.7 %first_lines.1 = (bf16[3,2,96,128]{3,2,1,0:T(8,128)(2,1)S(1)}, f32[2,96,128]{2,1,0:T(8,128)S(1)}, f32[64,192]{1,0:T(8,128)S(1)}, f32[64,128]{1,0:T(8,128)S(1)}, ...) custom-call(f32[32,128,256]{2,1,0:T(8,128)S(1)} %get-tuple-element.4, ...), custom_call_target="tpu_custom_call" | custom-call | flops 6000000000 | bytes 1048576 | tf_op jit(solution)/shard_map/first_lines/pallas_call | solution.py:28
  43.3 0.0 collective-permute-done.4.plane_two
  43.3 4.6 %last_lines.1 = (bf16[3,2,128,128]{3,2,1,0:T(8,128)(2,1)}, f32[32,1,128]{2,1,0:T(1,128)S(1)}) custom-call(f32[32,128,256]{2,1,0:T(8,128)S(1)} %get-tuple-element.46.acc, bf16[128,1024]{1,0:T(8,128)(2,1)S(1)} %collective-permute-done.3.plane_one, bf16[128,1024]{1,0:T(8,128)(2,1)S(1)} %collective-permute-done.4.plane_two, ...), custom_call_target="tpu_custom_call" | custom-call | flops 3000000000 | bytes 1048576 | tf_op jit(solution)/shard_map/last_lines/pallas_call | solution.py:28
  47.9 11.8 %all_to_all.5.received = f32[32,1,128]{2,1,0:T(1,128)S(1)} all-to-all(f32[32,1,128]{2,1,0:T(1,128)S(1)} %get-tuple-element.83), channel_id=1, replica_groups=mesh['gx'=2,'gy'=4,'gz'=4] {'gx','gy','gz'}, dimensions={0} | all-to-all | bytes 32768 | tf_op jit(solution)/shard_map/all_to_all | solution.py:802
  59.6 1.0 %settle.1 = f32[1,384]{1,0:T(1,128)} custom-call(f32[32,1,128]{2,1,0:T(1,128)S(1)} %all_to_all.5.received, s32[32,128]{1,0:T(8,128)S(1)} %get-tuple-element.84.group_of, bf16[128,4096]{1,0:T(8,128)(2,1)S(1)} %get-tuple-element.85.name_hot), custom_call_target="tpu_custom_call" | custom-call | flops 1000000 | bytes 1048576 | tf_op jit(solution)/shard_map/settle/pallas_call | solution.py:28
  (18 shorter events, 0.0 us)
Async XLA Ops:
  0.6 13.6 %copy-start.8 = (f32[32]{0:T(128)S(1)}, f32[32]{0:T(128)}, u32[]{:S(2)}) copy-start(f32[32]{0:T(128)} %param.12) | copy-start | bytes 388
  1.4 1.6 %copy-start = (bf16[32,2,128,128]{3,2,1,0:T(8,128)(2,1)S(1)}, bf16[32,2,128,128]{3,2,1,0:T(8,128)(2,1)}, u32[]{:S(2)}) copy-start(bf16[32,2,128,128]{3,2,1,0:T(8,128)(2,1)} %feat.1) | copy-start | bytes 6291460
  3.0 0.9 %copy-start.1 = (s32[2,128,128]{2,1,0:T(8,128)S(1)}, s32[2,128,128]{2,1,0:T(8,128)}, u32[]{:S(2)}) copy-start(s32[2,128,128]{2,1,0:T(8,128)} %frag.3) | copy-start | bytes 393220
  3.9 10.3 %copy-start.6 = (bf16[27,32,32]{2,1,0:T(8,128)(2,1)S(1)}, bf16[27,32,32]{2,1,0:T(8,128)(2,1)}, u32[]{:S(2)}) copy-start(bf16[27,32,32]{2,1,0:T(8,128)(2,1)} %conv_weight.1) | copy-start | bytes 165892
  6.2 5.2 %collective-permute-start = (bf16[272,128]{1,0:T(8,128)(2,1)S(1)}, bf16[272,128]{1,0:T(8,128)(2,1)S(1)}, u32[]{:S(2)}, u32[]{:S(2)}) collective-permute-start(bf16[272,128]{1,0:T(8,128)(2,1)S(1)} %get-tuple-element.49), channel_id=1, source_target_pairs={{0,16},{16,0},{1,17},{17,1},{2,18},{18,2},{3,19},{19,3},{4,20},{20... | collective-permute-start | bytes 208904 | tf_op jit(solution)/shard_map/ppermute | solution.py:610
  9.1 26.4 %collective-permute-start.5 = (bf16[128,3328]{1,0:T(8,128)(2,1)S(1)}, bf16[128,3328]{1,0:T(8,128)(2,1)S(1)}, u32[]{:S(2)}, u32[]{:S(2)}) collective-permute-start(bf16[128,3328]{1,0:T(8,128)(2,1)S(1)} %get-tuple-element.67), channel_id=1, source_target_pairs={{0,1},{1,0},{2,3},{3,2},{4,5},{5,4},{6,7},{7,6},{8,9},{9,8},{10,11... | collective-permute-start | bytes 2555912 | tf_op jit(solution)/shard_map/ppermute | solution.py:615
  10.7 24.8 %collective-permute-start.6 = (bf16[128,3328]{1,0:T(8,128)(2,1)S(1)}, bf16[128,3328]{1,0:T(8,128)(2,1)S(1)}, u32[]{:S(2)}, u32[]{:S(2)}) collective-permute-start(bf16[128,3328]{1,0:T(8,128)(2,1)S(1)} %get-tuple-element.68), channel_id=1, source_target_pairs={{1,2},{2,1},{5,6},{6,5},{9,10},{10,9},{13,14},{14,13},{17,18},{18,... | collective-permute-start | bytes 2555912 | tf_op jit(solution)/shard_map/ppermute | solution.py:615
  12.0 8.1 %collective-permute-start.1 = (bf16[2,48,128]{2,1,0:T(8,128)(2,1)S(1)}, bf16[2,48,128]{2,1,0:T(8,128)(2,1)S(1)}, u32[]{:S(2)}, u32[]{:S(2)}) collective-permute-start(bf16[2,48,128]{2,1,0:T(8,128)(2,1)S(1)} %get-tuple-element.53), channel_id=1, source_target_pairs={{0,4},{4,0},{8,12},{12,8},{1,5},{5,1},{9,13},{13,9},{2,6},{6,2},{1... | collective-permute-start | bytes 73736 | tf_op jit(solution)/shard_map/ppermute | solution.py:615
  12.1 8.1 %collective-permute-start.2 = (bf16[2,48,128]{2,1,0:T(8,128)(2,1)S(1)}, bf16[2,48,128]{2,1,0:T(8,128)(2,1)S(1)}, u32[]{:S(2)}, u32[]{:S(2)}) collective-permute-start(bf16[2,48,128]{2,1,0:T(8,128)(2,1)S(1)} %get-tuple-element.54), channel_id=1, source_target_pairs={{4,8},{8,4},{0,12},{12,0},{5,9},{9,5},{1,13},{13,1},{6,10},{10,6},... | collective-permute-start | bytes 73736 | tf_op jit(solution)/shard_map/ppermute | solution.py:615
  14.2 4.6 %copy-start.3 = (s32[2,1024]{1,0:T(2,128)S(1)}, s32[2,1024]{1,0:T(2,128)}, u32[]{:S(2)}) copy-start(s32[2,1024]{1,0:T(2,128)} %cells.3) | copy-start | bytes 24580
  14.2 4.7 %copy-start.4 = (s32[1,1536]{1,0:T(1,128)S(1)}, s32[1,1536]{1,0:T(1,128)}, u32[]{:S(2)}) copy-start(s32[1,1536]{1,0:T(1,128)} %recv.1) | copy-start | bytes 18436
  14.2 4.7 %copy-start.5 = (s32[1024,1]{0,1:T(1,128)S(1)}, s32[1024,1]{0,1:T(1,128)}, u32[]{:S(2)}) copy-start(s32[1024,1]{0,1:T(1,128)} %param.17) | copy-start | bytes 12292
  14.3 11.3 %copy-start.2 = (s32[2,128,128]{2,1,0:T(8,128)S(1)}, s32[2,128,128]{2,1,0:T(8,128)}, u32[]{:S(2)}) copy-start(s32[2,128,128]{2,1,0:T(8,128)} %frag.3) | copy-start | bytes 393220
  20.7 10.7 %collective-permute-start.7 = (bf16[224,128]{1,0:T(8,128)(2,1)S(1)}, bf16[224,128]{1,0:T(8,128)(2,1)S(1)}, u32[]{:S(2)}, u32[]{:S(2)}) collective-permute-start(bf16[224,128]{1,0:T(8,128)(2,1)S(1)} %get-tuple-element.69), channel_id=1, source_target_pairs={{0,1},{1,0},{2,3},{3,2},{4,5},{5,4},{6,7},{7,6},{8,9},{9,8},{10,11... | collective-permute-start | bytes 172040 | tf_op jit(solution)/shard_map/ppermute | solution.py:615
  24.6 10.8 %collective-permute-start.8 = (bf16[224,128]{1,0:T(8,128)(2,1)S(1)}, bf16[224,128]{1,0:T(8,128)(2,1)S(1)}, u32[]{:S(2)}, u32[]{:S(2)}) collective-permute-start(bf16[224,128]{1,0:T(8,128)(2,1)S(1)} %get-tuple-element.70), channel_id=1, source_target_pairs={{1,2},{2,1},{0,3},{3,0},{5,6},{6,5},{4,7},{7,4},{9,10},{10,9},{8,1... | collective-permute-start | bytes 172040 | tf_op jit(solution)/shard_map/ppermute | solution.py:615
  25.6 9.9 %copy-start.7 = (bf16[3,32]{1,0:T(4,128)(2,1)S(1)}, bf16[3,32]{1,0:T(4,128)(2,1)}, u32[]{:S(2)}) copy-start(bf16[3,32]{1,0:T(4,128)(2,1)} %head_weight.3) | copy-start | bytes 580
  25.6 9.9 %copy-start.9 = (f32[3]{0:T(128)S(1)}, f32[3]{0:T(128)}, u32[]{:S(2)}) copy-start(f32[3]{0:T(128)} %head_bias.3) | copy-start | bytes 40
  27.9 15.4 %collective-permute-start.3 = (bf16[128,1024]{1,0:T(8,128)(2,1)S(1)}, bf16[128,1024]{1,0:T(8,128)(2,1)S(1)}, u32[]{:S(2)}, u32[]{:S(2)}) collective-permute-start(bf16[128,1024]{1,0:T(8,128)(2,1)S(1)} %get-tuple-element.58), channel_id=1, source_target_pairs={{0,1},{1,0},{2,3},{3,2},{4,5},{5,4},{6,7},{7,6},{8,9},{9,8},{10,11... | collective-permute-start | bytes 786440 | tf_op jit(solution)/shard_map/ppermute | solution.py:615
  31.5 11.8 %collective-permute-start.4 = (bf16[128,1024]{1,0:T(8,128)(2,1)S(1)}, bf16[128,1024]{1,0:T(8,128)(2,1)S(1)}, u32[]{:S(2)}, u32[]{:S(2)}) collective-permute-start(bf16[128,1024]{1,0:T(8,128)(2,1)S(1)} %get-tuple-element.59), channel_id=1, source_target_pairs={{1,2},{2,1},{5,6},{6,5},{9,10},{10,9},{13,14},{14,13},{17,18},{18,... | collective-permute-start | bytes 786440 | tf_op jit(solution)/shard_map/ppermute | solution.py:615

commit v5 on v4

--- a/solution.py
+++ b/solution.py
@@ -13,6 +13,7 @@
 STACK = 8
 STEP = LANES + 8
 EDGE = 48
+RING = LANES + 2 * EDGE
 HEAD_STACKS = 3
 HEAD_GROUPS = HEAD_STACKS * STACK
 HEAD = (HEAD_GROUPS + 1) * LANES
@@ -32,7 +33,7 @@
         out_specs=jax.tree.map(lambda _: VMEM, out_shape),
         scratch_shapes=list(scratch),
         compiler_params=pltpu.CompilerParams(vmem_limit_bytes=28 << 20),
-        cost_estimate=pl.CostEstimate(flops=flops, bytes_accessed=1 << 20, transcendentals=0),
+        cost_estimate=pl.CostEstimate(flops=flops, bytes_accessed=1 << 17, transcendentals=0),
         name=name,
     )(*args)
 
@@ -57,12 +58,18 @@
     return high, (value - high.astype(F32)).astype(BF)
 
 
-def layout_kernel(flags, feat, frag, low, high, z_one, z_two, end_one, end_two, x_one, x_two, edge, first_col, rows):
-    x_odd, z_odd = flags[X_ODD] > 0, flags[Z_ODD] > 0
+def layout_kernel(flags, feat_hbm, low, high, z_one, z_two, end_one, end_two, feat, sems):
+    copies = []
+    for t in range(8):
+        lines = slice(16 * t, 16 * t + 16)
+        copies.append(pltpu.make_async_copy(feat_hbm.at[:, :, lines, :], feat.at[:, :, lines, :], sems.at[t]))
+        copies[-1].start()
+    odd = flags[Z_ODD] > 0
     zero = jnp.zeros((32, LANES), BF)
     last = [zero, zero]
-    tile_zero = [None, None]
     for t in range(9):
+        if t < 8:
+            copies[t].wait()
         both = []
         for z, plane in ((0, low), (1, high)):
             if t < 8:
@@ -74,36 +81,33 @@
             wide = turned.shape[1]
             plane[:, 512 * t : 512 * t + wide] = turned
             both.append(turned)
-            for side, line in ((0, turned[112:128].astype(F32)[15:16]), (1, turned[0:16].astype(F32)[0:1])):
-                for q in range(wide // LANES):
-                    spot = 4 * t + q
-                    rows[2 * side + z, spot : spot + 1, :] = line[:, LANES * q : LANES * (q + 1)]
-            if t == 0:
-                tile_zero[z] = turned[:, :LANES]
-            if t == 8:
-                lines = slice(LANES * z, LANES * (z + 1))
-                x_one[lines, :] = jnp.where(x_odd, tile_zero[z], turned)
-                x_two[lines, :] = jnp.where(x_odd, turned, tile_zero[z])
         for head, end, value in (
-            (z_one, end_one, jnp.where(z_odd, both[0], both[1])),
-            (z_two, end_two, jnp.where(z_odd, both[1], both[0])),
+            (z_one, end_one, jnp.where(odd, both[0], both[1])),
+            (z_two, end_two, jnp.where(odd, both[1], both[0])),
         ):
             cut = min(max(HEAD - 512 * t, 0), wide)
             if cut > 0:
                 head[:, 512 * t : 512 * t + cut] = value[:, :cut]
             if cut < wide:
                 end[:, 512 * t + cut - HEAD : 512 * t + wide - HEAD] = value[:, cut:]
-    for z in range(2):
+
+
+def face_kernel(low, high, frag, flags, x_one, x_two, edge, first_col, rows):
+    odd = flags[X_ODD] > 0
+    for z, plane in ((0, low), (1, high)):
+        lines = slice(LANES * z, LANES * (z + 1))
+        start, end = plane[:, :LANES], plane[:, WIDE - LANES :]
+        x_one[lines, :] = jnp.where(odd, start, end)
+        x_two[lines, :] = jnp.where(odd, end, start)
         turned = frag[z].astype(F32).T
         first_col[z : z + 1, :] = turned[0:1]
-        for side in range(2):
+        for side, line in ((0, plane[112:128, :].astype(F32)[15:16]), (1, plane[0:16, :].astype(F32)[0:1])):
+            for q in range(TILES):
+                rows[2 * side + z, q : q + 1, :] = line[:, LANES * q : LANES * (q + 1)]
             rows[2 * side + z, TILES:EDGE, :] = jnp.broadcast_to(turned[127:128], (EDGE - TILES, LANES))
             edge[2 * side + z] = rows[2 * side + z].astype(BF)
-    top = frag[1].astype(F32).astype(BF)
     lines = [jnp.broadcast_to(frag[z, 127:128, :], (8, LANES)).astype(F32) for z in range(2)]
     lines = jnp.concatenate(lines, axis=0).astype(BF)
-    for out in (z_one, z_two):
-        out[:, HEAD:] = top
     for out in (x_one, x_two):
         out[2 * LANES :, :] = lines
 
@@ -134,7 +138,7 @@
         x_code[z] = jnp.where(has_low, other[8 * z : 8 * z + 1], -1.0)
 
 
-def ring_kernel(face, got_one, got_two, flags, y_low, y_high, z_one, z_two):
+def ring_kernel(face, got_one, got_two, frag, flags, y_low, y_high, z_one, z_two):
     odd, z_odd = flags[Y_ODD] > 0, flags[Z_ODD] > 0
     none = jnp.zeros((EDGE, LANES), BF)
     rings = []
@@ -144,8 +148,11 @@
         y_low[z] = low
         y_high[z] = high
         rings.append(jnp.concatenate([face[z], low, high], axis=0))
-    z_one[...] = jnp.where(z_odd, rings[0], rings[1])
-    z_two[...] = jnp.where(z_odd, rings[1], rings[0])
+    z_one[:RING, :] = jnp.where(z_odd, rings[0], rings[1])
+    z_two[:RING, :] = jnp.where(z_odd, rings[1], rings[0])
+    top = frag[1].astype(F32).astype(BF)
+    for out in (z_one, z_two):
+        out[RING:, :] = top
 
 
 def banded(weight, z_off, dy, slot, quarter):
@@ -208,7 +215,9 @@
     return jnp.concatenate([wide[:GROUPS], wide[1:TILES]], axis=1).astype(BF)
 
 
-def edge_kernel(face, y_low, y_high, inner, lines, ends):
+def edge_kernel(
+    face, y_low, y_high, inner, plain, x_code, first_col, own_counts, flags, lines, ends, counts
+):
     for side, (dy, source) in enumerate(((0, y_low), (2, y_high))):
         left = jnp.concatenate([line_windows(source[z]) for z in range(2)], axis=1)
         lines[side] = jnp.dot(left, inner[dy], preferred_element_type=F32)
@@ -231,6 +240,12 @@
             + parts[1]
             + jnp.where(row == LANES - 1, 0.0, pltpu.roll(parts[2], LANES - 1, 0))
         )
+    ones = [jnp.ones((1, LANES), F32)] * 2
+    x_outer = faces_product([plain[z, 0:1, :] for z in range(2)], [x_code[z] for z in range(2)], ones)
+    y_outer = faces_product(
+        [first_col[z : z + 1, :] for z in range(2)], [y_partner(y_low, z, flags[Y_LOW] > 0) for z in range(2)], ones
+    )
+    counts[...] = jnp.concatenate([own_counts[...], jnp.zeros((F, F), F32), x_outer, y_outer], axis=1)
 
 
 def spread(row, copies):
@@ -273,7 +288,7 @@
     return jnp.where(has_low, y_low[z, TILES - 1 :, :].astype(F32)[8:9], -1.0)
 
 
-def count_kernel(frag, x_code, y_low, first_col, flags, out, plain, y_code, own_hot, pair_hot):
+def count_kernel(frag, out, plain, y_code, own_hot, pair_hot):
     load_numbers(frag, plain, y_code)
     one = jnp.ones((F, LANES), BF)
     none = jnp.zeros((F, LANES), BF)
@@ -295,13 +310,7 @@
             total = total + outer_product(own_hot[z], pair_hot[z])
         return total
 
-    own = lax.fori_loop(0, 4, body, jnp.zeros((F, F), F32))
-    ones = [jnp.ones((1, LANES), F32)] * 2
-    x_outer = faces_product([plain[z, 0:1, :] for z in range(2)], [x_code[z] for z in range(2)], ones)
-    y_outer = faces_product(
-        [first_col[z : z + 1, :] for z in range(2)], [y_partner(y_low, z, flags[Y_LOW] > 0) for z in range(2)], ones
-    )
-    out[...] = jnp.concatenate([own, jnp.zeros((F, F), F32), x_outer, y_outer], axis=1)
+    out[...] = lax.fori_loop(0, 4, body, jnp.zeros((F, F), F32))
 
 
 def slots_kernel(cells, owner, recv, rank_hot, column_hot, group, name_hot, place):
@@ -335,6 +344,26 @@
     lax.fori_loop(0, devices, body, 0, unroll=8)
 
 
+def ahead_kernel(
+    cells,
+    owner,
+    recv,
+    frag,
+    rank_hot,
+    column_hot,
+    group,
+    name_hot,
+    counts,
+    plain,
+    y_code,
+    place,
+    own_hot,
+    pair_hot,
+):
+    count_kernel(frag, counts, plain, y_code, own_hot, pair_hot)
+    slots_kernel(cells, owner, recv, rank_hot, column_hot, group, name_hot, place)
+
+
 def head_rows(head_weight):
     line, spot = iota((8, 256), 0), iota((8, 256), 1)
     head = []
@@ -350,7 +379,7 @@
     for i in range(2):
         left = jnp.concatenate(
             [
-                planes[i, :, pl.ds(pl.multiple_of((tile + g) * LANES, LANES), 2 * LANES)]
+                planes[i, :, (tile + g) * LANES : (tile + g + 2) * LANES]
                 for g in range(STACK)
             ],
             axis=0,
@@ -383,7 +412,7 @@
             both = logits[8 * i : 8 * i + 8]
             value = jnp.where(top_half, both[:, at : at + LANES], both[:, at + LANES : at + 2 * LANES])
             value = jax.nn.sigmoid(value + head_bias[i // 2]).astype(BF).astype(F32)
-            kept[i, pl.ds(pl.multiple_of(kept_at + 8 * pair, 8), 8), :] = value
+            kept[i, kept_at + 8 * pair : kept_at + 8 * pair + 8, :] = value
 
 
 def stack_table(x0, kept_at, first, plain, y_code, z_code, kept, own_hot, pair_hot):
@@ -439,12 +468,12 @@
     pair_hot,
 ):
     odd = flags[Z_ODD]
-    below = jnp.where(odd > 0, plane_one[:, HEAD:], plane_two[:, HEAD:])
+    below = jnp.where(odd > 0, ring_one[RING:, :], ring_two[RING:, :])
     z_code[...] = jnp.where(flags[Z_LOW] > 0, below.astype(F32), -1.0)
     lane = iota((LANES, LANES), 1)
     for plane, ring, i in ((plane_one, ring_one, 1 - odd), (plane_two, ring_two, odd)):
         live = jnp.where(i > 0, flags[Z_HIGH], flags[Z_LOW]) > 0
-        around = jnp.where(live, ring[...], jnp.zeros(ring.shape, BF))
+        around = jnp.where(live, ring[:RING, :], jnp.zeros((RING, LANES), BF))
         face = around[:LANES, :]
         planes[i, :, LANES:] = plane[:, LANES:HEAD]
         planes[i, :, :LANES] = jnp.where(lane < 32, face, plane[:, :LANES])
@@ -460,22 +489,29 @@
             lines[side, i] = lines[side, i] + inner_lines[side, :, LANES * i : LANES * (i + 1)]
     head = head_rows(head_weight)
 
-    def body(s, total):
-        base = pl.multiple_of(s * STACK, STACK)
-        x0 = pl.multiple_of(4 * STACK * s, 4 * STACK)
+    def affinities(s):
+        base, x0 = STACK * s, 4 * STACK * s
         add = [None] * STACK
-        add[0] = jnp.where(s == 0, inner_ends[0], 0.0)
+        if s == 0:
+            add[0] = inner_ends[0]
         stack_affinity(
-            pl.ds(base, STACK), base, lambda g: acc[base + g], add, planes, outer, lines, head, head_bias, scr, kept, x0
+            slice(base, base + STACK), base, lambda g: acc[base + g], add, planes, outer, lines, head, head_bias, scr, kept, x0
         )
-        all_lines = pl.ds(x0, 4 * STACK)
+        all_lines = slice(x0, x0 + 4 * STACK)
         for i in range(6):
             affinity[i // 2, i % 2, all_lines, :] = kept[i, all_lines, :].astype(BF)
-        first = jnp.where(s > 0, 0.0, -128.0)
-        low, high = stack_table(x0, x0, first, plain, y_code, z_code, kept, own_hot, pair_hot)
-        return total[0] + low, total[1] + high
-
-    low, high = lax.fori_loop(0, HEAD_STACKS, body, (jnp.zeros((F, 3 * F), F32), jnp.zeros((F, 2 * F), F32)))
+
+    def table(s):
+        x0 = 4 * STACK * s
+        return stack_table(x0, x0, 0.0 if s else -128.0, plain, y_code, z_code, kept, own_hot, pair_hot)
+
+    affinities(0)
+    low, high = jnp.zeros((F, 3 * F), F32), jnp.zeros((F, 2 * F), F32)
+    for s in range(HEAD_STACKS):
+        if s + 1 < HEAD_STACKS:
+            affinities(s + 1)
+        more = table(s)
+        low, high = low + more[0], high + more[1]
     low_out[...] = low
     high_out[...] = high
     kept_y[...] = kept[4:6]
@@ -641,30 +677,19 @@
         flags += [at[axis], size[axis] - 1 - at[axis], at[axis] % 2]
     flags = jnp.stack(flags + [edge_count[0]]).astype(jnp.int32)
 
-    xt_low, xt_high, z_one, z_two, end_one, end_two, x_one, x_two, edge, first_col = pl.pallas_call(
+    xt_low, xt_high, z_one, z_two, end_one, end_two = pl.pallas_call(
         layout_kernel,
-        out_shape=(
-            shape((LANES, WIDE), BF),
-            shape((LANES, WIDE), BF),
-            shape((LANES, HEAD + LANES), BF),
-            shape((LANES, HEAD + LANES), BF),
-            shape((LANES, WIDE - HEAD), BF),
-            shape((LANES, WIDE - HEAD), BF),
-            shape((2 * LANES + 16, LANES), BF),
-            shape((2 * LANES + 16, LANES), BF),
-            shape((4, EDGE, LANES), BF),
-            shape((2, LANES), F32),
-        ),
-        in_specs=[SMEM, VMEM, VMEM],
-        out_specs=(VMEM,) * 10,
-        scratch_shapes=[pltpu.VMEM((4, EDGE, LANES), F32)],
+        out_shape=(shape((LANES, WIDE), BF),) * 2
+        + (shape((LANES, HEAD), BF),) * 2
+        + (shape((LANES, WIDE - HEAD), BF),) * 2,
+        in_specs=[SMEM, pl.BlockSpec(memory_space=pltpu.HBM)],
+        out_specs=(VMEM,) * 6,
+        scratch_shapes=[pltpu.VMEM(features.shape, BF), pltpu.SemaphoreType.DMA((8,))],
         compiler_params=pltpu.CompilerParams(vmem_limit_bytes=28 << 20),
-        cost_estimate=pl.CostEstimate(flops=1_000_000, bytes_accessed=1 << 20, transcendentals=0),
+        cost_estimate=pl.CostEstimate(flops=1_000_000, bytes_accessed=1 << 17, transcendentals=0),
         name="layout",
-    )(flags, features, fragments)
+    )(flags, pltpu.with_memory_space_constraint(features, pltpu.HBM))
     plane_one, plane_two = swap(z_one, z_two, "gz", False)
-    x_got = swap(x_one, x_two, "gx", True)
-
     acc, inner, outer = call(
         own_kernel,
         "own_planes",
@@ -672,22 +697,42 @@
         (xt_low, xt_high, conv_weight, conv_bias.reshape(1, -1)),
         0,
         [pltpu.VMEM((27, 32, LANES), BF), pltpu.VMEM((STEP * STACK + 8, 768), F32)],
-        flops=5_000_000_000,
-    )
+        flops=300_000_000,
+    )
+    x_one, x_two, edge, first_col = call(
+        face_kernel,
+        "faces",
+        (
+            shape((2 * LANES + 16, LANES), BF),
+            shape((2 * LANES + 16, LANES), BF),
+            shape((4, EDGE, LANES), BF),
+            shape((2, LANES), F32),
+        ),
+        (xt_low, xt_high, fragments, flags),
+        1,
+        [pltpu.VMEM((4, EDGE, LANES), F32)],
+    )
+    x_got = swap(x_one, x_two, "gx", True)
+
     owner = edge_owner.reshape(1, slots)
-    rank_hot, column_hot, group, name_hot = call(
-        slots_kernel,
-        "slots",
+    rank_hot, column_hot, group, name_hot, own_counts, plain, y_code = call(
+        ahead_kernel,
+        "ahead",
         (
             shape((2, LANES, slots), BF),
             shape((4 * F, 2 * slots), BF),
             shape((devices, LANES), jnp.int32),
             shape((LANES, devices * LANES), BF),
+            shape((F, F), F32),
+            shape((2, LANES, LANES), F32),
+            shape((2, LANES, LANES), F32),
         ),
-        (edge_cells, owner, recv_slot),
+        (edge_cells, owner, recv_slot, fragments),
         0,
-        [pltpu.VMEM((devices, LANES), jnp.int32)],
-    )
+        [pltpu.VMEM((devices, LANES), jnp.int32), pltpu.VMEM((2, F, 4096), F8), pltpu.VMEM((2, F, 4096), F8)],
+        flops=75_000_000,
+    )
+    *x_got, group = lax.optimization_barrier((*x_got, group))
     face, x_code, y_one, y_two = call(
         x_face_kernel,
         "x_face",
@@ -700,32 +745,25 @@
         (*x_got, edge, flags),
         1,
     )
+    *y_got, outer = lax.optimization_barrier((*swap(y_one, y_two, "gy", True), outer))
     y_low, y_high, ring_one, ring_two = call(
         ring_kernel,
         "ring",
-        (shape((2, EDGE, LANES), BF),) * 2 + (shape((LANES + 2 * EDGE, LANES), BF),) * 2,
-        (face, *swap(y_one, y_two, "gy", True), flags),
+        (shape((2, EDGE, LANES), BF),) * 2 + (shape((RING + LANES, LANES), BF),) * 2,
+        (face, *y_got, fragments, flags),
         1,
     )
-    ring_one, ring_two = swap(ring_one, ring_two, "gz", True)
-
-    lines, ends = call(
+    ring_one, ring_two = swap(ring_one, ring_two, "gz", False)
+
+    lines, ends, counts = call(
         edge_kernel,
         "edges",
-        (shape((2, GROUPS, 256), F32), shape((2, LANES, 256), F32)),
-        (face, y_low, y_high, inner),
-        0,
-        flops=500_000_000,
-    )
-    counts, plain, y_code = call(
-        count_kernel,
-        "pair_counts",
-        (shape((F, 4 * F), F32), shape((2, LANES, LANES), F32), shape((2, LANES, LANES), F32)),
-        (fragments, x_code, y_low, first_col, flags),
+        (shape((2, GROUPS, 256), F32), shape((2, LANES, 256), F32), shape((F, 4 * F), F32)),
+        (face, y_low, y_high, inner, plain, x_code, first_col, own_counts, flags),
         1,
-        [pltpu.VMEM((2, F, 4096), F8), pltpu.VMEM((2, F, 4096), F8)],
-        flops=4_000_000_000,
-    )
+        flops=50_000_000,
+    )
+
     end_one, end_two, counts = lax.optimization_barrier((end_one, end_two, counts))
     end_one, end_two = swap(end_one, end_two, "gz", False)
 

time: 60.9 us -> 55.8 us (0.916)
  waiting for transfers between devices: 6.48 us -> 0.04 us
  local copies, waits for them, and re-layouts: 2.62 us -> 0.13 us
  blocking collectives: 11.8 us -> 13.2 us
  starting transfers between devices: 13 us -> 14.2 us
  Pallas kernels: 25.3 us -> 26.4 us
    ppermute x8, waiting for transfers between devices: 6.48 us -> 0.02 us  [swap(): lax.ppermute(value, axis, [pair for a, b in pairs for pair in ((a, b), (b...]
    ppermute x8, starting transfers between devices: 10 us -> 12.8 us  [swap(): lax.ppermute(value, axis, [pair for a, b in pairs for pair in ((a, b), (b...]
    unnamed x20 -> x16, local copies, waits for them, and re-layouts: 2.53 us -> 0.04 us
    ppermute x1, starting transfers between devices: 2.94 us -> 1.49 us  [swap(): got = lax.ppermute(one, axis, [(0, 1), (1, 0)])]
    all_to_all x1, blocking collectives: 11.8 us -> 13.2 us  [shards(): lax.all_to_all(outgoing, axes, split_axis=0, concat_axis=0, tiled=True)]
  transfers between devices with their start and end apart: 9 -> 9, of which waited for: 2 -> 0; matrix products, arithmetic and copies ran while one was open for 0% -> 0% of each run, Pallas kernels for 29% -> 32%
where the time goes in v5:
time: 55.8 us; the launch traced here: 55.6 us
  Pallas kernels  26.4 us (47%)
  starting transfers between devices  14.2 us (25%)
  blocking collectives  13.2 us (24%)
  between operations  1.56 us (3%)
    pallas_call x9, Pallas kernels, call(): pl.pallas_call(kernel, out_shape=out_shape, in_specs=[VMEM] * (len(args)...  23.5 us
    all_to_all x1, blocking collectives, shards(): lax.all_to_all(outgoing, axes, split_axis=0, concat_axis=0, tiled=True)  13.2 us
    ppermute x8, starting transfers between devices, swap(): lax.ppermute(value, axis, [pair for a, b in pairs for pair in ((a, b), (b...  12.8 us
    pallas_call x1, Pallas kernels, shards(): pl.pallas_call(layout_kernel, out_shape=(shape((LANES, WIDE), BF),) * 2 +...  2.87 us
    ppermute x1, starting transfers between devices, swap(): got = lax.ppermute(one, axis, [(0, 1), (1, 0)])  1.49 us
  transfers between devices with their start and end apart: 9, of which 0 were waited for; matrix products, arithmetic and copies ran while one was open for 0% of the time, Pallas kernels for 32%

profile of v5, /device:TPU:0, one launch (start us, length us, event | category | flops | bytes accessed | tf_op | source)
XLA Modules:
  0.0 55.6 jit_solution(15410839893885067690)
XLA Ops:
  1.3 0.1 stack.39.flags
  1.4 0.0 copy-start.4
  1.4 0.0 copy-start.5
  1.5 0.0 copy-start.1
  1.5 0.0 copy-start.2
  1.5 2.9 %layout.1 = (bf16[128,4224]{1,0:T(8,128)(2,1)S(1)}, bf16[128,4224]{1,0:T(8,128)(2,1)S(1)}, bf16[128,3200]{1,0:T(8,128)(2,1)S(1)}, bf16[128,3200]{1,0:T(8,128)(2,...) custom-call(s32[10]{0:T(128)S(1)} %stack.39.flags, bf16[32,2,128,128]{3,2,1,0:T(8,128)(2,1)} %feat_hbm.1), custom_call_target="tpu_custom_call" | custom-call | flops 1000000 | bytes 131072 | tf_op jit(solution)/shard_map/layout/pallas_call | solution.py:680
  4.4 3.1 %collective-permute-start.5 = (bf16[128,3200]{1,0:T(8,128)(2,1)S(1)}, bf16[128,3200]{1,0:T(8,128)(2,1)S(1)}, u32[]{:S(2)}, u32[]{:S(2)}) collective-permute-start(bf16[128,3200]{1,0:T(8,128)(2,1)S(1)} %get-tuple-element.81), channel_id=1, source_target_pairs={{0,1},{1,0},{2,3},{3,2},{4,5},{5,4},{6,7},{7,6},{8,9},{9,8},{10,11... | collective-permute-start | bytes 2457608 | tf_op jit(solution)/shard_map/ppermute | solution.py:651
  7.5 0.7 %collective-permute-start.6 = (bf16[128,3200]{1,0:T(8,128)(2,1)S(1)}, bf16[128,3200]{1,0:T(8,128)(2,1)S(1)}, u32[]{:S(2)}, u32[]{:S(2)}) collective-permute-start(bf16[128,3200]{1,0:T(8,128)(2,1)S(1)} %get-tuple-element.82), channel_id=1, source_target_pairs={{1,2},{2,1},{5,6},{6,5},{9,10},{10,9},{13,14},{14,13},{17,18},{18,... | collective-permute-start | bytes 2457608 | tf_op jit(solution)/shard_map/ppermute | solution.py:651
  8.2 1.3 %faces.1 = (bf16[272,128]{1,0:T(8,128)(2,1)S(1)}, bf16[272,128]{1,0:T(8,128)(2,1)}, bf16[4,48,128]{2,1,0:T(8,128)(2,1)S(1)}, f32[2,128]{1,0:T(2,128)S(1)}) custom-call(bf16[128,4224]{1,0:T(8,128)(2,1)S(1)} %get-tuple-element.51.low, bf16[128,4224]{1,0:T(8,128)(2,1)S(1)} %get-tuple-element.52.high, s32[2,128,128]{2,1,0:T(8,128)S(1)} %copy-done, ...), custom_call_target="tpu_custom_call" | custom-call | flops 1000000 | bytes 131072 | tf_op jit(solution)/shard_map/faces/pallas_call | solution.py:29
  9.4 1.5 %collective-permute-start = (bf16[272,128]{1,0:T(8,128)(2,1)S(1)}, bf16[272,128]{1,0:T(8,128)(2,1)S(1)}, u32[]{:S(2)}, u32[]{:S(2)}) collective-permute-start(bf16[272,128]{1,0:T(8,128)(2,1)S(1)} %get-tuple-element.56), channel_id=1, source_target_pairs={{0,16},{16,0},{1,17},{17,1},{2,18},{18,2},{3,19},{19,3},{4,20},{20... | collective-permute-start | bytes 208904 | tf_op jit(solution)/shard_map/ppermute | solution.py:646
  10.9 0.0 copy-start.7
  11.0 2.8 %ahead.1 = (bf16[2,128,1024]{2,1,0:T(8,128)(2,1)S(1)}, bf16[256,2048]{1,0:T(8,128)(2,1)S(1)}, s32[32,128]{1,0:T(8,128)S(1)}, bf16[128,4096]{1,0:T(8,128)(2,1)S(1...) custom-call(s32[2,1024]{1,0:T(2,128)S(1)} %copy-done.3, s32[1,1024]{1,0:T(1,128)S(1)} %bitcast.12, ...), custom_call_target="tpu_custom_call" | custom-call | flops 75000000 | bytes 131072 | tf_op jit(solution)/shard_map/ahead/pallas_call | solution.py:29
  13.7 0.0 collective-permute-done.got_one.got_two
  13.7 0.6 %x_face.1 = (bf16[2,128,128]{2,1,0:T(8,128)(2,1)S(1)}, f32[2,1,128]{2,1,0:T(1,128)S(1)}, bf16[2,48,128]{2,1,0:T(8,128)(2,1)S(1)}, bf16[2,48,128]{2,1,0:T(8,128)(2,1)S(1)}) custom-call(bf16[272,128]{1,0:T(8,128)(2,1)S(1)} %collective-permute-done.got_one.got_two, bf16[272,128]{1,0:T(8,128)(2,1)S(1)} %collective-permute-done.got_one.got_two, ...), custom_call_target="tpu_custom_call" | custom-call | flops 1000000 | bytes 131072 | tf_op jit(solution)/shard_map/x_face/pallas_call | solution.py:29
  14.3 0.1 collective-permute-start.1
  14.4 1.6 %collective-permute-start.2 = (bf16[2,48,128]{2,1,0:T(8,128)(2,1)S(1)}, bf16[2,48,128]{2,1,0:T(8,128)(2,1)S(1)}, u32[]{:S(2)}, u32[]{:S(2)}) collective-permute-start(bf16[2,48,128]{2,1,0:T(8,128)(2,1)S(1)} %get-tuple-element.63), channel_id=1, source_target_pairs={{4,8},{8,4},{0,12},{12,0},{5,9},{9,5},{1,13},{13,1},{6,10},{10,6},... | collective-permute-start | bytes 73736 | tf_op jit(solution)/shard_map/ppermute | solution.py:651
  16.0 4.6 %own_planes.1 = (f32[32,128,256]{2,1,0:T(8,128)S(1)}, bf16[3,512,256]{2,1,0:T(8,128)(2,1)S(1)}, bf16[2,256,384]{2,1,0:T(8,128)(2,1)S(1)}) custom-call(bf16[128,4224]{1,0:T(8,128)(2,1)S(1)} %get-tuple-element.51.low, bf16[128,4224]{1,0:T(8,128)(2,1)S(1)} %get-tuple-element.52.high, bf16[27,32,32]{2,1,0:T(8,128)(2,1)S(1)} %copy-done.1, f32[1,32]{1,0:T(1,128)S(1)} %bitcast.11), custom_call_target="tpu_custom_call" | custom-call | flops 300000000 | bytes 131072 | tf_op jit(solution)/shard_map/own_planes/pallas_call | solution.py:29
  20.7 0.0 collective-permute-done.1.got_one
  20.7 0.0 collective-permute-done.2.got_two
  20.7 0.6 %ring.1 = (bf16[2,48,128]{2,1,0:T(8,128)(2,1)S(1)}, bf16[2,48,128]{2,1,0:T(8,128)(2,1)S(1)}, bf16[352,128]{1,0:T(8,128)(2,1)S(1)}, bf16[352,128]{1,0:T(8,128)(2,1)S(1)}) custom-call(bf16[2,128,128]{2,1,0:T(8,128)(2,1)S(1)} %get-tuple-element.61.face, bf16[2,48,128]{2,1,0:T(8,128)(2,1)S(1)} %collective-permute-done.1.got_one, ...), custom_call_target="tpu_custom_call" | custom-call | flops 1000000 | bytes 131072 | tf_op jit(solution)/shard_map/ring/pallas_call | solution.py:29
  21.3 4.4 %collective-permute-start.7 = (bf16[352,128]{1,0:T(8,128)(2,1)S(1)}, bf16[352,128]{1,0:T(8,128)(2,1)S(1)}, u32[]{:S(2)}, u32[]{:S(2)}) collective-permute-start(bf16[352,128]{1,0:T(8,128)(2,1)S(1)} %get-tuple-element.83), channel_id=1, source_target_pairs={{0,1},{1,0},{2,3},{3,2},{4,5},{5,4},{6,7},{7,6},{8,9},{9,8},{10,11... | collective-permute-start | bytes 270344 | tf_op jit(solution)/shard_map/ppermute | solution.py:651
  25.7 0.7 %collective-permute-start.8 = (bf16[352,128]{1,0:T(8,128)(2,1)S(1)}, bf16[352,128]{1,0:T(8,128)(2,1)S(1)}, u32[]{:S(2)}, u32[]{:S(2)}) collective-permute-start(bf16[352,128]{1,0:T(8,128)(2,1)S(1)} %get-tuple-element.84), channel_id=1, source_target_pairs={{1,2},{2,1},{5,6},{6,5},{9,10},{10,9},{13,14},{14,13},{17,18},{18,... | collective-permute-start | bytes 270344 | tf_op jit(solution)/shard_map/ppermute | solution.py:651
  26.3 1.0 %edges.1 = (f32[2,32,256]{2,1,0:T(8,128)S(1)}, f32[2,128,256]{2,1,0:T(8,128)S(1)}, f32[64,256]{1,0:T(8,128)S(1)}) custom-call(bf16[2,128,128]{2,1,0:T(8,128)(2,1)S(1)} %get-tuple-element.61.face, bf16[2,48,128]{2,1,0:T(8,128)(2,1)S(1)} %get-tuple-element.67.y_low, bf16[2,48,128]{2,1,0:T(8,128)(2,1)S(1)} %get-tuple-element.68.y_high, ...), custom_call_target="tpu_custom_call" | custom-call | flops 50000000 | bytes 131072 | tf_op jit(solution)/shard_map/edges/pallas_call | solution.py:29
  27.3 1.3 %collective-permute-start.3 = (bf16[128,1024]{1,0:T(8,128)(2,1)S(1)}, bf16[128,1024]{1,0:T(8,128)(2,1)S(1)}, u32[]{:S(2)}, u32[]{:S(2)}) collective-permute-start(bf16[128,1024]{1,0:T(8,128)(2,1)S(1)} %get-tuple-element.75), channel_id=1, source_target_pairs={{0,1},{1,0},{2,3},{3,2},{4,5},{5,4},{6,7},{7,6},{8,9},{9,8},{10,11... | collective-permute-start | bytes 786440 | tf_op jit(solution)/shard_map/ppermute | solution.py:651
  28.7 0.8 %collective-permute-start.4 = (bf16[128,1024]{1,0:T(8,128)(2,1)S(1)}, bf16[128,1024]{1,0:T(8,128)(2,1)S(1)}, u32[]{:S(2)}, u32[]{:S(2)}) collective-permute-start(bf16[128,1024]{1,0:T(8,128)(2,1)S(1)} %get-tuple-element.76), channel_id=1, source_target_pairs={{1,2},{2,1},{5,6},{6,5},{9,10},{10,9},{13,14},{14,13},{17,18},{18,... | collective-permute-start | bytes 786440 | tf_op jit(solution)/shard_map/ppermute | solution.py:651
  29.6 0.0 collective-permute-done.8.ring_two
  29.6 0.0 collective-permute-done.6.plane_two
  29.6 7.1 %first_lines.1 = (bf16[3,2,96,128]{3,2,1,0:T(8,128)(2,1)S(1)}, f32[2,96,128]{2,1,0:T(8,128)S(1)}, f32[64,192]{1,0:T(8,128)S(1)}, f32[64,128]{1,0:T(8,128)S(1)}, ...) custom-call(f32[32,128,256]{2,1,0:T(8,128)S(1)} %get-tuple-element.5, ...), custom_call_target="tpu_custom_call" | custom-call | flops 6000000000 | bytes 131072 | tf_op jit(solution)/shard_map/first_lines/pallas_call | solution.py:29
  36.8 0.0 collective-permute-done.4.plane_two
  36.8 4.6 %last_lines.1 = (bf16[3,2,128,128]{3,2,1,0:T(8,128)(2,1)}, f32[32,1,128]{2,1,0:T(1,128)S(1)}) custom-call(f32[32,128,256]{2,1,0:T(8,128)S(1)} %get-tuple-element.53.acc, bf16[128,1024]{1,0:T(8,128)(2,1)S(1)} %collective-permute-done.3.plane_one, bf16[128,1024]{1,0:T(8,128)(2,1)S(1)} %collective-permute-done.4.plane_two, ...), custom_call_target="tpu_custom_call" | custom-call | flops 3000000000 | bytes 131072 | tf_op jit(solution)/shard_map/last_lines/pallas_call | solution.py:29
  41.3 13.2 %all_to_all.5.received = f32[32,1,128]{2,1,0:T(1,128)S(1)} all-to-all(f32[32,1,128]{2,1,0:T(1,128)S(1)} %get-tuple-element.97), channel_id=1, replica_groups=mesh['gx'=2,'gy'=4,'gz'=4] {'gx','gy','gz'}, dimensions={0} | all-to-all | bytes 32768 | tf_op jit(solution)/shard_map/all_to_all | solution.py:840
  54.5 1.0 %settle.1 = f32[1,384]{1,0:T(1,128)} custom-call(f32[32,1,128]{2,1,0:T(1,128)S(1)} %all_to_all.5.received, s32[32,128]{1,0:T(8,128)S(1)} %get-tuple-element.98.group_of, bf16[128,4096]{1,0:T(8,128)(2,1)S(1)} %get-tuple-element.99.name_hot), custom_call_target="tpu_custom_call" | custom-call | flops 1000000 | bytes 131072 | tf_op jit(solution)/shard_map/settle/pallas_call | solution.py:29
  (14 shorter events, 0.0 us)
Async XLA Ops:
  0.6 7.5 %copy-start = (s32[2,128,128]{2,1,0:T(8,128)S(1)}, s32[2,128,128]{2,1,0:T(8,128)}, u32[]{:S(2)}) copy-start(s32[2,128,128]{2,1,0:T(8,128)} %frag.5) | copy-start | bytes 393220
  1.4 9.5 %copy-start.3 = (s32[2,1024]{1,0:T(2,128)S(1)}, s32[2,1024]{1,0:T(2,128)}, u32[]{:S(2)}) copy-start(s32[2,1024]{1,0:T(2,128)} %cells.3) | copy-start | bytes 24580
  1.4 9.5 %copy-start.4 = (s32[1,1536]{1,0:T(1,128)S(1)}, s32[1,1536]{1,0:T(1,128)}, u32[]{:S(2)}) copy-start(s32[1,1536]{1,0:T(1,128)} %recv.1) | copy-start | bytes 18436
  1.4 9.5 %copy-start.5 = (s32[1024,1]{0,1:T(1,128)S(1)}, s32[1024,1]{0,1:T(1,128)}, u32[]{:S(2)}) copy-start(s32[1024,1]{0,1:T(1,128)} %param.17) | copy-start | bytes 12292
  1.5 14.6 %copy-start.1 = (bf16[27,32,32]{2,1,0:T(8,128)(2,1)S(1)}, bf16[27,32,32]{2,1,0:T(8,128)(2,1)}, u32[]{:S(2)}) copy-start(bf16[27,32,32]{2,1,0:T(8,128)(2,1)} %conv_weight.1) | copy-start | bytes 165892
  1.5 14.6 %copy-start.2 = (f32[32]{0:T(128)S(1)}, f32[32]{0:T(128)}, u32[]{:S(2)}) copy-start(f32[32]{0:T(128)} %param.12) | copy-start | bytes 388
  4.4 25.2 %collective-permute-start.5 = (bf16[128,3200]{1,0:T(8,128)(2,1)S(1)}, bf16[128,3200]{1,0:T(8,128)(2,1)S(1)}, u32[]{:S(2)}, u32[]{:S(2)}) collective-permute-start(bf16[128,3200]{1,0:T(8,128)(2,1)S(1)} %get-tuple-element.81), channel_id=1, source_target_pairs={{0,1},{1,0},{2,3},{3,2},{4,5},{5,4},{6,7},{7,6},{8,9},{9,8},{10,11... | collective-permute-start | bytes 2457608 | tf_op jit(solution)/shard_map/ppermute | solution.py:651
  7.5 22.1 %collective-permute-start.6 = (bf16[128,3200]{1,0:T(8,128)(2,1)S(1)}, bf16[128,3200]{1,0:T(8,128)(2,1)S(1)}, u32[]{:S(2)}, u32[]{:S(2)}) collective-permute-start(bf16[128,3200]{1,0:T(8,128)(2,1)S(1)} %get-tuple-element.82), channel_id=1, source_target_pairs={{1,2},{2,1},{5,6},{6,5},{9,10},{10,9},{13,14},{14,13},{17,18},{18,... | collective-permute-start | bytes 2457608 | tf_op jit(solution)/shard_map/ppermute | solution.py:651
  9.4 4.3 %collective-permute-start = (bf16[272,128]{1,0:T(8,128)(2,1)S(1)}, bf16[272,128]{1,0:T(8,128)(2,1)S(1)}, u32[]{:S(2)}, u32[]{:S(2)}) collective-permute-start(bf16[272,128]{1,0:T(8,128)(2,1)S(1)} %get-tuple-element.56), channel_id=1, source_target_pairs={{0,16},{16,0},{1,17},{17,1},{2,18},{18,2},{3,19},{19,3},{4,20},{20... | collective-permute-start | bytes 208904 | tf_op jit(solution)/shard_map/ppermute | solution.py:646
  10.9 18.7 %copy-start.6 = (bf16[3,32]{1,0:T(4,128)(2,1)S(1)}, bf16[3,32]{1,0:T(4,128)(2,1)}, u32[]{:S(2)}) copy-start(bf16[3,32]{1,0:T(4,128)(2,1)} %head_weight.3) | copy-start | bytes 580
  10.9 18.7 %copy-start.7 = (f32[3]{0:T(128)S(1)}, f32[3]{0:T(128)}, u32[]{:S(2)}) copy-start(f32[3]{0:T(128)} %head_bias.3) | copy-start | bytes 40
  14.3 6.3 %collective-permute-start.1 = (bf16[2,48,128]{2,1,0:T(8,128)(2,1)S(1)}, bf16[2,48,128]{2,1,0:T(8,128)(2,1)S(1)}, u32[]{:S(2)}, u32[]{:S(2)}) collective-permute-start(bf16[2,48,128]{2,1,0:T(8,128)(2,1)S(1)} %get-tuple-element.62), channel_id=1, source_target_pairs={{0,4},{4,0},{8,12},{12,8},{1,5},{5,1},{9,13},{13,9},{2,6},{6,2},{1... | collective-permute-start | bytes 73736 | tf_op jit(solution)/shard_map/ppermute | solution.py:651
  14.4 6.3 %collective-permute-start.2 = (bf16[2,48,128]{2,1,0:T(8,128)(2,1)S(1)}, bf16[2,48,128]{2,1,0:T(8,128)(2,1)S(1)}, u32[]{:S(2)}, u32[]{:S(2)}) collective-permute-start(bf16[2,48,128]{2,1,0:T(8,128)(2,1)S(1)} %get-tuple-element.63), channel_id=1, source_target_pairs={{4,8},{8,4},{0,12},{12,0},{5,9},{9,5},{1,13},{13,1},{6,10},{10,6},... | collective-permute-start | bytes 73736 | tf_op jit(solution)/shard_map/ppermute | solution.py:651
  21.3 7.4 %collective-permute-start.7 = (bf16[352,128]{1,0:T(8,128)(2,1)S(1)}, bf16[352,128]{1,0:T(8,128)(2,1)S(1)}, u32[]{:S(2)}, u32[]{:S(2)}) collective-permute-start(bf16[352,128]{1,0:T(8,128)(2,1)S(1)} %get-tuple-element.83), channel_id=1, source_target_pairs={{0,1},{1,0},{2,3},{3,2},{4,5},{5,4},{6,7},{7,6},{8,9},{9,8},{10,11... | collective-permute-start | bytes 270344 | tf_op jit(solution)/shard_map/ppermute | solution.py:651
  25.7 3.9 %collective-permute-start.8 = (bf16[352,128]{1,0:T(8,128)(2,1)S(1)}, bf16[352,128]{1,0:T(8,128)(2,1)S(1)}, u32[]{:S(2)}, u32[]{:S(2)}) collective-permute-start(bf16[352,128]{1,0:T(8,128)(2,1)S(1)} %get-tuple-element.84), channel_id=1, source_target_pairs={{1,2},{2,1},{5,6},{6,5},{9,10},{10,9},{13,14},{14,13},{17,18},{18,... | collective-permute-start | bytes 270344 | tf_op jit(solution)/shard_map/ppermute | solution.py:651
  27.3 9.4 %collective-permute-start.3 = (bf16[128,1024]{1,0:T(8,128)(2,1)S(1)}, bf16[128,1024]{1,0:T(8,128)(2,1)S(1)}, u32[]{:S(2)}, u32[]{:S(2)}) collective-permute-start(bf16[128,1024]{1,0:T(8,128)(2,1)S(1)} %get-tuple-element.75), channel_id=1, source_target_pairs={{0,1},{1,0},{2,3},{3,2},{4,5},{5,4},{6,7},{7,6},{8,9},{9,8},{10,11... | collective-permute-start | bytes 786440 | tf_op jit(solution)/shard_map/ppermute | solution.py:651
  28.7 8.1 %collective-permute-start.4 = (bf16[128,1024]{1,0:T(8,128)(2,1)S(1)}, bf16[128,1024]{1,0:T(8,128)(2,1)S(1)}, u32[]{:S(2)}, u32[]{:S(2)}) collective-permute-start(bf16[128,1024]{1,0:T(8,128)(2,1)S(1)} %get-tuple-element.76), channel_id=1, source_target_pairs={{1,2},{2,1},{5,6},{6,5},{9,10},{10,9},{13,14},{14,13},{17,18},{18,... | collective-permute-start | bytes 786440 | tf_op jit(solution)/shard_map/ppermute | solution.py:651

commit v6 on v5

--- a/solution.py
+++ b/solution.py
@@ -14,6 +14,7 @@
 STEP = LANES + 8
 EDGE = 48
 RING = LANES + 2 * EDGE
+PART = 8
 HEAD_STACKS = 3
 HEAD_GROUPS = HEAD_STACKS * STACK
 HEAD = (HEAD_GROUPS + 1) * LANES
@@ -92,13 +93,21 @@
                 end[:, 512 * t + cut - HEAD : 512 * t + wide - HEAD] = value[:, cut:]
 
 
-def face_kernel(low, high, frag, flags, x_one, x_two, edge, first_col, rows):
+def face_kernel(low, high, frag, flags, x_one, x_two):
     odd = flags[X_ODD] > 0
     for z, plane in ((0, low), (1, high)):
         lines = slice(LANES * z, LANES * (z + 1))
         start, end = plane[:, :LANES], plane[:, WIDE - LANES :]
         x_one[lines, :] = jnp.where(odd, start, end)
         x_two[lines, :] = jnp.where(odd, end, start)
+    lines = [jnp.broadcast_to(frag[z, 127:128, :], (8, LANES)).astype(F32) for z in range(2)]
+    lines = jnp.concatenate(lines, axis=0).astype(BF)
+    for out in (x_one, x_two):
+        out[2 * LANES :, :] = lines
+
+
+def line_kernel(low, high, frag, edge, first_col, rows):
+    for z, plane in ((0, low), (1, high)):
         turned = frag[z].astype(F32).T
         first_col[z : z + 1, :] = turned[0:1]
         for side, line in ((0, plane[112:128, :].astype(F32)[15:16]), (1, plane[0:16, :].astype(F32)[0:1])):
@@ -106,10 +115,6 @@
                 rows[2 * side + z, q : q + 1, :] = line[:, LANES * q : LANES * (q + 1)]
             rows[2 * side + z, TILES:EDGE, :] = jnp.broadcast_to(turned[127:128], (EDGE - TILES, LANES))
             edge[2 * side + z] = rows[2 * side + z].astype(BF)
-    lines = [jnp.broadcast_to(frag[z, 127:128, :], (8, LANES)).astype(F32) for z in range(2)]
-    lines = jnp.concatenate(lines, axis=0).astype(BF)
-    for out in (x_one, x_two):
-        out[2 * LANES :, :] = lines
 
 
 def x_face_kernel(got_one, got_two, edge, flags, face, x_code, y_one, y_two):
@@ -349,6 +354,8 @@
     owner,
     recv,
     frag,
+    low,
+    high,
     rank_hot,
     column_hot,
     group,
@@ -356,10 +363,14 @@
     counts,
     plain,
     y_code,
+    edge,
+    first_col,
     place,
     own_hot,
     pair_hot,
+    rows,
 ):
+    line_kernel(low, high, frag, edge, first_col, rows)
     count_kernel(frag, counts, plain, y_code, own_hot, pair_hot)
     slots_kernel(cells, owner, recv, rank_hot, column_hot, group, name_hot, place)
 
@@ -415,27 +426,36 @@
             kept[i, kept_at + 8 * pair : kept_at + 8 * pair + 8, :] = value
 
 
-def stack_table(x0, kept_at, first, plain, y_code, z_code, kept, own_hot, pair_hot):
+def table_pieces(x0, kept_at, plain, y_code, z_code, kept, lines):
     names, one, none = numbers(F), jnp.ones((F, LANES), BF), jnp.zeros((F, LANES), BF)
-    hot_before = None
-    for j in range(32):
-        t, x = j // 16, x0 + j
-        spot = slice(LANES * (j % 16), LANES * (j % 16 + 1))
-        weight = [spread(kept[i, pl.ds(kept_at + j, 1), :], 4) for i in range(6)]
-        hot, x_hot, y_hot = line_partners(plain, y_code, x, first, hot_before)
-        hot_before = hot
-        for z in range(2):
-            own_hot[t, z, :, spot] = jnp.where(hot[z], one, none)
-            pair_hot[t, z, 0:F, spot] = jnp.where(x_hot[z], weight[2 + z], none) + jnp.where(
-                y_hot[z], weight[4 + z], none
-            )
-        pair_hot[t, 1, F : 2 * F, spot] = jnp.where(hot[0], weight[1], none)
-        z_hot = spread(z_code[pl.ds(x, 1), :], 4) == names
-        pair_hot[t, 0, F : 2 * F, spot] = jnp.where(z_hot, weight[0], none)
-        pair_hot[t, 0, 2 * F :, spot] = jnp.where(z_hot, one, none)
-    low = outer_product(own_hot[0, 0], pair_hot[0, 0]) + outer_product(own_hot[1, 0], pair_hot[1, 0])
-    high = outer_product(own_hot[0, 1], pair_hot[0, 1, : 2 * F]) + outer_product(own_hot[1, 1], pair_hot[1, 1, : 2 * F])
-    return low, high
+    low, high = jnp.zeros((3 * F, F), F32), jnp.zeros((2 * F, F), F32)
+    def one_hot(row):
+        return jnp.where(spread(row, 4) == names, one, none)
+
+    before = None
+    for t in range(lines // PART):
+        own_rows, pair_rows = [[], []], [[], []]
+        for j in range(PART):
+            at = PART * t + j
+            x = x0 + at
+            line = slice(x, x + 1)
+            weight = [spread(kept[i, kept_at + at : kept_at + at + 1, :], 4) for i in range(6)]
+            hot = [one_hot(plain[z, line, :]) for z in range(2)]
+            if before is None:
+                before = [one_hot(plain[z, x - 1 : x, :]) if x > 0 else none for z in range(2)]
+            z_hot = one_hot(z_code[line, :])
+            for z in range(2):
+                own_rows[z].append(hot[z])
+                pair = [before[z] * weight[2 + z] + one_hot(y_code[z, line, :]) * weight[4 + z]]
+                pair += [hot[0] * weight[1]] if z else [z_hot * weight[0], z_hot]
+                pair_rows[z].append(jnp.concatenate(pair, axis=0))
+            before = hot
+        parts = [
+            outer_product(jnp.concatenate(pair_rows[z], axis=1), jnp.concatenate(own_rows[z], axis=1))
+            for z in range(2)
+        ]
+        low, high = low + parts[0], high + parts[1]
+    return low.T, high.T
 
 
 def first_kernel(
@@ -464,8 +484,6 @@
     planes,
     scr,
     kept,
-    own_hot,
-    pair_hot,
 ):
     odd = flags[Z_ODD]
     below = jnp.where(odd > 0, ring_one[RING:, :], ring_two[RING:, :])
@@ -495,23 +513,15 @@
         if s == 0:
             add[0] = inner_ends[0]
         stack_affinity(
-            slice(base, base + STACK), base, lambda g: acc[base + g], add, planes, outer, lines, head, head_bias, scr, kept, x0
+            slice(base, base + STACK), base, lambda g: acc[base + g], add, planes, outer, lines, head, head_bias, scr.at[s % 2], kept, x0
         )
         all_lines = slice(x0, x0 + 4 * STACK)
         for i in range(6):
             affinity[i // 2, i % 2, all_lines, :] = kept[i, all_lines, :].astype(BF)
 
-    def table(s):
-        x0 = 4 * STACK * s
-        return stack_table(x0, x0, 0.0 if s else -128.0, plain, y_code, z_code, kept, own_hot, pair_hot)
-
-    affinities(0)
-    low, high = jnp.zeros((F, 3 * F), F32), jnp.zeros((F, 2 * F), F32)
     for s in range(HEAD_STACKS):
-        if s + 1 < HEAD_STACKS:
-            affinities(s + 1)
-        more = table(s)
-        low, high = low + more[0], high + more[1]
+        affinities(s)
+    low, high = table_pieces(0, 0, plain, y_code, z_code, kept, HEAD_LINES)
     low_out[...] = low
     high_out[...] = high
     kept_y[...] = kept[4:6]
@@ -553,8 +563,6 @@
     planes,
     scr,
     kept,
-    own_hot,
-    pair_hot,
 ):
     odd = flags[Z_ODD]
     lane = iota((LANES, LANES), 1)
@@ -568,12 +576,14 @@
     add[-1] = inner_ends[1]
     groups = pl.ds(HEAD_GROUPS, STACK)
     stack_affinity(
-        groups, 0, lambda g: acc[HEAD_GROUPS + g], add, planes, outer, lines, head_rows(head_weight), head_bias, scr, kept, 0
+        groups, 0, lambda g: acc[HEAD_GROUPS + g], add, planes, outer, lines, head_rows(head_weight), head_bias, scr.at[0], kept, 0
     )
     for i in range(6):
         affinity[i // 2, i % 2, :HEAD_LINES, :] = affinity_head[i // 2, i % 2]
         affinity[i // 2, i % 2, HEAD_LINES:, :] = kept[i].astype(BF)
-    low, high = stack_table(HEAD_LINES, 0, 0.0, plain, y_code, z_code, kept, own_hot, pair_hot)
+    low, high = table_pieces(
+        HEAD_LINES, 0, plain, y_code, z_code, kept, LANES - HEAD_LINES
+    )
     low, high = low_head[...] + low, high_head[...] + high
     own = low[:, :F] + high[:, :F] + high[:, F:]
     y_outer = faces_product(
@@ -699,23 +709,20 @@
         [pltpu.VMEM((27, 32, LANES), BF), pltpu.VMEM((STEP * STACK + 8, 768), F32)],
         flops=300_000_000,
     )
-    x_one, x_two, edge, first_col = call(
+    x_one, x_two = call(
         face_kernel,
         "faces",
         (
             shape((2 * LANES + 16, LANES), BF),
             shape((2 * LANES + 16, LANES), BF),
-            shape((4, EDGE, LANES), BF),
-            shape((2, LANES), F32),
         ),
         (xt_low, xt_high, fragments, flags),
         1,
-        [pltpu.VMEM((4, EDGE, LANES), F32)],
     )
     x_got = swap(x_one, x_two, "gx", True)
 
     owner = edge_owner.reshape(1, slots)
-    rank_hot, column_hot, group, name_hot, own_counts, plain, y_code = call(
+    rank_hot, column_hot, group, name_hot, own_counts, plain, y_code, edge, first_col = call(
         ahead_kernel,
         "ahead",
         (
@@ -726,10 +733,17 @@
             shape((F, F), F32),
             shape((2, LANES, LANES), F32),
             shape((2, LANES, LANES), F32),
+            shape((4, EDGE, LANES), BF),
+            shape((2, LANES), F32),
         ),
-        (edge_cells, owner, recv_slot, fragments),
+        (edge_cells, owner, recv_slot, fragments, xt_low, xt_high),
         0,
-        [pltpu.VMEM((devices, LANES), jnp.int32), pltpu.VMEM((2, F, 4096), F8), pltpu.VMEM((2, F, 4096), F8)],
+        [
+            pltpu.VMEM((devices, LANES), jnp.int32),
+            pltpu.VMEM((2, F, 4096), F8),
+            pltpu.VMEM((2, F, 4096), F8),
+            pltpu.VMEM((4, EDGE, LANES), F32),
+        ],
         flops=75_000_000,
     )
     *x_got, group = lax.optimization_barrier((*x_got, group))
@@ -770,10 +784,8 @@
     def stack_scratch(tiles, kept_lines):
         return [
             pltpu.VMEM((2, LANES, tiles * LANES), BF),
-            pltpu.VMEM((2, STEP * STACK + 8, 3 * LANES), F32),
+            pltpu.VMEM((min(2, kept_lines // 32), 2, STEP * STACK + 8, 3 * LANES), F32),
             pltpu.VMEM((6, kept_lines, LANES), F32),
-            pltpu.VMEM((2, 2, F, 2048), BF),
-            pltpu.VMEM((2, 2, 3 * F, 2048), BF),
         ]
 
     done = call(

time: 55.8 us -> 54.4 us (0.975)
  Pallas kernels: 26.4 us -> 25 us
    pallas_call x9, Pallas kernels: 23.5 us -> 22.1 us  [call(): pl.pallas_call(kernel, out_shape=out_shape, in_specs=[VMEM] * (len(args)...]
  transfers between devices with their start and end apart: 9 -> 9, of which waited for: 0 -> 0; matrix products, arithmetic and copies ran while one was open for 0% -> 0% of each run, Pallas kernels for 32% -> 31%
where the time goes in v6:
time: 54.4 us; the launch traced here: 54.2 us
  Pallas kernels  25 us (46%)
  starting transfers between devices  14.2 us (26%)
  blocking collectives  13.2 us (24%)
  between operations  1.57 us (3%)
    pallas_call x9, Pallas kernels, call(): pl.pallas_call(kernel, out_shape=out_shape, in_specs=[VMEM] * (len(args)...  22.1 us
    all_to_all x1, blocking collectives, shards(): lax.all_to_all(outgoing, axes, split_axis=0, concat_axis=0, tiled=True)  13.2 us
    ppermute x8, starting transfers between devices, swap(): lax.ppermute(value, axis, [pair for a, b in pairs for pair in ((a, b), (b...  12.8 us
    pallas_call x1, Pallas kernels, shards(): pl.pallas_call(layout_kernel, out_shape=(shape((LANES, WIDE), BF),) * 2 +...  2.87 us
    ppermute x1, starting transfers between devices, swap(): got = lax.ppermute(one, axis, [(0, 1), (1, 0)])  1.49 us
  transfers between devices with their start and end apart: 9, of which 0 were waited for; matrix products, arithmetic and copies ran while one was open for 0% of the time, Pallas kernels for 31%

profile of v6, /device:TPU:0, one launch (start us, length us, event | category | flops | bytes accessed | tf_op | source)
XLA Modules:
  0.0 54.2 jit_solution(9351245243326208712)
XLA Ops:
  1.3 0.1 stack.39.flags
  1.4 0.0 copy-start.3
  1.4 0.0 copy-start.4
  1.5 2.9 %layout.1 = (bf16[128,4224]{1,0:T(8,128)(2,1)S(1)}, bf16[128,4224]{1,0:T(8,128)(2,1)S(1)}, bf16[128,3200]{1,0:T(8,128)(2,1)S(1)}, bf16[128,3200]{1,0:T(8,128)(2,...) custom-call(s32[10]{0:T(128)S(1)} %stack.39.flags, bf16[32,2,128,128]{3,2,1,0:T(8,128)(2,1)} %feat_hbm.1), custom_call_target="tpu_custom_call" | custom-call | flops 1000000 | bytes 131072 | tf_op jit(solution)/shard_map/layout/pallas_call | solution.py:690
  4.3 3.1 %collective-permute-start.5 = (bf16[128,3200]{1,0:T(8,128)(2,1)S(1)}, bf16[128,3200]{1,0:T(8,128)(2,1)S(1)}, u32[]{:S(2)}, u32[]{:S(2)}) collective-permute-start(bf16[128,3200]{1,0:T(8,128)(2,1)S(1)} %get-tuple-element.81), channel_id=1, source_target_pairs={{0,1},{1,0},{2,3},{3,2},{4,5},{5,4},{6,7},{7,6},{8,9},{9,8},{10,11... | collective-permute-start | bytes 2457608 | tf_op jit(solution)/shard_map/ppermute | solution.py:661
  7.4 0.7 %collective-permute-start.6 = (bf16[128,3200]{1,0:T(8,128)(2,1)S(1)}, bf16[128,3200]{1,0:T(8,128)(2,1)S(1)}, u32[]{:S(2)}, u32[]{:S(2)}) collective-permute-start(bf16[128,3200]{1,0:T(8,128)(2,1)S(1)} %get-tuple-element.82), channel_id=1, source_target_pairs={{1,2},{2,1},{5,6},{6,5},{9,10},{10,9},{13,14},{14,13},{17,18},{18,... | collective-permute-start | bytes 2457608 | tf_op jit(solution)/shard_map/ppermute | solution.py:661
  8.2 0.0 copy-start.1
  8.2 0.0 copy-start.5
  8.2 1.2 %faces.1 = (bf16[272,128]{1,0:T(8,128)(2,1)S(1)}, bf16[272,128]{1,0:T(8,128)(2,1)}) custom-call(bf16[128,4224]{1,0:T(8,128)(2,1)S(1)} %get-tuple-element.51.low, bf16[128,4224]{1,0:T(8,128)(2,1)S(1)} %get-tuple-element.52.high, s32[2,128,128]{2,1,0:T(8,128)S(1)} %copy-done, s32[10]{0:T(128)S(1)} %stack.39.flags), custom_call_target="tpu_custom_call" | custom-call | flops 1000000 | bytes 131072 | tf_op jit(solution)/shard_map/faces/pallas_call | solution.py:30
  9.4 1.5 %collective-permute-start = (bf16[272,128]{1,0:T(8,128)(2,1)S(1)}, bf16[272,128]{1,0:T(8,128)(2,1)S(1)}, u32[]{:S(2)}, u32[]{:S(2)}) collective-permute-start(bf16[272,128]{1,0:T(8,128)(2,1)S(1)} %get-tuple-element.56), channel_id=1, source_target_pairs={{0,16},{16,0},{1,17},{17,1},{2,18},{18,2},{3,19},{19,3},{4,20},{20... | collective-permute-start | bytes 208904 | tf_op jit(solution)/shard_map/ppermute | solution.py:656
  10.9 2.8 %ahead.1 = (bf16[2,128,1024]{2,1,0:T(8,128)(2,1)S(1)}, bf16[256,2048]{1,0:T(8,128)(2,1)S(1)}, s32[32,128]{1,0:T(8,128)S(1)}, bf16[128,4096]{1,0:T(8,128)(2,1)S(1...) custom-call(s32[2,1024]{1,0:T(2,128)S(1)} %copy-done.2, ...), custom_call_target="tpu_custom_call" | custom-call | flops 75000000 | bytes 131072 | tf_op jit(solution)/shard_map/ahead/pallas_call | solution.py:30
  13.7 0.0 copy-start.6
  13.7 0.0 copy-start.7
  13.7 0.6 %x_face.1 = (bf16[2,128,128]{2,1,0:T(8,128)(2,1)S(1)}, f32[2,1,128]{2,1,0:T(1,128)S(1)}, bf16[2,48,128]{2,1,0:T(8,128)(2,1)S(1)}, bf16[2,48,128]{2,1,0:T(8,128)(2,1)S(1)}) custom-call(bf16[272,128]{1,0:T(8,128)(2,1)S(1)} %collective-permute-done.got_one.got_two, bf16[272,128]{1,0:T(8,128)(2,1)S(1)} %collective-permute-done.got_one.got_two, ...), custom_call_target="tpu_custom_call" | custom-call | flops 1000000 | bytes 131072 | tf_op jit(solution)/shard_map/x_face/pallas_call | solution.py:30
  14.3 0.1 collective-permute-start.1
  14.4 1.6 %collective-permute-start.2 = (bf16[2,48,128]{2,1,0:T(8,128)(2,1)S(1)}, bf16[2,48,128]{2,1,0:T(8,128)(2,1)S(1)}, u32[]{:S(2)}, u32[]{:S(2)}) collective-permute-start(bf16[2,48,128]{2,1,0:T(8,128)(2,1)S(1)} %get-tuple-element.63), channel_id=1, source_target_pairs={{4,8},{8,4},{0,12},{12,0},{5,9},{9,5},{1,13},{13,1},{6,10},{10,6},... | collective-permute-start | bytes 73736 | tf_op jit(solution)/shard_map/ppermute | solution.py:661
  16.0 4.6 %own_planes.1 = (f32[32,128,256]{2,1,0:T(8,128)S(1)}, bf16[3,512,256]{2,1,0:T(8,128)(2,1)S(1)}, bf16[2,256,384]{2,1,0:T(8,128)(2,1)S(1)}) custom-call(bf16[128,4224]{1,0:T(8,128)(2,1)S(1)} %get-tuple-element.51.low, bf16[128,4224]{1,0:T(8,128)(2,1)S(1)} %get-tuple-element.52.high, bf16[27,32,32]{2,1,0:T(8,128)(2,1)S(1)} %copy-done.1, f32[1,32]{1,0:T(1,128)S(1)} %bitcast.13), custom_call_target="tpu_custom_call" | custom-call | flops 300000000 | bytes 131072 | tf_op jit(solution)/shard_map/own_planes/pallas_call | solution.py:30
  20.7 0.0 collective-permute-done.2.got_two
  20.7 0.6 %ring.1 = (bf16[2,48,128]{2,1,0:T(8,128)(2,1)S(1)}, bf16[2,48,128]{2,1,0:T(8,128)(2,1)S(1)}, bf16[352,128]{1,0:T(8,128)(2,1)S(1)}, bf16[352,128]{1,0:T(8,128)(2,1)S(1)}) custom-call(bf16[2,128,128]{2,1,0:T(8,128)(2,1)S(1)} %get-tuple-element.61.face, bf16[2,48,128]{2,1,0:T(8,128)(2,1)S(1)} %collective-permute-done.1.got_one, ...), custom_call_target="tpu_custom_call" | custom-call | flops 1000000 | bytes 131072 | tf_op jit(solution)/shard_map/ring/pallas_call | solution.py:30
  21.3 4.4 %collective-permute-start.7 = (bf16[352,128]{1,0:T(8,128)(2,1)S(1)}, bf16[352,128]{1,0:T(8,128)(2,1)S(1)}, u32[]{:S(2)}, u32[]{:S(2)}) collective-permute-start(bf16[352,128]{1,0:T(8,128)(2,1)S(1)} %get-tuple-element.83), channel_id=1, source_target_pairs={{0,1},{1,0},{2,3},{3,2},{4,5},{5,4},{6,7},{7,6},{8,9},{9,8},{10,11... | collective-permute-start | bytes 270344 | tf_op jit(solution)/shard_map/ppermute | solution.py:661
  25.7 0.7 %collective-permute-start.8 = (bf16[352,128]{1,0:T(8,128)(2,1)S(1)}, bf16[352,128]{1,0:T(8,128)(2,1)S(1)}, u32[]{:S(2)}, u32[]{:S(2)}) collective-permute-start(bf16[352,128]{1,0:T(8,128)(2,1)S(1)} %get-tuple-element.84), channel_id=1, source_target_pairs={{1,2},{2,1},{5,6},{6,5},{9,10},{10,9},{13,14},{14,13},{17,18},{18,... | collective-permute-start | bytes 270344 | tf_op jit(solution)/shard_map/ppermute | solution.py:661
  26.3 1.0 %edges.1 = (f32[2,32,256]{2,1,0:T(8,128)S(1)}, f32[2,128,256]{2,1,0:T(8,128)S(1)}, f32[64,256]{1,0:T(8,128)S(1)}) custom-call(bf16[2,128,128]{2,1,0:T(8,128)(2,1)S(1)} %get-tuple-element.61.face, bf16[2,48,128]{2,1,0:T(8,128)(2,1)S(1)} %get-tuple-element.67.y_low, bf16[2,48,128]{2,1,0:T(8,128)(2,1)S(1)} %get-tuple-element.68.y_high, ...), custom_call_target="tpu_custom_call" | custom-call | flops 50000000 | bytes 131072 | tf_op jit(solution)/shard_map/edges/pallas_call | solution.py:30
  27.3 1.3 %collective-permute-start.3 = (bf16[128,1024]{1,0:T(8,128)(2,1)S(1)}, bf16[128,1024]{1,0:T(8,128)(2,1)S(1)}, u32[]{:S(2)}, u32[]{:S(2)}) collective-permute-start(bf16[128,1024]{1,0:T(8,128)(2,1)S(1)} %get-tuple-element.75), channel_id=1, source_target_pairs={{0,1},{1,0},{2,3},{3,2},{4,5},{5,4},{6,7},{7,6},{8,9},{9,8},{10,11... | collective-permute-start | bytes 786440 | tf_op jit(solution)/shard_map/ppermute | solution.py:661
  28.7 0.0 collective-permute-done.7.ring_one
  28.7 0.8 %collective-permute-start.4 = (bf16[128,1024]{1,0:T(8,128)(2,1)S(1)}, bf16[128,1024]{1,0:T(8,128)(2,1)S(1)}, u32[]{:S(2)}, u32[]{:S(2)}) collective-permute-start(bf16[128,1024]{1,0:T(8,128)(2,1)S(1)} %get-tuple-element.76), channel_id=1, source_target_pairs={{1,2},{2,1},{5,6},{6,5},{9,10},{10,9},{13,14},{14,13},{17,18},{18,... | collective-permute-start | bytes 786440 | tf_op jit(solution)/shard_map/ppermute | solution.py:661
  29.6 0.0 collective-permute-done.5.plane_one
  29.6 0.0 collective-permute-done.6.plane_two
  29.6 6.0 %first_lines.1 = (bf16[3,2,96,128]{3,2,1,0:T(8,128)(2,1)S(1)}, f32[2,96,128]{2,1,0:T(8,128)S(1)}, f32[64,192]{1,0:T(8,128)S(1)}, f32[64,128]{1,0:T(8,128)S(1)}, ...) custom-call(f32[32,128,256]{2,1,0:T(8,128)S(1)} %get-tuple-element.5, ...), custom_call_target="tpu_custom_call" | custom-call | flops 6000000000 | bytes 131072 | tf_op jit(solution)/shard_map/first_lines/pallas_call | solution.py:30
  35.6 0.0 collective-permute-done.3.plane_one
  35.7 4.3 %last_lines.1 = (bf16[3,2,128,128]{3,2,1,0:T(8,128)(2,1)}, f32[32,1,128]{2,1,0:T(1,128)S(1)}) custom-call(f32[32,128,256]{2,1,0:T(8,128)S(1)} %get-tuple-element.53.acc, bf16[128,1024]{1,0:T(8,128)(2,1)S(1)} %collective-permute-done.3.plane_one, bf16[128,1024]{1,0:T(8,128)(2,1)S(1)} %collective-permute-done.4.plane_two, ...), custom_call_target="tpu_custom_call" | custom-call | flops 3000000000 | bytes 131072 | tf_op jit(solution)/shard_map/last_lines/pallas_call | solution.py:30
  39.9 13.2 %all_to_all.5.received = f32[32,1,128]{2,1,0:T(1,128)S(1)} all-to-all(f32[32,1,128]{2,1,0:T(1,128)S(1)} %get-tuple-element.97), channel_id=1, replica_groups=mesh['gx'=2,'gy'=4,'gz'=4] {'gx','gy','gz'}, dimensions={0} | all-to-all | bytes 32768 | tf_op jit(solution)/shard_map/all_to_all | solution.py:852
  53.1 1.0 %settle.1 = f32[1,384]{1,0:T(1,128)} custom-call(f32[32,1,128]{2,1,0:T(1,128)S(1)} %all_to_all.5.received, s32[32,128]{1,0:T(8,128)S(1)} %get-tuple-element.98.group_of, bf16[128,4096]{1,0:T(8,128)(2,1)S(1)} %get-tuple-element.99.name_hot), custom_call_target="tpu_custom_call" | custom-call | flops 1000000 | bytes 131072 | tf_op jit(solution)/shard_map/settle/pallas_call | solution.py:30
  (14 shorter events, 0.0 us)
Async XLA Ops:
  0.6 7.5 %copy-start = (s32[2,128,128]{2,1,0:T(8,128)S(1)}, s32[2,128,128]{2,1,0:T(8,128)}, u32[]{:S(2)}) copy-start(s32[2,128,128]{2,1,0:T(8,128)} %frag.5) | copy-start | bytes 393220
  1.4 9.4 %copy-start.2 = (s32[2,1024]{1,0:T(2,128)S(1)}, s32[2,1024]{1,0:T(2,128)}, u32[]{:S(2)}) copy-start(s32[2,1024]{1,0:T(2,128)} %cells.3) | copy-start | bytes 24580
  1.4 9.4 %copy-start.3 = (s32[1,1536]{1,0:T(1,128)S(1)}, s32[1,1536]{1,0:T(1,128)}, u32[]{:S(2)}) copy-start(s32[1,1536]{1,0:T(1,128)} %recv.1) | copy-start | bytes 18436
  1.4 9.4 %copy-start.4 = (s32[1024,1]{0,1:T(1,128)S(1)}, s32[1024,1]{0,1:T(1,128)}, u32[]{:S(2)}) copy-start(s32[1024,1]{0,1:T(1,128)} %param.17) | copy-start | bytes 12292
  4.3 25.2 %collective-permute-start.5 = (bf16[128,3200]{1,0:T(8,128)(2,1)S(1)}, bf16[128,3200]{1,0:T(8,128)(2,1)S(1)}, u32[]{:S(2)}, u32[]{:S(2)}) collective-permute-start(bf16[128,3200]{1,0:T(8,128)(2,1)S(1)} %get-tuple-element.81), channel_id=1, source_target_pairs={{0,1},{1,0},{2,3},{3,2},{4,5},{5,4},{6,7},{7,6},{8,9},{9,8},{10,11... | collective-permute-start | bytes 2457608 | tf_op jit(solution)/shard_map/ppermute | solution.py:661
  7.4 22.1 %collective-permute-start.6 = (bf16[128,3200]{1,0:T(8,128)(2,1)S(1)}, bf16[128,3200]{1,0:T(8,128)(2,1)S(1)}, u32[]{:S(2)}, u32[]{:S(2)}) collective-permute-start(bf16[128,3200]{1,0:T(8,128)(2,1)S(1)} %get-tuple-element.82), channel_id=1, source_target_pairs={{1,2},{2,1},{5,6},{6,5},{9,10},{10,9},{13,14},{14,13},{17,18},{18,... | collective-permute-start | bytes 2457608 | tf_op jit(solution)/shard_map/ppermute | solution.py:661
  8.2 7.9 %copy-start.1 = (bf16[27,32,32]{2,1,0:T(8,128)(2,1)S(1)}, bf16[27,32,32]{2,1,0:T(8,128)(2,1)}, u32[]{:S(2)}) copy-start(bf16[27,32,32]{2,1,0:T(8,128)(2,1)} %conv_weight.1) | copy-start | bytes 165892
  8.2 7.9 %copy-start.5 = (f32[32]{0:T(128)S(1)}, f32[32]{0:T(128)}, u32[]{:S(2)}) copy-start(f32[32]{0:T(128)} %param.12) | copy-start | bytes 388
  9.4 4.4 %collective-permute-start = (bf16[272,128]{1,0:T(8,128)(2,1)S(1)}, bf16[272,128]{1,0:T(8,128)(2,1)S(1)}, u32[]{:S(2)}, u32[]{:S(2)}) collective-permute-start(bf16[272,128]{1,0:T(8,128)(2,1)S(1)} %get-tuple-element.56), channel_id=1, source_target_pairs={{0,16},{16,0},{1,17},{17,1},{2,18},{18,2},{3,19},{19,3},{4,20},{20... | collective-permute-start | bytes 208904 | tf_op jit(solution)/shard_map/ppermute | solution.py:656
  13.7 15.9 %copy-start.6 = (bf16[3,32]{1,0:T(4,128)(2,1)S(1)}, bf16[3,32]{1,0:T(4,128)(2,1)}, u32[]{:S(2)}) copy-start(bf16[3,32]{1,0:T(4,128)(2,1)} %head_weight.3) | copy-start | bytes 580
  13.7 15.9 %copy-start.7 = (f32[3]{0:T(128)S(1)}, f32[3]{0:T(128)}, u32[]{:S(2)}) copy-start(f32[3]{0:T(128)} %head_bias.3) | copy-start | bytes 40
  14.3 6.3 %collective-permute-start.1 = (bf16[2,48,128]{2,1,0:T(8,128)(2,1)S(1)}, bf16[2,48,128]{2,1,0:T(8,128)(2,1)S(1)}, u32[]{:S(2)}, u32[]{:S(2)}) collective-permute-start(bf16[2,48,128]{2,1,0:T(8,128)(2,1)S(1)} %get-tuple-element.62), channel_id=1, source_target_pairs={{0,4},{4,0},{8,12},{12,8},{1,5},{5,1},{9,13},{13,9},{2,6},{6,2},{1... | collective-permute-start | bytes 73736 | tf_op jit(solution)/shard_map/ppermute | solution.py:661
  14.4 6.3 %collective-permute-start.2 = (bf16[2,48,128]{2,1,0:T(8,128)(2,1)S(1)}, bf16[2,48,128]{2,1,0:T(8,128)(2,1)S(1)}, u32[]{:S(2)}, u32[]{:S(2)}) collective-permute-start(bf16[2,48,128]{2,1,0:T(8,128)(2,1)S(1)} %get-tuple-element.63), channel_id=1, source_target_pairs={{4,8},{8,4},{0,12},{12,0},{5,9},{9,5},{1,13},{13,1},{6,10},{10,6},... | collective-permute-start | bytes 73736 | tf_op jit(solution)/shard_map/ppermute | solution.py:661
  21.3 7.4 %collective-permute-start.7 = (bf16[352,128]{1,0:T(8,128)(2,1)S(1)}, bf16[352,128]{1,0:T(8,128)(2,1)S(1)}, u32[]{:S(2)}, u32[]{:S(2)}) collective-permute-start(bf16[352,128]{1,0:T(8,128)(2,1)S(1)} %get-tuple-element.83), channel_id=1, source_target_pairs={{0,1},{1,0},{2,3},{3,2},{4,5},{5,4},{6,7},{7,6},{8,9},{9,8},{10,11... | collective-permute-start | bytes 270344 | tf_op jit(solution)/shard_map/ppermute | solution.py:661
  25.7 3.9 %collective-permute-start.8 = (bf16[352,128]{1,0:T(8,128)(2,1)S(1)}, bf16[352,128]{1,0:T(8,128)(2,1)S(1)}, u32[]{:S(2)}, u32[]{:S(2)}) collective-permute-start(bf16[352,128]{1,0:T(8,128)(2,1)S(1)} %get-tuple-element.84), channel_id=1, source_target_pairs={{1,2},{2,1},{5,6},{6,5},{9,10},{10,9},{13,14},{14,13},{17,18},{18,... | collective-permute-start | bytes 270344 | tf_op jit(solution)/shard_map/ppermute | solution.py:661
  27.3 8.3 %collective-permute-start.3 = (bf16[128,1024]{1,0:T(8,128)(2,1)S(1)}, bf16[128,1024]{1,0:T(8,128)(2,1)S(1)}, u32[]{:S(2)}, u32[]{:S(2)}) collective-permute-start(bf16[128,1024]{1,0:T(8,128)(2,1)S(1)} %get-tuple-element.75), channel_id=1, source_target_pairs={{0,1},{1,0},{2,3},{3,2},{4,5},{5,4},{6,7},{7,6},{8,9},{9,8},{10,11... | collective-permute-start | bytes 786440 | tf_op jit(solution)/shard_map/ppermute | solution.py:661
  28.7 7.0 %collective-permute-start.4 = (bf16[128,1024]{1,0:T(8,128)(2,1)S(1)}, bf16[128,1024]{1,0:T(8,128)(2,1)S(1)}, u32[]{:S(2)}, u32[]{:S(2)}) collective-permute-start(bf16[128,1024]{1,0:T(8,128)(2,1)S(1)} %get-tuple-element.76), channel_id=1, source_target_pairs={{1,2},{2,1},{5,6},{6,5},{9,10},{10,9},{13,14},{14,13},{17,18},{18,... | collective-permute-start | bytes 786440 | tf_op jit(solution)/shard_map/ppermute | solution.py:661

commit v7 on v6

--- a/solution.py
+++ b/solution.py
@@ -13,7 +13,8 @@
 STACK = 8
 STEP = LANES + 8
 EDGE = 48
-RING = LANES + 2 * EDGE
+HALF = LANES // 2
+RING = HALF + 2 * EDGE
 PART = 8
 HEAD_STACKS = 3
 HEAD_GROUPS = HEAD_STACKS * STACK
@@ -93,16 +94,16 @@
                 end[:, 512 * t + cut - HEAD : 512 * t + wide - HEAD] = value[:, cut:]
 
 
-def face_kernel(low, high, frag, flags, x_one, x_two):
+def face_kernel(low, high, frag, flags, *outs):
     odd = flags[X_ODD] > 0
     for z, plane in ((0, low), (1, high)):
         lines = slice(LANES * z, LANES * (z + 1))
         start, end = plane[:, :LANES], plane[:, WIDE - LANES :]
-        x_one[lines, :] = jnp.where(odd, start, end)
-        x_two[lines, :] = jnp.where(odd, end, start)
+        for out, pair in zip(outs, ((start, end), (end, start))):
+            out[lines, :] = jnp.where(odd, *pair)
     lines = [jnp.broadcast_to(frag[z, 127:128, :], (8, LANES)).astype(F32) for z in range(2)]
     lines = jnp.concatenate(lines, axis=0).astype(BF)
-    for out in (x_one, x_two):
+    for out in outs:
         out[2 * LANES :, :] = lines
 
 
@@ -152,7 +153,9 @@
         high = jnp.where(flags[Y_HIGH] > 0, jnp.where(odd, got_two[z], got_one[z]), none)
         y_low[z] = low
         y_high[z] = high
-        rings.append(jnp.concatenate([face[z], low, high], axis=0))
+        tile = face[z]
+        folded = jnp.where(iota((HALF, LANES), 1) < HALF, tile[:HALF], pltpu.roll(tile[HALF:], HALF, 1))
+        rings.append(jnp.concatenate([folded, low, high], axis=0))
     z_one[:RING, :] = jnp.where(z_odd, rings[0], rings[1])
     z_two[:RING, :] = jnp.where(z_odd, rings[1], rings[0])
     top = frag[1].astype(F32).astype(BF)
@@ -492,13 +495,13 @@
     for plane, ring, i in ((plane_one, ring_one, 1 - odd), (plane_two, ring_two, odd)):
         live = jnp.where(i > 0, flags[Z_HIGH], flags[Z_LOW]) > 0
         around = jnp.where(live, ring[:RING, :], jnp.zeros((RING, LANES), BF))
-        face = around[:LANES, :]
+        face = jnp.concatenate([around[:HALF], pltpu.roll(around[:HALF], HALF, 1)], axis=0)
         planes[i, :, LANES:] = plane[:, LANES:HEAD]
         planes[i, :, :LANES] = jnp.where(lane < 32, face, plane[:, :LANES])
         carry[i] = plane[:, HEAD - LANES : HEAD]
         carry[2 + i] = face
         for side, dy in ((0, 0), (1, 2)):
-            chunks = around[LANES + EDGE * side : LANES + EDGE * (side + 1), :]
+            chunks = around[HALF + EDGE * side : HALF + EDGE * (side + 1), :]
             lines[side, i] = jnp.dot(
                 line_windows(chunks), outer[i, :, LANES * dy : LANES * (dy + 1)], preferred_element_type=F32
             )
@@ -709,17 +712,14 @@
         [pltpu.VMEM((27, 32, LANES), BF), pltpu.VMEM((STEP * STACK + 8, 768), F32)],
         flops=300_000_000,
     )
-    x_one, x_two = call(
+    x_sent = call(
         face_kernel,
         "faces",
-        (
-            shape((2 * LANES + 16, LANES), BF),
-            shape((2 * LANES + 16, LANES), BF),
-        ),
+        (shape((2 * LANES + 16, LANES), BF),) * (1 if size["gx"] == 2 else 2),
         (xt_low, xt_high, fragments, flags),
         1,
     )
-    x_got = swap(x_one, x_two, "gx", True)
+    x_got = swap(x_sent[0], x_sent[-1], "gx", True)
 
     owner = edge_owner.reshape(1, slots)
     rank_hot, column_hot, group, name_hot, own_counts, plain, y_code, edge, first_col = call(

time: 54.4 us -> 54.1 us (level)
  transfers between devices with their start and end apart: 9 -> 9, of which waited for: 0 -> 0; matrix products, arithmetic and copies ran while one was open for 0% -> 0% of each run, Pallas kernels for 31% -> 30%
where the time goes in v7:
time: 54.1 us; the launch traced here: 53.9 us
  Pallas kernels  24.5 us (45%)
  starting transfers between devices  14.3 us (26%)
  blocking collectives  13.4 us (25%)
  between operations  1.57 us (3%)
    pallas_call x9, Pallas kernels, call(): pl.pallas_call(kernel, out_shape=out_shape, in_specs=[VMEM] * (len(args)...  21.6 us
    all_to_all x1, blocking collectives, shards(): lax.all_to_all(outgoing, axes, split_axis=0, concat_axis=0, tiled=True)  13.4 us
    ppermute x8, starting transfers between devices, swap(): lax.ppermute(value, axis, [pair for a, b in pairs for pair in ((a, b), (b...  12.8 us
    pallas_call x1, Pallas kernels, shards(): pl.pallas_call(layout_kernel, out_shape=(shape((LANES, WIDE), BF),) * 2 +...  2.87 us
    ppermute x1, starting transfers between devices, swap(): got = lax.ppermute(one, axis, [(0, 1), (1, 0)])  1.56 us
  transfers between devices with their start and end apart: 9, of which 0 were waited for; matrix products, arithmetic and copies ran while one was open for 0% of the time, Pallas kernels for 30%

profile of v7, /device:TPU:0, one launch (start us, length us, event | category | flops | bytes accessed | tf_op | source)
XLA Modules:
  0.0 53.9 jit_solution(11664252658547324598)
XLA Ops:
  1.3 0.1 stack.39.flags
  1.4 0.0 copy-start.3
  1.4 0.0 copy-start.4
  1.5 2.9 %layout.1 = (bf16[128,4224]{1,0:T(8,128)(2,1)S(1)}, bf16[128,4224]{1,0:T(8,128)(2,1)S(1)}, bf16[128,3200]{1,0:T(8,128)(2,1)S(1)}, bf16[128,3200]{1,0:T(8,128)(2,...) custom-call(s32[10]{0:T(128)S(1)} %stack.39.flags, bf16[32,2,128,128]{3,2,1,0:T(8,128)(2,1)} %feat_hbm.1), custom_call_target="tpu_custom_call" | custom-call | flops 1000000 | bytes 131072 | tf_op jit(solution)/shard_map/layout/pallas_call | solution.py:693
  4.3 3.1 %collective-permute-start.5 = (bf16[128,3200]{1,0:T(8,128)(2,1)S(1)}, bf16[128,3200]{1,0:T(8,128)(2,1)S(1)}, u32[]{:S(2)}, u32[]{:S(2)}) collective-permute-start(bf16[128,3200]{1,0:T(8,128)(2,1)S(1)} %get-tuple-element.79), channel_id=1, source_target_pairs={{0,1},{1,0},{2,3},{3,2},{4,5},{5,4},{6,7},{7,6},{8,9},{9,8},{10,11... | collective-permute-start | bytes 2457608 | tf_op jit(solution)/shard_map/ppermute | solution.py:664
  7.4 0.7 %collective-permute-start.6 = (bf16[128,3200]{1,0:T(8,128)(2,1)S(1)}, bf16[128,3200]{1,0:T(8,128)(2,1)S(1)}, u32[]{:S(2)}, u32[]{:S(2)}) collective-permute-start(bf16[128,3200]{1,0:T(8,128)(2,1)S(1)} %get-tuple-element.80), channel_id=1, source_target_pairs={{1,2},{2,1},{5,6},{6,5},{9,10},{10,9},{13,14},{14,13},{17,18},{18,... | collective-permute-start | bytes 2457608 | tf_op jit(solution)/shard_map/ppermute | solution.py:664
  8.2 0.0 copy-start.1
  8.2 0.0 copy-start.5
  8.2 0.6 %faces.1 = bf16[272,128]{1,0:T(8,128)(2,1)S(1)} custom-call(bf16[128,4224]{1,0:T(8,128)(2,1)S(1)} %get-tuple-element.50.low, bf16[128,4224]{1,0:T(8,128)(2,1)S(1)} %get-tuple-element.51.high, s32[2,128,128]{2,1,0:T(8,128)S(1)} %copy-done, s32[10]{0:T(128)S(1)} %stack.39.flags), custom_call_target="tpu_custom_call" | custom-call | flops 1000000 | bytes 131072 | tf_op jit(solution)/shard_map/faces/pallas_call | solution.py:31
  8.7 1.6 %collective-permute-start = (bf16[272,128]{1,0:T(8,128)(2,1)S(1)}, bf16[272,128]{1,0:T(8,128)(2,1)S(1)}, u32[]{:S(2)}, u32[]{:S(2)}) collective-permute-start(bf16[272,128]{1,0:T(8,128)(2,1)S(1)} %faces.1), channel_id=1, source_target_pairs={{0,16},{16,0},{1,17},{17,1},{2,18},{18,2},{3,19},{19,3},{4,20},{20... | collective-permute-start | bytes 208904 | tf_op jit(solution)/shard_map/ppermute | solution.py:659
  10.3 2.8 %ahead.1 = (bf16[2,128,1024]{2,1,0:T(8,128)(2,1)S(1)}, bf16[256,2048]{1,0:T(8,128)(2,1)S(1)}, s32[32,128]{1,0:T(8,128)S(1)}, bf16[128,4096]{1,0:T(8,128)(2,1)S(1...) custom-call(s32[2,1024]{1,0:T(2,128)S(1)} %copy-done.2, ...), custom_call_target="tpu_custom_call" | custom-call | flops 75000000 | bytes 131072 | tf_op jit(solution)/shard_map/ahead/pallas_call | solution.py:31
  13.1 0.0 copy-start.6
  13.2 0.0 copy-start.7
  13.2 0.0 collective-permute-done.got_one.got_two
  13.2 0.6 %x_face.1 = (bf16[2,128,128]{2,1,0:T(8,128)(2,1)S(1)}, f32[2,1,128]{2,1,0:T(1,128)S(1)}, bf16[2,48,128]{2,1,0:T(8,128)(2,1)S(1)}, bf16[2,48,128]{2,1,0:T(8,128)(2,1)S(1)}) custom-call(bf16[272,128]{1,0:T(8,128)(2,1)S(1)} %collective-permute-done.got_one.got_two, bf16[272,128]{1,0:T(8,128)(2,1)S(1)} %collective-permute-done.got_one.got_two, ...), custom_call_target="tpu_custom_call" | custom-call | flops 1000000 | bytes 131072 | tf_op jit(solution)/shard_map/x_face/pallas_call | solution.py:31
  13.8 0.1 collective-permute-start.1
  13.8 1.6 %collective-permute-start.2 = (bf16[2,48,128]{2,1,0:T(8,128)(2,1)S(1)}, bf16[2,48,128]{2,1,0:T(8,128)(2,1)S(1)}, u32[]{:S(2)}, u32[]{:S(2)}) collective-permute-start(bf16[2,48,128]{2,1,0:T(8,128)(2,1)S(1)} %get-tuple-element.61), channel_id=1, source_target_pairs={{4,8},{8,4},{0,12},{12,0},{5,9},{9,5},{1,13},{13,1},{6,10},{10,6},... | collective-permute-start | bytes 73736 | tf_op jit(solution)/shard_map/ppermute | solution.py:664
  15.5 4.6 %own_planes.1 = (f32[32,128,256]{2,1,0:T(8,128)S(1)}, bf16[3,512,256]{2,1,0:T(8,128)(2,1)S(1)}, bf16[2,256,384]{2,1,0:T(8,128)(2,1)S(1)}) custom-call(bf16[128,4224]{1,0:T(8,128)(2,1)S(1)} %get-tuple-element.50.low, bf16[128,4224]{1,0:T(8,128)(2,1)S(1)} %get-tuple-element.51.high, bf16[27,32,32]{2,1,0:T(8,128)(2,1)S(1)} %copy-done.1, f32[1,32]{1,0:T(1,128)S(1)} %bitcast.13), custom_call_target="tpu_custom_call" | custom-call | flops 300000000 | bytes 131072 | tf_op jit(solution)/shard_map/own_planes/pallas_call | solution.py:31
  20.1 0.6 %ring.1 = (bf16[2,48,128]{2,1,0:T(8,128)(2,1)S(1)}, bf16[2,48,128]{2,1,0:T(8,128)(2,1)S(1)}, bf16[288,128]{1,0:T(8,128)(2,1)S(1)}, bf16[288,128]{1,0:T(8,128)(2,1)S(1)}) custom-call(bf16[2,128,128]{2,1,0:T(8,128)(2,1)S(1)} %get-tuple-element.59.face, bf16[2,48,128]{2,1,0:T(8,128)(2,1)S(1)} %collective-permute-done.1.got_one, ...), custom_call_target="tpu_custom_call" | custom-call | flops 1000000 | bytes 131072 | tf_op jit(solution)/shard_map/ring/pallas_call | solution.py:31
  20.7 4.4 %collective-permute-start.7 = (bf16[288,128]{1,0:T(8,128)(2,1)S(1)}, bf16[288,128]{1,0:T(8,128)(2,1)S(1)}, u32[]{:S(2)}, u32[]{:S(2)}) collective-permute-start(bf16[288,128]{1,0:T(8,128)(2,1)S(1)} %get-tuple-element.81), channel_id=1, source_target_pairs={{0,1},{1,0},{2,3},{3,2},{4,5},{5,4},{6,7},{7,6},{8,9},{9,8},{10,11... | collective-permute-start | bytes 221192 | tf_op jit(solution)/shard_map/ppermute | solution.py:664
  25.2 0.7 %collective-permute-start.8 = (bf16[288,128]{1,0:T(8,128)(2,1)S(1)}, bf16[288,128]{1,0:T(8,128)(2,1)S(1)}, u32[]{:S(2)}, u32[]{:S(2)}) collective-permute-start(bf16[288,128]{1,0:T(8,128)(2,1)S(1)} %get-tuple-element.82), channel_id=1, source_target_pairs={{1,2},{2,1},{5,6},{6,5},{9,10},{10,9},{13,14},{14,13},{17,18},{18,... | collective-permute-start | bytes 221192 | tf_op jit(solution)/shard_map/ppermute | solution.py:664
  25.8 1.0 %edges.1 = (f32[2,32,256]{2,1,0:T(8,128)S(1)}, f32[2,128,256]{2,1,0:T(8,128)S(1)}, f32[64,256]{1,0:T(8,128)S(1)}) custom-call(bf16[2,128,128]{2,1,0:T(8,128)(2,1)S(1)} %get-tuple-element.59.face, bf16[2,48,128]{2,1,0:T(8,128)(2,1)S(1)} %get-tuple-element.65.y_low, bf16[2,48,128]{2,1,0:T(8,128)(2,1)S(1)} %get-tuple-element.66.y_high, ...), custom_call_target="tpu_custom_call" | custom-call | flops 50000000 | bytes 131072 | tf_op jit(solution)/shard_map/edges/pallas_call | solution.py:31
  26.8 1.3 %collective-permute-start.3 = (bf16[128,1024]{1,0:T(8,128)(2,1)S(1)}, bf16[128,1024]{1,0:T(8,128)(2,1)S(1)}, u32[]{:S(2)}, u32[]{:S(2)}) collective-permute-start(bf16[128,1024]{1,0:T(8,128)(2,1)S(1)} %get-tuple-element.73), channel_id=1, source_target_pairs={{0,1},{1,0},{2,3},{3,2},{4,5},{5,4},{6,7},{7,6},{8,9},{9,8},{10,11... | collective-permute-start | bytes 786440 | tf_op jit(solution)/shard_map/ppermute | solution.py:664
  28.2 0.0 collective-permute-done.7.ring_one
  28.2 0.8 %collective-permute-start.4 = (bf16[128,1024]{1,0:T(8,128)(2,1)S(1)}, bf16[128,1024]{1,0:T(8,128)(2,1)S(1)}, u32[]{:S(2)}, u32[]{:S(2)}) collective-permute-start(bf16[128,1024]{1,0:T(8,128)(2,1)S(1)} %get-tuple-element.74), channel_id=1, source_target_pairs={{1,2},{2,1},{5,6},{6,5},{9,10},{10,9},{13,14},{14,13},{17,18},{18,... | collective-permute-start | bytes 786440 | tf_op jit(solution)/shard_map/ppermute | solution.py:664
  29.0 0.0 collective-permute-done.5.plane_one
  29.0 0.0 collective-permute-done.6.plane_two
  29.1 6.1 %first_lines.1 = (bf16[3,2,96,128]{3,2,1,0:T(8,128)(2,1)S(1)}, f32[2,96,128]{2,1,0:T(8,128)S(1)}, f32[64,192]{1,0:T(8,128)S(1)}, f32[64,128]{1,0:T(8,128)S(1)}, ...) custom-call(f32[32,128,256]{2,1,0:T(8,128)S(1)} %get-tuple-element.5, ...), custom_call_target="tpu_custom_call" | custom-call | flops 6000000000 | bytes 131072 | tf_op jit(solution)/shard_map/first_lines/pallas_call | solution.py:31
  35.2 0.0 collective-permute-done.3.plane_one
  35.2 4.3 %last_lines.1 = (bf16[3,2,128,128]{3,2,1,0:T(8,128)(2,1)}, f32[32,1,128]{2,1,0:T(1,128)S(1)}) custom-call(f32[32,128,256]{2,1,0:T(8,128)S(1)} %get-tuple-element.52.acc, bf16[128,1024]{1,0:T(8,128)(2,1)S(1)} %collective-permute-done.3.plane_one, bf16[128,1024]{1,0:T(8,128)(2,1)S(1)} %collective-permute-done.4.plane_two, ...), custom_call_target="tpu_custom_call" | custom-call | flops 3000000000 | bytes 131072 | tf_op jit(solution)/shard_map/last_lines/pallas_call | solution.py:31
  39.5 13.4 %all_to_all.5.received = f32[32,1,128]{2,1,0:T(1,128)S(1)} all-to-all(f32[32,1,128]{2,1,0:T(1,128)S(1)} %get-tuple-element.95), channel_id=1, replica_groups=mesh['gx'=2,'gy'=4,'gz'=4] {'gx','gy','gz'}, dimensions={0} | all-to-all | bytes 32768 | tf_op jit(solution)/shard_map/all_to_all | solution.py:852
  52.8 1.0 %settle.1 = f32[1,384]{1,0:T(1,128)} custom-call(f32[32,1,128]{2,1,0:T(1,128)S(1)} %all_to_all.5.received, s32[32,128]{1,0:T(8,128)S(1)} %get-tuple-element.96.group_of, bf16[128,4096]{1,0:T(8,128)(2,1)S(1)} %get-tuple-element.97.name_hot), custom_call_target="tpu_custom_call" | custom-call | flops 1000000 | bytes 131072 | tf_op jit(solution)/shard_map/settle/pallas_call | solution.py:31
  (14 shorter events, 0.0 us)
Async XLA Ops:
  0.6 7.5 %copy-start = (s32[2,128,128]{2,1,0:T(8,128)S(1)}, s32[2,128,128]{2,1,0:T(8,128)}, u32[]{:S(2)}) copy-start(s32[2,128,128]{2,1,0:T(8,128)} %frag.5) | copy-start | bytes 393220
  1.4 8.9 %copy-start.2 = (s32[2,1024]{1,0:T(2,128)S(1)}, s32[2,1024]{1,0:T(2,128)}, u32[]{:S(2)}) copy-start(s32[2,1024]{1,0:T(2,128)} %cells.3) | copy-start | bytes 24580
  1.4 8.9 %copy-start.3 = (s32[1,1536]{1,0:T(1,128)S(1)}, s32[1,1536]{1,0:T(1,128)}, u32[]{:S(2)}) copy-start(s32[1,1536]{1,0:T(1,128)} %recv.1) | copy-start | bytes 18436
  1.4 8.9 %copy-start.4 = (s32[1024,1]{0,1:T(1,128)S(1)}, s32[1024,1]{0,1:T(1,128)}, u32[]{:S(2)}) copy-start(s32[1024,1]{0,1:T(1,128)} %param.17) | copy-start | bytes 12292
  4.3 24.7 %collective-permute-start.5 = (bf16[128,3200]{1,0:T(8,128)(2,1)S(1)}, bf16[128,3200]{1,0:T(8,128)(2,1)S(1)}, u32[]{:S(2)}, u32[]{:S(2)}) collective-permute-start(bf16[128,3200]{1,0:T(8,128)(2,1)S(1)} %get-tuple-element.79), channel_id=1, source_target_pairs={{0,1},{1,0},{2,3},{3,2},{4,5},{5,4},{6,7},{7,6},{8,9},{9,8},{10,11... | collective-permute-start | bytes 2457608 | tf_op jit(solution)/shard_map/ppermute | solution.py:664
  7.4 21.6 %collective-permute-start.6 = (bf16[128,3200]{1,0:T(8,128)(2,1)S(1)}, bf16[128,3200]{1,0:T(8,128)(2,1)S(1)}, u32[]{:S(2)}, u32[]{:S(2)}) collective-permute-start(bf16[128,3200]{1,0:T(8,128)(2,1)S(1)} %get-tuple-element.80), channel_id=1, source_target_pairs={{1,2},{2,1},{5,6},{6,5},{9,10},{10,9},{13,14},{14,13},{17,18},{18,... | collective-permute-start | bytes 2457608 | tf_op jit(solution)/shard_map/ppermute | solution.py:664
  8.2 7.3 %copy-start.1 = (bf16[27,32,32]{2,1,0:T(8,128)(2,1)S(1)}, bf16[27,32,32]{2,1,0:T(8,128)(2,1)}, u32[]{:S(2)}) copy-start(bf16[27,32,32]{2,1,0:T(8,128)(2,1)} %conv_weight.1) | copy-start | bytes 165892
  8.2 7.3 %copy-start.5 = (f32[32]{0:T(128)S(1)}, f32[32]{0:T(128)}, u32[]{:S(2)}) copy-start(f32[32]{0:T(128)} %param.12) | copy-start | bytes 388
  8.7 4.4 %collective-permute-start = (bf16[272,128]{1,0:T(8,128)(2,1)S(1)}, bf16[272,128]{1,0:T(8,128)(2,1)S(1)}, u32[]{:S(2)}, u32[]{:S(2)}) collective-permute-start(bf16[272,128]{1,0:T(8,128)(2,1)S(1)} %faces.1), channel_id=1, source_target_pairs={{0,16},{16,0},{1,17},{17,1},{2,18},{18,2},{3,19},{19,3},{4,20},{20... | collective-permute-start | bytes 208904 | tf_op jit(solution)/shard_map/ppermute | solution.py:659
  13.1 15.9 %copy-start.6 = (bf16[3,32]{1,0:T(4,128)(2,1)S(1)}, bf16[3,32]{1,0:T(4,128)(2,1)}, u32[]{:S(2)}) copy-start(bf16[3,32]{1,0:T(4,128)(2,1)} %head_weight.3) | copy-start | bytes 580
  13.2 15.9 %copy-start.7 = (f32[3]{0:T(128)S(1)}, f32[3]{0:T(128)}, u32[]{:S(2)}) copy-start(f32[3]{0:T(128)} %head_bias.3) | copy-start | bytes 40
  13.8 6.3 %collective-permute-start.1 = (bf16[2,48,128]{2,1,0:T(8,128)(2,1)S(1)}, bf16[2,48,128]{2,1,0:T(8,128)(2,1)S(1)}, u32[]{:S(2)}, u32[]{:S(2)}) collective-permute-start(bf16[2,48,128]{2,1,0:T(8,128)(2,1)S(1)} %get-tuple-element.60), channel_id=1, source_target_pairs={{0,4},{4,0},{8,12},{12,8},{1,5},{5,1},{9,13},{13,9},{2,6},{6,2},{1... | collective-permute-start | bytes 73736 | tf_op jit(solution)/shard_map/ppermute | solution.py:664
  13.8 6.3 %collective-permute-start.2 = (bf16[2,48,128]{2,1,0:T(8,128)(2,1)S(1)}, bf16[2,48,128]{2,1,0:T(8,128)(2,1)S(1)}, u32[]{:S(2)}, u32[]{:S(2)}) collective-permute-start(bf16[2,48,128]{2,1,0:T(8,128)(2,1)S(1)} %get-tuple-element.61), channel_id=1, source_target_pairs={{4,8},{8,4},{0,12},{12,0},{5,9},{9,5},{1,13},{13,1},{6,10},{10,6},... | collective-permute-start | bytes 73736 | tf_op jit(solution)/shard_map/ppermute | solution.py:664
  20.7 7.4 %collective-permute-start.7 = (bf16[288,128]{1,0:T(8,128)(2,1)S(1)}, bf16[288,128]{1,0:T(8,128)(2,1)S(1)}, u32[]{:S(2)}, u32[]{:S(2)}) collective-permute-start(bf16[288,128]{1,0:T(8,128)(2,1)S(1)} %get-tuple-element.81), channel_id=1, source_target_pairs={{0,1},{1,0},{2,3},{3,2},{4,5},{5,4},{6,7},{7,6},{8,9},{9,8},{10,11... | collective-permute-start | bytes 221192 | tf_op jit(solution)/shard_map/ppermute | solution.py:664
  25.2 3.9 %collective-permute-start.8 = (bf16[288,128]{1,0:T(8,128)(2,1)S(1)}, bf16[288,128]{1,0:T(8,128)(2,1)S(1)}, u32[]{:S(2)}, u32[]{:S(2)}) collective-permute-start(bf16[288,128]{1,0:T(8,128)(2,1)S(1)} %get-tuple-element.82), channel_id=1, source_target_pairs={{1,2},{2,1},{5,6},{6,5},{9,10},{10,9},{13,14},{14,13},{17,18},{18,... | collective-permute-start | bytes 221192 | tf_op jit(solution)/shard_map/ppermute | solution.py:664
  26.8 8.4 %collective-permute-start.3 = (bf16[128,1024]{1,0:T(8,128)(2,1)S(1)}, bf16[128,1024]{1,0:T(8,128)(2,1)S(1)}, u32[]{:S(2)}, u32[]{:S(2)}) collective-permute-start(bf16[128,1024]{1,0:T(8,128)(2,1)S(1)} %get-tuple-element.73), channel_id=1, source_target_pairs={{0,1},{1,0},{2,3},{3,2},{4,5},{5,4},{6,7},{7,6},{8,9},{9,8},{10,11... | collective-permute-start | bytes 786440 | tf_op jit(solution)/shard_map/ppermute | solution.py:664
  28.2 7.0 %collective-permute-start.4 = (bf16[128,1024]{1,0:T(8,128)(2,1)S(1)}, bf16[128,1024]{1,0:T(8,128)(2,1)S(1)}, u32[]{:S(2)}, u32[]{:S(2)}) collective-permute-start(bf16[128,1024]{1,0:T(8,128)(2,1)S(1)} %get-tuple-element.74), channel_id=1, source_target_pairs={{1,2},{2,1},{5,6},{6,5},{9,10},{10,9},{13,14},{14,13},{17,18},{18,... | collective-permute-start | bytes 786440 | tf_op jit(solution)/shard_map/ppermute | solution.py:664

commit v8 on v7

--- a/solution.py
+++ b/solution.py
@@ -15,7 +15,7 @@
 EDGE = 48
 HALF = LANES // 2
 RING = HALF + 2 * EDGE
-PART = 8
+PART = 16
 HEAD_STACKS = 3
 HEAD_GROUPS = HEAD_STACKS * STACK
 HEAD = (HEAD_GROUPS + 1) * LANES
@@ -522,9 +522,14 @@
         for i in range(6):
             affinity[i // 2, i % 2, all_lines, :] = kept[i, all_lines, :].astype(BF)
 
+    affinities(0)
+    low, high = jnp.zeros((F, 3 * F), F32), jnp.zeros((F, 2 * F), F32)
     for s in range(HEAD_STACKS):
-        affinities(s)
-    low, high = table_pieces(0, 0, plain, y_code, z_code, kept, HEAD_LINES)
+        if s + 1 < HEAD_STACKS:
+            affinities(s + 1)
+        x0 = 4 * STACK * s
+        more = table_pieces(x0, x0, plain, y_code, z_code, kept, 4 * STACK)
+        low, high = low + more[0], high + more[1]
     low_out[...] = low
     high_out[...] = high
     kept_y[...] = kept[4:6]
@@ -779,6 +784,7 @@
     )
 
     end_one, end_two, counts = lax.optimization_barrier((end_one, end_two, counts))
+    end_two, plane_one = lax.optimization_barrier((end_two, plane_one))
     end_one, end_two = swap(end_one, end_two, "gz", False)
 
     def stack_scratch(tiles, kept_lines):

time: 54.1 us -> 53.8 us (level)
  Pallas kernels: 24.5 us -> 23.9 us
    pallas_call x9, Pallas kernels: 21.6 us -> 21 us  [call(): pl.pallas_call(kernel, out_shape=out_shape, in_specs=[VMEM] * (len(args)...]
  transfers between devices with their start and end apart: 9 -> 9, of which waited for: 0 -> 1; matrix products, arithmetic and copies ran while one was open for 0% -> 0% of each run, Pallas kernels for 30% -> 29%
where the time goes in v8:
time: 53.8 us; the launch traced here: 53.6 us
  Pallas kernels  23.9 us (44%)
  starting transfers between devices  14.3 us (27%)
  blocking collectives  13.4 us (25%)
  between operations  1.56 us (3%)
    pallas_call x9, Pallas kernels, call(): pl.pallas_call(kernel, out_shape=out_shape, in_specs=[VMEM] * (len(args)...  21 us
    all_to_all x1, blocking collectives, shards(): lax.all_to_all(outgoing, axes, split_axis=0, concat_axis=0, tiled=True)  13.4 us
    ppermute x8, starting transfers between devices, swap(): lax.ppermute(value, axis, [pair for a, b in pairs for pair in ((a, b), (b...  12.8 us
    pallas_call x1, Pallas kernels, shards(): pl.pallas_call(layout_kernel, out_shape=(shape((LANES, WIDE), BF),) * 2 +...  2.87 us
    ppermute x1, starting transfers between devices, swap(): got = lax.ppermute(one, axis, [(0, 1), (1, 0)])  1.56 us
  transfers between devices with their start and end apart: 9, of which 1 were waited for; matrix products, arithmetic and copies ran while one was open for 0% of the time, Pallas kernels for 29%

profile of v8, /device:TPU:0, one launch (start us, length us, event | category | flops | bytes accessed | tf_op | source)
XLA Modules:
  0.0 53.6 jit_solution(3126086957449232830)
XLA Ops:
  1.3 0.1 stack.39.flags
  1.4 0.0 copy-start.3
  1.4 0.0 copy-start.4
  1.5 2.9 %layout.1 = (bf16[128,4224]{1,0:T(8,128)(2,1)S(1)}, bf16[128,4224]{1,0:T(8,128)(2,1)S(1)}, bf16[128,3200]{1,0:T(8,128)(2,1)S(1)}, bf16[128,3200]{1,0:T(8,128)(2,...) custom-call(s32[10]{0:T(128)S(1)} %stack.39.flags, bf16[32,2,128,128]{3,2,1,0:T(8,128)(2,1)} %feat_hbm.1), custom_call_target="tpu_custom_call" | custom-call | flops 1000000 | bytes 131072 | tf_op jit(solution)/shard_map/layout/pallas_call | solution.py:698
  4.3 3.1 %collective-permute-start.4 = (bf16[128,3200]{1,0:T(8,128)(2,1)S(1)}, bf16[128,3200]{1,0:T(8,128)(2,1)S(1)}, u32[]{:S(2)}, u32[]{:S(2)}) collective-permute-start(bf16[128,3200]{1,0:T(8,128)(2,1)S(1)} %get-tuple-element.77), channel_id=1, source_target_pairs={{0,1},{1,0},{2,3},{3,2},{4,5},{5,4},{6,7},{7,6},{8,9},{9,8},{10,11... | collective-permute-start | bytes 2457608 | tf_op jit(solution)/shard_map/ppermute | solution.py:669
  7.4 0.7 %collective-permute-start.6 = (bf16[128,3200]{1,0:T(8,128)(2,1)S(1)}, bf16[128,3200]{1,0:T(8,128)(2,1)S(1)}, u32[]{:S(2)}, u32[]{:S(2)}) collective-permute-start(bf16[128,3200]{1,0:T(8,128)(2,1)S(1)} %get-tuple-element.84), channel_id=1, source_target_pairs={{1,2},{2,1},{5,6},{6,5},{9,10},{10,9},{13,14},{14,13},{17,18},{18,... | collective-permute-start | bytes 2457608 | tf_op jit(solution)/shard_map/ppermute | solution.py:669
  8.2 0.0 copy-start.1
  8.2 0.0 copy-start.5
  8.2 0.6 %faces.1 = bf16[272,128]{1,0:T(8,128)(2,1)S(1)} custom-call(bf16[128,4224]{1,0:T(8,128)(2,1)S(1)} %get-tuple-element.52.low, bf16[128,4224]{1,0:T(8,128)(2,1)S(1)} %get-tuple-element.53.high, s32[2,128,128]{2,1,0:T(8,128)S(1)} %copy-done, s32[10]{0:T(128)S(1)} %stack.39.flags), custom_call_target="tpu_custom_call" | custom-call | flops 1000000 | bytes 131072 | tf_op jit(solution)/shard_map/faces/pallas_call | solution.py:31
  8.7 1.6 %collective-permute-start = (bf16[272,128]{1,0:T(8,128)(2,1)S(1)}, bf16[272,128]{1,0:T(8,128)(2,1)S(1)}, u32[]{:S(2)}, u32[]{:S(2)}) collective-permute-start(bf16[272,128]{1,0:T(8,128)(2,1)S(1)} %faces.1), channel_id=1, source_target_pairs={{0,16},{16,0},{1,17},{17,1},{2,18},{18,2},{3,19},{19,3},{4,20},{20... | collective-permute-start | bytes 208904 | tf_op jit(solution)/shard_map/ppermute | solution.py:664
  10.3 2.8 %ahead.1 = (bf16[2,128,1024]{2,1,0:T(8,128)(2,1)S(1)}, bf16[256,2048]{1,0:T(8,128)(2,1)S(1)}, s32[32,128]{1,0:T(8,128)S(1)}, bf16[128,4096]{1,0:T(8,128)(2,1)S(1...) custom-call(s32[2,1024]{1,0:T(2,128)S(1)} %copy-done.2, ...), custom_call_target="tpu_custom_call" | custom-call | flops 75000000 | bytes 131072 | tf_op jit(solution)/shard_map/ahead/pallas_call | solution.py:31
  13.1 0.0 copy-start.6
  13.2 0.0 copy-start.7
  13.2 0.0 collective-permute-done.got_one.got_two
  13.2 0.6 %x_face.1 = (bf16[2,128,128]{2,1,0:T(8,128)(2,1)S(1)}, f32[2,1,128]{2,1,0:T(1,128)S(1)}, bf16[2,48,128]{2,1,0:T(8,128)(2,1)S(1)}, bf16[2,48,128]{2,1,0:T(8,128)(2,1)S(1)}) custom-call(bf16[272,128]{1,0:T(8,128)(2,1)S(1)} %collective-permute-done.got_one.got_two, bf16[272,128]{1,0:T(8,128)(2,1)S(1)} %collective-permute-done.got_one.got_two, ...), custom_call_target="tpu_custom_call" | custom-call | flops 1000000 | bytes 131072 | tf_op jit(solution)/shard_map/x_face/pallas_call | solution.py:31
  13.8 0.1 collective-permute-start.1
  13.8 1.6 %collective-permute-start.2 = (bf16[2,48,128]{2,1,0:T(8,128)(2,1)S(1)}, bf16[2,48,128]{2,1,0:T(8,128)(2,1)S(1)}, u32[]{:S(2)}, u32[]{:S(2)}) collective-permute-start(bf16[2,48,128]{2,1,0:T(8,128)(2,1)S(1)} %get-tuple-element.63), channel_id=1, source_target_pairs={{4,8},{8,4},{0,12},{12,0},{5,9},{9,5},{1,13},{13,1},{6,10},{10,6},... | collective-permute-start | bytes 73736 | tf_op jit(solution)/shard_map/ppermute | solution.py:669
  15.5 4.6 %own_planes.1 = (f32[32,128,256]{2,1,0:T(8,128)S(1)}, bf16[3,512,256]{2,1,0:T(8,128)(2,1)S(1)}, bf16[2,256,384]{2,1,0:T(8,128)(2,1)S(1)}) custom-call(bf16[128,4224]{1,0:T(8,128)(2,1)S(1)} %get-tuple-element.52.low, bf16[128,4224]{1,0:T(8,128)(2,1)S(1)} %get-tuple-element.53.high, bf16[27,32,32]{2,1,0:T(8,128)(2,1)S(1)} %copy-done.1, f32[1,32]{1,0:T(1,128)S(1)} %bitcast.13), custom_call_target="tpu_custom_call" | custom-call | flops 300000000 | bytes 131072 | tf_op jit(solution)/shard_map/own_planes/pallas_call | solution.py:31
  20.1 0.6 %ring.1 = (bf16[2,48,128]{2,1,0:T(8,128)(2,1)S(1)}, bf16[2,48,128]{2,1,0:T(8,128)(2,1)S(1)}, bf16[288,128]{1,0:T(8,128)(2,1)S(1)}, bf16[288,128]{1,0:T(8,128)(2,1)S(1)}) custom-call(bf16[2,128,128]{2,1,0:T(8,128)(2,1)S(1)} %get-tuple-element.61.face, bf16[2,48,128]{2,1,0:T(8,128)(2,1)S(1)} %collective-permute-done.1.got_one, ...), custom_call_target="tpu_custom_call" | custom-call | flops 1000000 | bytes 131072 | tf_op jit(solution)/shard_map/ring/pallas_call | solution.py:31
  20.7 4.4 %collective-permute-start.7 = (bf16[288,128]{1,0:T(8,128)(2,1)S(1)}, bf16[288,128]{1,0:T(8,128)(2,1)S(1)}, u32[]{:S(2)}, u32[]{:S(2)}) collective-permute-start(bf16[288,128]{1,0:T(8,128)(2,1)S(1)} %get-tuple-element.85), channel_id=1, source_target_pairs={{0,1},{1,0},{2,3},{3,2},{4,5},{5,4},{6,7},{7,6},{8,9},{9,8},{10,11... | collective-permute-start | bytes 221192 | tf_op jit(solution)/shard_map/ppermute | solution.py:669
  25.2 0.7 %collective-permute-start.8 = (bf16[288,128]{1,0:T(8,128)(2,1)S(1)}, bf16[288,128]{1,0:T(8,128)(2,1)S(1)}, u32[]{:S(2)}, u32[]{:S(2)}) collective-permute-start(bf16[288,128]{1,0:T(8,128)(2,1)S(1)} %get-tuple-element.86), channel_id=1, source_target_pairs={{1,2},{2,1},{5,6},{6,5},{9,10},{10,9},{13,14},{14,13},{17,18},{18,... | collective-permute-start | bytes 221192 | tf_op jit(solution)/shard_map/ppermute | solution.py:669
  25.8 1.0 %edges.1 = (f32[2,32,256]{2,1,0:T(8,128)S(1)}, f32[2,128,256]{2,1,0:T(8,128)S(1)}, f32[64,256]{1,0:T(8,128)S(1)}) custom-call(bf16[2,128,128]{2,1,0:T(8,128)(2,1)S(1)} %get-tuple-element.61.face, bf16[2,48,128]{2,1,0:T(8,128)(2,1)S(1)} %get-tuple-element.67.y_low, bf16[2,48,128]{2,1,0:T(8,128)(2,1)S(1)} %get-tuple-element.68.y_high, ...), custom_call_target="tpu_custom_call" | custom-call | flops 50000000 | bytes 131072 | tf_op jit(solution)/shard_map/edges/pallas_call | solution.py:31
  26.8 1.3 %collective-permute-start.3 = (bf16[128,1024]{1,0:T(8,128)(2,1)S(1)}, bf16[128,1024]{1,0:T(8,128)(2,1)S(1)}, u32[]{:S(2)}, u32[]{:S(2)}) collective-permute-start(bf16[128,1024]{1,0:T(8,128)(2,1)S(1)} %get-tuple-element.75), channel_id=1, source_target_pairs={{0,1},{1,0},{2,3},{3,2},{4,5},{5,4},{6,7},{7,6},{8,9},{9,8},{10,11... | collective-permute-start | bytes 786440 | tf_op jit(solution)/shard_map/ppermute | solution.py:669
  28.2 0.0 collective-permute-done.4.plane_one
  28.2 0.8 %collective-permute-start.5 = (bf16[128,1024]{1,0:T(8,128)(2,1)S(1)}, bf16[128,1024]{1,0:T(8,128)(2,1)S(1)}, u32[]{:S(2)}, u32[]{:S(2)}) collective-permute-start(bf16[128,1024]{1,0:T(8,128)(2,1)S(1)} %get-tuple-element.78), channel_id=1, source_target_pairs={{1,2},{2,1},{5,6},{6,5},{9,10},{10,9},{13,14},{14,13},{17,18},{18,... | collective-permute-start | bytes 786440 | tf_op jit(solution)/shard_map/ppermute | solution.py:669
  29.0 0.0 collective-permute-done.8.ring_two
  29.0 0.0 collective-permute-done.6.plane_two
  29.1 5.5 %first_lines.1 = (bf16[3,2,96,128]{3,2,1,0:T(8,128)(2,1)S(1)}, f32[2,96,128]{2,1,0:T(8,128)S(1)}, f32[64,192]{1,0:T(8,128)S(1)}, f32[64,128]{1,0:T(8,128)S(1)}, ...) custom-call(f32[32,128,256]{2,1,0:T(8,128)S(1)} %get-tuple-element.5, ...), custom_call_target="tpu_custom_call" | custom-call | flops 6000000000 | bytes 131072 | tf_op jit(solution)/shard_map/first_lines/pallas_call | solution.py:31
  34.6 0.3 collective-permute-done.3.plane_one
  34.9 4.3 %last_lines.1 = (bf16[3,2,128,128]{3,2,1,0:T(8,128)(2,1)}, f32[32,1,128]{2,1,0:T(1,128)S(1)}) custom-call(f32[32,128,256]{2,1,0:T(8,128)S(1)} %get-tuple-element.54.acc, bf16[128,1024]{1,0:T(8,128)(2,1)S(1)} %collective-permute-done.3.plane_one, bf16[128,1024]{1,0:T(8,128)(2,1)S(1)} %collective-permute-done.5.plane_two, ...), custom_call_target="tpu_custom_call" | custom-call | flops 3000000000 | bytes 131072 | tf_op jit(solution)/shard_map/last_lines/pallas_call | solution.py:31
  39.2 13.4 %all_to_all.5.received = f32[32,1,128]{2,1,0:T(1,128)S(1)} all-to-all(f32[32,1,128]{2,1,0:T(1,128)S(1)} %get-tuple-element.99), channel_id=1, replica_groups=mesh['gx'=2,'gy'=4,'gz'=4] {'gx','gy','gz'}, dimensions={0} | all-to-all | bytes 32768 | tf_op jit(solution)/shard_map/all_to_all | solution.py:858
  52.6 1.0 %settle.1 = f32[1,384]{1,0:T(1,128)} custom-call(f32[32,1,128]{2,1,0:T(1,128)S(1)} %all_to_all.5.received, s32[32,128]{1,0:T(8,128)S(1)} %get-tuple-element.100.group_of, bf16[128,4096]{1,0:T(8,128)(2,1)S(1)} %get-tuple-element.101.name_hot), custom_call_target="tpu_custom_call" | custom-call | flops 1000000 | bytes 131072 | tf_op jit(solution)/shard_map/settle/pallas_call | solution.py:31
  (14 shorter events, 0.0 us)
Async XLA Ops:
  0.6 7.5 %copy-start = (s32[2,128,128]{2,1,0:T(8,128)S(1)}, s32[2,128,128]{2,1,0:T(8,128)}, u32[]{:S(2)}) copy-start(s32[2,128,128]{2,1,0:T(8,128)} %frag.5) | copy-start | bytes 393220
  1.4 8.9 %copy-start.2 = (s32[2,1024]{1,0:T(2,128)S(1)}, s32[2,1024]{1,0:T(2,128)}, u32[]{:S(2)}) copy-start(s32[2,1024]{1,0:T(2,128)} %cells.3) | copy-start | bytes 24580
  1.4 8.9 %copy-start.3 = (s32[1,1536]{1,0:T(1,128)S(1)}, s32[1,1536]{1,0:T(1,128)}, u32[]{:S(2)}) copy-start(s32[1,1536]{1,0:T(1,128)} %recv.1) | copy-start | bytes 18436
  1.4 8.9 %copy-start.4 = (s32[1024,1]{0,1:T(1,128)S(1)}, s32[1024,1]{0,1:T(1,128)}, u32[]{:S(2)}) copy-start(s32[1024,1]{0,1:T(1,128)} %param.17) | copy-start | bytes 12292
  4.3 23.8 %collective-permute-start.4 = (bf16[128,3200]{1,0:T(8,128)(2,1)S(1)}, bf16[128,3200]{1,0:T(8,128)(2,1)S(1)}, u32[]{:S(2)}, u32[]{:S(2)}) collective-permute-start(bf16[128,3200]{1,0:T(8,128)(2,1)S(1)} %get-tuple-element.77), channel_id=1, source_target_pairs={{0,1},{1,0},{2,3},{3,2},{4,5},{5,4},{6,7},{7,6},{8,9},{9,8},{10,11... | collective-permute-start | bytes 2457608 | tf_op jit(solution)/shard_map/ppermute | solution.py:669
  7.4 21.6 %collective-permute-start.6 = (bf16[128,3200]{1,0:T(8,128)(2,1)S(1)}, bf16[128,3200]{1,0:T(8,128)(2,1)S(1)}, u32[]{:S(2)}, u32[]{:S(2)}) collective-permute-start(bf16[128,3200]{1,0:T(8,128)(2,1)S(1)} %get-tuple-element.84), channel_id=1, source_target_pairs={{1,2},{2,1},{5,6},{6,5},{9,10},{10,9},{13,14},{14,13},{17,18},{18,... | collective-permute-start | bytes 2457608 | tf_op jit(solution)/shard_map/ppermute | solution.py:669
  8.2 7.3 %copy-start.1 = (bf16[27,32,32]{2,1,0:T(8,128)(2,1)S(1)}, bf16[27,32,32]{2,1,0:T(8,128)(2,1)}, u32[]{:S(2)}) copy-start(bf16[27,32,32]{2,1,0:T(8,128)(2,1)} %conv_weight.1) | copy-start | bytes 165892
  8.2 7.3 %copy-start.5 = (f32[32]{0:T(128)S(1)}, f32[32]{0:T(128)}, u32[]{:S(2)}) copy-start(f32[32]{0:T(128)} %param.12) | copy-start | bytes 388
  8.7 4.4 %collective-permute-start = (bf16[272,128]{1,0:T(8,128)(2,1)S(1)}, bf16[272,128]{1,0:T(8,128)(2,1)S(1)}, u32[]{:S(2)}, u32[]{:S(2)}) collective-permute-start(bf16[272,128]{1,0:T(8,128)(2,1)S(1)} %faces.1), channel_id=1, source_target_pairs={{0,16},{16,0},{1,17},{17,1},{2,18},{18,2},{3,19},{19,3},{4,20},{20... | collective-permute-start | bytes 208904 | tf_op jit(solution)/shard_map/ppermute | solution.py:664
  13.1 15.9 %copy-start.6 = (bf16[3,32]{1,0:T(4,128)(2,1)S(1)}, bf16[3,32]{1,0:T(4,128)(2,1)}, u32[]{:S(2)}) copy-start(bf16[3,32]{1,0:T(4,128)(2,1)} %head_weight.3) | copy-start | bytes 580
  13.2 15.9 %copy-start.7 = (f32[3]{0:T(128)S(1)}, f32[3]{0:T(128)}, u32[]{:S(2)}) copy-start(f32[3]{0:T(128)} %head_bias.3) | copy-start | bytes 40
  13.8 6.3 %collective-permute-start.1 = (bf16[2,48,128]{2,1,0:T(8,128)(2,1)S(1)}, bf16[2,48,128]{2,1,0:T(8,128)(2,1)S(1)}, u32[]{:S(2)}, u32[]{:S(2)}) collective-permute-start(bf16[2,48,128]{2,1,0:T(8,128)(2,1)S(1)} %get-tuple-element.62), channel_id=1, source_target_pairs={{0,4},{4,0},{8,12},{12,8},{1,5},{5,1},{9,13},{13,9},{2,6},{6,2},{1... | collective-permute-start | bytes 73736 | tf_op jit(solution)/shard_map/ppermute | solution.py:669
  13.8 6.3 %collective-permute-start.2 = (bf16[2,48,128]{2,1,0:T(8,128)(2,1)S(1)}, bf16[2,48,128]{2,1,0:T(8,128)(2,1)S(1)}, u32[]{:S(2)}, u32[]{:S(2)}) collective-permute-start(bf16[2,48,128]{2,1,0:T(8,128)(2,1)S(1)} %get-tuple-element.63), channel_id=1, source_target_pairs={{4,8},{8,4},{0,12},{12,0},{5,9},{9,5},{1,13},{13,1},{6,10},{10,6},... | collective-permute-start | bytes 73736 | tf_op jit(solution)/shard_map/ppermute | solution.py:669
  20.7 8.3 %collective-permute-start.7 = (bf16[288,128]{1,0:T(8,128)(2,1)S(1)}, bf16[288,128]{1,0:T(8,128)(2,1)S(1)}, u32[]{:S(2)}, u32[]{:S(2)}) collective-permute-start(bf16[288,128]{1,0:T(8,128)(2,1)S(1)} %get-tuple-element.85), channel_id=1, source_target_pairs={{0,1},{1,0},{2,3},{3,2},{4,5},{5,4},{6,7},{7,6},{8,9},{9,8},{10,11... | collective-permute-start | bytes 221192 | tf_op jit(solution)/shard_map/ppermute | solution.py:669
  25.2 3.9 %collective-permute-start.8 = (bf16[288,128]{1,0:T(8,128)(2,1)S(1)}, bf16[288,128]{1,0:T(8,128)(2,1)S(1)}, u32[]{:S(2)}, u32[]{:S(2)}) collective-permute-start(bf16[288,128]{1,0:T(8,128)(2,1)S(1)} %get-tuple-element.86), channel_id=1, source_target_pairs={{1,2},{2,1},{5,6},{6,5},{9,10},{10,9},{13,14},{14,13},{17,18},{18,... | collective-permute-start | bytes 221192 | tf_op jit(solution)/shard_map/ppermute | solution.py:669
  26.8 8.1 %collective-permute-start.3 = (bf16[128,1024]{1,0:T(8,128)(2,1)S(1)}, bf16[128,1024]{1,0:T(8,128)(2,1)S(1)}, u32[]{:S(2)}, u32[]{:S(2)}) collective-permute-start(bf16[128,1024]{1,0:T(8,128)(2,1)S(1)} %get-tuple-element.75), channel_id=1, source_target_pairs={{0,1},{1,0},{2,3},{3,2},{4,5},{5,4},{6,7},{7,6},{8,9},{9,8},{10,11... | collective-permute-start | bytes 786440 | tf_op jit(solution)/shard_map/ppermute | solution.py:669
  28.2 6.7 %collective-permute-start.5 = (bf16[128,1024]{1,0:T(8,128)(2,1)S(1)}, bf16[128,1024]{1,0:T(8,128)(2,1)S(1)}, u32[]{:S(2)}, u32[]{:S(2)}) collective-permute-start(bf16[128,1024]{1,0:T(8,128)(2,1)S(1)} %get-tuple-element.78), channel_id=1, source_target_pairs={{1,2},{2,1},{5,6},{6,5},{9,10},{10,9},{13,14},{14,13},{17,18},{18,... | collective-permute-start | bytes 786440 | tf_op jit(solution)/shard_map/ppermute | solution.py:669

commit v9 on v8

--- a/solution.py
+++ b/solution.py
@@ -15,7 +15,7 @@
 EDGE = 48
 HALF = LANES // 2
 RING = HALF + 2 * EDGE
-PART = 16
+PART = 32
 HEAD_STACKS = 3
 HEAD_GROUPS = HEAD_STACKS * STACK
 HEAD = (HEAD_GROUPS + 1) * LANES

time: 53.8 us -> 53.6 us (level)
  no operation moved by 1% of the time
where the time goes in v9:
time: 53.6 us; the launch traced here: 53.4 us
  Pallas kernels  23.7 us (44%)
  starting transfers between devices  14.3 us (27%)
  blocking collectives  13.3 us (25%)
  between operations  1.56 us (3%)
    pallas_call x9, Pallas kernels, call(): pl.pallas_call(kernel, out_shape=out_shape, in_specs=[VMEM] * (len(args)...  20.9 us
    all_to_all x1, blocking collectives, shards(): lax.all_to_all(outgoing, axes, split_axis=0, concat_axis=0, tiled=True)  13.3 us
    ppermute x8, starting transfers between devices, swap(): lax.ppermute(value, axis, [pair for a, b in pairs for pair in ((a, b), (b...  12.8 us
    pallas_call x1, Pallas kernels, shards(): pl.pallas_call(layout_kernel, out_shape=(shape((LANES, WIDE), BF),) * 2 +...  2.87 us
    ppermute x1, starting transfers between devices, swap(): got = lax.ppermute(one, axis, [(0, 1), (1, 0)])  1.56 us
  transfers between devices with their start and end apart: 9, of which 1 were waited for; matrix products, arithmetic and copies ran while one was open for 0% of the time, Pallas kernels for 29%

profile of v9, /device:TPU:0, one launch (start us, length us, event | category | flops | bytes accessed | tf_op | source)
XLA Modules:
  0.0 53.4 jit_solution(62054988825512092)
XLA Ops:
  1.3 0.1 stack.39.flags
  1.4 0.0 copy-start.3
  1.4 0.0 copy-start.4
  1.5 2.9 %layout.1 = (bf16[128,4224]{1,0:T(8,128)(2,1)S(1)}, bf16[128,4224]{1,0:T(8,128)(2,1)S(1)}, bf16[128,3200]{1,0:T(8,128)(2,1)S(1)}, bf16[128,3200]{1,0:T(8,128)(2,...) custom-call(s32[10]{0:T(128)S(1)} %stack.39.flags, bf16[32,2,128,128]{3,2,1,0:T(8,128)(2,1)} %feat_hbm.1), custom_call_target="tpu_custom_call" | custom-call | flops 1000000 | bytes 131072 | tf_op jit(solution)/shard_map/layout/pallas_call | solution.py:698
  4.3 3.1 %collective-permute-start.4 = (bf16[128,3200]{1,0:T(8,128)(2,1)S(1)}, bf16[128,3200]{1,0:T(8,128)(2,1)S(1)}, u32[]{:S(2)}, u32[]{:S(2)}) collective-permute-start(bf16[128,3200]{1,0:T(8,128)(2,1)S(1)} %get-tuple-element.77), channel_id=1, source_target_pairs={{0,1},{1,0},{2,3},{3,2},{4,5},{5,4},{6,7},{7,6},{8,9},{9,8},{10,11... | collective-permute-start | bytes 2457608 | tf_op jit(solution)/shard_map/ppermute | solution.py:669
  7.4 0.7 %collective-permute-start.6 = (bf16[128,3200]{1,0:T(8,128)(2,1)S(1)}, bf16[128,3200]{1,0:T(8,128)(2,1)S(1)}, u32[]{:S(2)}, u32[]{:S(2)}) collective-permute-start(bf16[128,3200]{1,0:T(8,128)(2,1)S(1)} %get-tuple-element.84), channel_id=1, source_target_pairs={{1,2},{2,1},{5,6},{6,5},{9,10},{10,9},{13,14},{14,13},{17,18},{18,... | collective-permute-start | bytes 2457608 | tf_op jit(solution)/shard_map/ppermute | solution.py:669
  8.2 0.0 copy-start.1
  8.2 0.0 copy-start.5
  8.2 0.6 %faces.1 = bf16[272,128]{1,0:T(8,128)(2,1)S(1)} custom-call(bf16[128,4224]{1,0:T(8,128)(2,1)S(1)} %get-tuple-element.52.low, bf16[128,4224]{1,0:T(8,128)(2,1)S(1)} %get-tuple-element.53.high, s32[2,128,128]{2,1,0:T(8,128)S(1)} %copy-done, s32[10]{0:T(128)S(1)} %stack.39.flags), custom_call_target="tpu_custom_call" | custom-call | flops 1000000 | bytes 131072 | tf_op jit(solution)/shard_map/faces/pallas_call | solution.py:31
  8.7 1.6 %collective-permute-start = (bf16[272,128]{1,0:T(8,128)(2,1)S(1)}, bf16[272,128]{1,0:T(8,128)(2,1)S(1)}, u32[]{:S(2)}, u32[]{:S(2)}) collective-permute-start(bf16[272,128]{1,0:T(8,128)(2,1)S(1)} %faces.1), channel_id=1, source_target_pairs={{0,16},{16,0},{1,17},{17,1},{2,18},{18,2},{3,19},{19,3},{4,20},{20... | collective-permute-start | bytes 208904 | tf_op jit(solution)/shard_map/ppermute | solution.py:664
  10.3 2.8 %ahead.1 = (bf16[2,128,1024]{2,1,0:T(8,128)(2,1)S(1)}, bf16[256,2048]{1,0:T(8,128)(2,1)S(1)}, s32[32,128]{1,0:T(8,128)S(1)}, bf16[128,4096]{1,0:T(8,128)(2,1)S(1...) custom-call(s32[2,1024]{1,0:T(2,128)S(1)} %copy-done.2, ...), custom_call_target="tpu_custom_call" | custom-call | flops 75000000 | bytes 131072 | tf_op jit(solution)/shard_map/ahead/pallas_call | solution.py:31
  13.1 0.0 copy-start.6
  13.2 0.0 copy-start.7
  13.2 0.0 collective-permute-done.got_one.got_two
  13.2 0.6 %x_face.1 = (bf16[2,128,128]{2,1,0:T(8,128)(2,1)S(1)}, f32[2,1,128]{2,1,0:T(1,128)S(1)}, bf16[2,48,128]{2,1,0:T(8,128)(2,1)S(1)}, bf16[2,48,128]{2,1,0:T(8,128)(2,1)S(1)}) custom-call(bf16[272,128]{1,0:T(8,128)(2,1)S(1)} %collective-permute-done.got_one.got_two, bf16[272,128]{1,0:T(8,128)(2,1)S(1)} %collective-permute-done.got_one.got_two, ...), custom_call_target="tpu_custom_call" | custom-call | flops 1000000 | bytes 131072 | tf_op jit(solution)/shard_map/x_face/pallas_call | solution.py:31
  13.8 0.1 collective-permute-start.1
  13.8 1.6 %collective-permute-start.2 = (bf16[2,48,128]{2,1,0:T(8,128)(2,1)S(1)}, bf16[2,48,128]{2,1,0:T(8,128)(2,1)S(1)}, u32[]{:S(2)}, u32[]{:S(2)}) collective-permute-start(bf16[2,48,128]{2,1,0:T(8,128)(2,1)S(1)} %get-tuple-element.63), channel_id=1, source_target_pairs={{4,8},{8,4},{0,12},{12,0},{5,9},{9,5},{1,13},{13,1},{6,10},{10,6},... | collective-permute-start | bytes 73736 | tf_op jit(solution)/shard_map/ppermute | solution.py:669
  15.5 4.6 %own_planes.1 = (f32[32,128,256]{2,1,0:T(8,128)S(1)}, bf16[3,512,256]{2,1,0:T(8,128)(2,1)S(1)}, bf16[2,256,384]{2,1,0:T(8,128)(2,1)S(1)}) custom-call(bf16[128,4224]{1,0:T(8,128)(2,1)S(1)} %get-tuple-element.52.low, bf16[128,4224]{1,0:T(8,128)(2,1)S(1)} %get-tuple-element.53.high, bf16[27,32,32]{2,1,0:T(8,128)(2,1)S(1)} %copy-done.1, f32[1,32]{1,0:T(1,128)S(1)} %bitcast.13), custom_call_target="tpu_custom_call" | custom-call | flops 300000000 | bytes 131072 | tf_op jit(solution)/shard_map/own_planes/pallas_call | solution.py:31
  20.1 0.6 %ring.1 = (bf16[2,48,128]{2,1,0:T(8,128)(2,1)S(1)}, bf16[2,48,128]{2,1,0:T(8,128)(2,1)S(1)}, bf16[288,128]{1,0:T(8,128)(2,1)S(1)}, bf16[288,128]{1,0:T(8,128)(2,1)S(1)}) custom-call(bf16[2,128,128]{2,1,0:T(8,128)(2,1)S(1)} %get-tuple-element.61.face, bf16[2,48,128]{2,1,0:T(8,128)(2,1)S(1)} %collective-permute-done.1.got_one, ...), custom_call_target="tpu_custom_call" | custom-call | flops 1000000 | bytes 131072 | tf_op jit(solution)/shard_map/ring/pallas_call | solution.py:31
  20.7 4.4 %collective-permute-start.7 = (bf16[288,128]{1,0:T(8,128)(2,1)S(1)}, bf16[288,128]{1,0:T(8,128)(2,1)S(1)}, u32[]{:S(2)}, u32[]{:S(2)}) collective-permute-start(bf16[288,128]{1,0:T(8,128)(2,1)S(1)} %get-tuple-element.85), channel_id=1, source_target_pairs={{0,1},{1,0},{2,3},{3,2},{4,5},{5,4},{6,7},{7,6},{8,9},{9,8},{10,11... | collective-permute-start | bytes 221192 | tf_op jit(solution)/shard_map/ppermute | solution.py:669
  25.2 0.7 %collective-permute-start.8 = (bf16[288,128]{1,0:T(8,128)(2,1)S(1)}, bf16[288,128]{1,0:T(8,128)(2,1)S(1)}, u32[]{:S(2)}, u32[]{:S(2)}) collective-permute-start(bf16[288,128]{1,0:T(8,128)(2,1)S(1)} %get-tuple-element.86), channel_id=1, source_target_pairs={{1,2},{2,1},{5,6},{6,5},{9,10},{10,9},{13,14},{14,13},{17,18},{18,... | collective-permute-start | bytes 221192 | tf_op jit(solution)/shard_map/ppermute | solution.py:669
  25.8 1.0 %edges.1 = (f32[2,32,256]{2,1,0:T(8,128)S(1)}, f32[2,128,256]{2,1,0:T(8,128)S(1)}, f32[64,256]{1,0:T(8,128)S(1)}) custom-call(bf16[2,128,128]{2,1,0:T(8,128)(2,1)S(1)} %get-tuple-element.61.face, bf16[2,48,128]{2,1,0:T(8,128)(2,1)S(1)} %get-tuple-element.67.y_low, bf16[2,48,128]{2,1,0:T(8,128)(2,1)S(1)} %get-tuple-element.68.y_high, ...), custom_call_target="tpu_custom_call" | custom-call | flops 50000000 | bytes 131072 | tf_op jit(solution)/shard_map/edges/pallas_call | solution.py:31
  26.8 1.3 %collective-permute-start.3 = (bf16[128,1024]{1,0:T(8,128)(2,1)S(1)}, bf16[128,1024]{1,0:T(8,128)(2,1)S(1)}, u32[]{:S(2)}, u32[]{:S(2)}) collective-permute-start(bf16[128,1024]{1,0:T(8,128)(2,1)S(1)} %get-tuple-element.75), channel_id=1, source_target_pairs={{0,1},{1,0},{2,3},{3,2},{4,5},{5,4},{6,7},{7,6},{8,9},{9,8},{10,11... | collective-permute-start | bytes 786440 | tf_op jit(solution)/shard_map/ppermute | solution.py:669
  28.2 0.0 collective-permute-done.4.plane_one
  28.2 0.8 %collective-permute-start.5 = (bf16[128,1024]{1,0:T(8,128)(2,1)S(1)}, bf16[128,1024]{1,0:T(8,128)(2,1)S(1)}, u32[]{:S(2)}, u32[]{:S(2)}) collective-permute-start(bf16[128,1024]{1,0:T(8,128)(2,1)S(1)} %get-tuple-element.78), channel_id=1, source_target_pairs={{1,2},{2,1},{5,6},{6,5},{9,10},{10,9},{13,14},{14,13},{17,18},{18,... | collective-permute-start | bytes 786440 | tf_op jit(solution)/shard_map/ppermute | solution.py:669
  29.0 0.0 collective-permute-done.8.ring_two
  29.0 0.0 collective-permute-done.6.plane_two
  29.1 5.5 %first_lines.1 = (bf16[3,2,96,128]{3,2,1,0:T(8,128)(2,1)S(1)}, f32[2,96,128]{2,1,0:T(8,128)S(1)}, f32[64,192]{1,0:T(8,128)S(1)}, f32[64,128]{1,0:T(8,128)S(1)}, ...) custom-call(f32[32,128,256]{2,1,0:T(8,128)S(1)} %get-tuple-element.5, ...), custom_call_target="tpu_custom_call" | custom-call | flops 6000000000 | bytes 131072 | tf_op jit(solution)/shard_map/first_lines/pallas_call | solution.py:31
  34.5 0.3 collective-permute-done.3.plane_one
  34.9 4.2 %last_lines.1 = (bf16[3,2,128,128]{3,2,1,0:T(8,128)(2,1)}, f32[32,1,128]{2,1,0:T(1,128)S(1)}) custom-call(f32[32,128,256]{2,1,0:T(8,128)S(1)} %get-tuple-element.54.acc, bf16[128,1024]{1,0:T(8,128)(2,1)S(1)} %collective-permute-done.3.plane_one, bf16[128,1024]{1,0:T(8,128)(2,1)S(1)} %collective-permute-done.5.plane_two, ...), custom_call_target="tpu_custom_call" | custom-call | flops 3000000000 | bytes 131072 | tf_op jit(solution)/shard_map/last_lines/pallas_call | solution.py:31
  39.1 13.3 %all_to_all.5.received = f32[32,1,128]{2,1,0:T(1,128)S(1)} all-to-all(f32[32,1,128]{2,1,0:T(1,128)S(1)} %get-tuple-element.99), channel_id=1, replica_groups=mesh['gx'=2,'gy'=4,'gz'=4] {'gx','gy','gz'}, dimensions={0} | all-to-all | bytes 32768 | tf_op jit(solution)/shard_map/all_to_all | solution.py:858
  52.4 1.0 %settle.1 = f32[1,384]{1,0:T(1,128)} custom-call(f32[32,1,128]{2,1,0:T(1,128)S(1)} %all_to_all.5.received, s32[32,128]{1,0:T(8,128)S(1)} %get-tuple-element.100.group_of, bf16[128,4096]{1,0:T(8,128)(2,1)S(1)} %get-tuple-element.101.name_hot), custom_call_target="tpu_custom_call" | custom-call | flops 1000000 | bytes 131072 | tf_op jit(solution)/shard_map/settle/pallas_call | solution.py:31
  (14 shorter events, 0.0 us)
Async XLA Ops:
  0.6 7.5 %copy-start = (s32[2,128,128]{2,1,0:T(8,128)S(1)}, s32[2,128,128]{2,1,0:T(8,128)}, u32[]{:S(2)}) copy-start(s32[2,128,128]{2,1,0:T(8,128)} %frag.5) | copy-start | bytes 393220
  1.4 8.9 %copy-start.2 = (s32[2,1024]{1,0:T(2,128)S(1)}, s32[2,1024]{1,0:T(2,128)}, u32[]{:S(2)}) copy-start(s32[2,1024]{1,0:T(2,128)} %cells.3) | copy-start | bytes 24580
  1.4 8.9 %copy-start.3 = (s32[1,1536]{1,0:T(1,128)S(1)}, s32[1,1536]{1,0:T(1,128)}, u32[]{:S(2)}) copy-start(s32[1,1536]{1,0:T(1,128)} %recv.1) | copy-start | bytes 18436
  1.4 8.9 %copy-start.4 = (s32[1024,1]{0,1:T(1,128)S(1)}, s32[1024,1]{0,1:T(1,128)}, u32[]{:S(2)}) copy-start(s32[1024,1]{0,1:T(1,128)} %param.17) | copy-start | bytes 12292
  4.3 23.8 %collective-permute-start.4 = (bf16[128,3200]{1,0:T(8,128)(2,1)S(1)}, bf16[128,3200]{1,0:T(8,128)(2,1)S(1)}, u32[]{:S(2)}, u32[]{:S(2)}) collective-permute-start(bf16[128,3200]{1,0:T(8,128)(2,1)S(1)} %get-tuple-element.77), channel_id=1, source_target_pairs={{0,1},{1,0},{2,3},{3,2},{4,5},{5,4},{6,7},{7,6},{8,9},{9,8},{10,11... | collective-permute-start | bytes 2457608 | tf_op jit(solution)/shard_map/ppermute | solution.py:669
  7.4 21.6 %collective-permute-start.6 = (bf16[128,3200]{1,0:T(8,128)(2,1)S(1)}, bf16[128,3200]{1,0:T(8,128)(2,1)S(1)}, u32[]{:S(2)}, u32[]{:S(2)}) collective-permute-start(bf16[128,3200]{1,0:T(8,128)(2,1)S(1)} %get-tuple-element.84), channel_id=1, source_target_pairs={{1,2},{2,1},{5,6},{6,5},{9,10},{10,9},{13,14},{14,13},{17,18},{18,... | collective-permute-start | bytes 2457608 | tf_op jit(solution)/shard_map/ppermute | solution.py:669
  8.2 7.3 %copy-start.1 = (bf16[27,32,32]{2,1,0:T(8,128)(2,1)S(1)}, bf16[27,32,32]{2,1,0:T(8,128)(2,1)}, u32[]{:S(2)}) copy-start(bf16[27,32,32]{2,1,0:T(8,128)(2,1)} %conv_weight.1) | copy-start | bytes 165892
  8.2 7.3 %copy-start.5 = (f32[32]{0:T(128)S(1)}, f32[32]{0:T(128)}, u32[]{:S(2)}) copy-start(f32[32]{0:T(128)} %param.12) | copy-start | bytes 388
  8.7 4.4 %collective-permute-start = (bf16[272,128]{1,0:T(8,128)(2,1)S(1)}, bf16[272,128]{1,0:T(8,128)(2,1)S(1)}, u32[]{:S(2)}, u32[]{:S(2)}) collective-permute-start(bf16[272,128]{1,0:T(8,128)(2,1)S(1)} %faces.1), channel_id=1, source_target_pairs={{0,16},{16,0},{1,17},{17,1},{2,18},{18,2},{3,19},{19,3},{4,20},{20... | collective-permute-start | bytes 208904 | tf_op jit(solution)/shard_map/ppermute | solution.py:664
  13.1 15.9 %copy-start.6 = (bf16[3,32]{1,0:T(4,128)(2,1)S(1)}, bf16[3,32]{1,0:T(4,128)(2,1)}, u32[]{:S(2)}) copy-start(bf16[3,32]{1,0:T(4,128)(2,1)} %head_weight.3) | copy-start | bytes 580
  13.2 15.9 %copy-start.7 = (f32[3]{0:T(128)S(1)}, f32[3]{0:T(128)}, u32[]{:S(2)}) copy-start(f32[3]{0:T(128)} %head_bias.3) | copy-start | bytes 40
  13.8 6.3 %collective-permute-start.1 = (bf16[2,48,128]{2,1,0:T(8,128)(2,1)S(1)}, bf16[2,48,128]{2,1,0:T(8,128)(2,1)S(1)}, u32[]{:S(2)}, u32[]{:S(2)}) collective-permute-start(bf16[2,48,128]{2,1,0:T(8,128)(2,1)S(1)} %get-tuple-element.62), channel_id=1, source_target_pairs={{0,4},{4,0},{8,12},{12,8},{1,5},{5,1},{9,13},{13,9},{2,6},{6,2},{1... | collective-permute-start | bytes 73736 | tf_op jit(solution)/shard_map/ppermute | solution.py:669
  13.8 6.3 %collective-permute-start.2 = (bf16[2,48,128]{2,1,0:T(8,128)(2,1)S(1)}, bf16[2,48,128]{2,1,0:T(8,128)(2,1)S(1)}, u32[]{:S(2)}, u32[]{:S(2)}) collective-permute-start(bf16[2,48,128]{2,1,0:T(8,128)(2,1)S(1)} %get-tuple-element.63), channel_id=1, source_target_pairs={{4,8},{8,4},{0,12},{12,0},{5,9},{9,5},{1,13},{13,1},{6,10},{10,6},... | collective-permute-start | bytes 73736 | tf_op jit(solution)/shard_map/ppermute | solution.py:669
  20.7 8.3 %collective-permute-start.7 = (bf16[288,128]{1,0:T(8,128)(2,1)S(1)}, bf16[288,128]{1,0:T(8,128)(2,1)S(1)}, u32[]{:S(2)}, u32[]{:S(2)}) collective-permute-start(bf16[288,128]{1,0:T(8,128)(2,1)S(1)} %get-tuple-element.85), channel_id=1, source_target_pairs={{0,1},{1,0},{2,3},{3,2},{4,5},{5,4},{6,7},{7,6},{8,9},{9,8},{10,11... | collective-permute-start | bytes 221192 | tf_op jit(solution)/shard_map/ppermute | solution.py:669
  25.2 3.9 %collective-permute-start.8 = (bf16[288,128]{1,0:T(8,128)(2,1)S(1)}, bf16[288,128]{1,0:T(8,128)(2,1)S(1)}, u32[]{:S(2)}, u32[]{:S(2)}) collective-permute-start(bf16[288,128]{1,0:T(8,128)(2,1)S(1)} %get-tuple-element.86), channel_id=1, source_target_pairs={{1,2},{2,1},{5,6},{6,5},{9,10},{10,9},{13,14},{14,13},{17,18},{18,... | collective-permute-start | bytes 221192 | tf_op jit(solution)/shard_map/ppermute | solution.py:669
  26.8 8.1 %collective-permute-start.3 = (bf16[128,1024]{1,0:T(8,128)(2,1)S(1)}, bf16[128,1024]{1,0:T(8,128)(2,1)S(1)}, u32[]{:S(2)}, u32[]{:S(2)}) collective-permute-start(bf16[128,1024]{1,0:T(8,128)(2,1)S(1)} %get-tuple-element.75), channel_id=1, source_target_pairs={{0,1},{1,0},{2,3},{3,2},{4,5},{5,4},{6,7},{7,6},{8,9},{9,8},{10,11... | collective-permute-start | bytes 786440 | tf_op jit(solution)/shard_map/ppermute | solution.py:669
  28.2 6.7 %collective-permute-start.5 = (bf16[128,1024]{1,0:T(8,128)(2,1)S(1)}, bf16[128,1024]{1,0:T(8,128)(2,1)S(1)}, u32[]{:S(2)}, u32[]{:S(2)}) collective-permute-start(bf16[128,1024]{1,0:T(8,128)(2,1)S(1)} %get-tuple-element.78), channel_id=1, source_target_pairs={{1,2},{2,1},{5,6},{6,5},{9,10},{10,9},{13,14},{14,13},{17,18},{18,... | collective-permute-start | bytes 786440 | tf_op jit(solution)/shard_map/ppermute | solution.py:669
